TPU v7x, 128 devices: a whole 4x4x4 slice. The times are simulated.
128 devices in a mesh: tm: 16 (over z, y), chan: 8 (over x, core).
Axes of the slice: x: 4, y: 4, z: 4, core: 2. Of those that a mesh axis runs over, the one named last changes fastest.
Arguments:
- visibilities: bfloat16 [64, 4096, 2, 1024], P('tm', None, None, 'chan'), may hold values from -6 to 6
- owner_order: int32 [4096], replicated, may hold values from 0 to 4095, each once
- group_ids: int32 [4096], replicated, may hold values from 0 to 511, never falling along the last dimension, each value on 1 to 32 neighbouring positions
- partner_flags: int32 [4096, 8], replicated, may hold values 0 or 1
Outputs:
- pair_power: float32 [4096, 16, 1024], P(('tm', 'chan'))
Inputs may be any that keep to these rules, and one draw needn't show every extreme that they name: `owner_order`: each slot holds a different correlator baseline. `group_ids`: never falls along slots; each group holds 1 to 32 slots, one exactly 32. `partner_flags`: a 1 in column k lists slot s + k + 1 for slot s.
All inputs are finite; a program needn't handle non-finite values.
Results may differ from a plain program's by a relative error of at most 0.0055.
Values may be sent and summed in bfloat16 or wider, within the bound.
No kernel may reach another device: no remote copies, remote signals or barrier semaphores. Data moves between devices by JAX's collectives and lax.ppermute only.
A program may use at most 128 MiB of HBM per device.

v0:
```python
import math

import jax
import jax.numpy as jnp
from jax import lax
from jax.sharding import PartitionSpec as P


def extended_2(cells, sides, width):
    for axis, dim in sides:
        count = lax.axis_size(axis)
        ends = count - 1
        head = lax.slice_in_dim(cells, 0, width, axis=dim)
        tail = lax.slice_in_dim(cells, cells.shape[dim] - width, cells.shape[dim], axis=dim)
        cells = jnp.concatenate(
            [
                lax.ppermute(tail, axis, [(i, (i + 1) % count) for i in range(ends)]),
                cells,
                lax.ppermute(head, axis, [((i + 1) % count, i) for i in range(ends)]),
            ],
            axis=dim,
        )
    return cells


def delay_table(n_chan):
    channel_index = jnp.arange(n_chan, dtype=jnp.int32)
    phase_index = channel_index[:, None] * channel_index[None, :] % n_chan
    phase_angle = 2.0 * math.pi / n_chan * phase_index.astype(jnp.float32)
    base_angle = 2.0 * math.pi / n_chan * channel_index.astype(jnp.float32)
    window_taper = (
        0.35875
        - 0.48829 * jnp.cos(base_angle)
        + 0.14128 * jnp.cos(2.0 * base_angle)
        - 0.01168 * jnp.cos(3.0 * base_angle)
    )
    weights_norm = window_taper / jnp.sqrt(jnp.sum(window_taper * window_taper))
    cosine = weights_norm[:, None] * jnp.cos(phase_angle)
    sine_part = weights_norm[:, None] * jnp.sin(phase_angle)
    upper_half = jnp.concatenate([cosine, -sine_part], 1)
    bottom = jnp.concatenate([sine_part, cosine], 1)
    return jnp.concatenate([upper_half, bottom], 0).astype(jnp.bfloat16)


def pair_sum(row_spectra, partner_rows):
    summed = jnp.einsum(
        "tbc,tbc->bc", row_spectra, partner_rows, preferred_element_type=jnp.float32
    )
    half_width = summed.shape[1] // 2
    return (summed[:, :half_width] + summed[:, half_width:]) / row_spectra.shape[0]


def body(visibilities, owner_order, group_ids, partner_flags):
    n_tm = lax.axis_size("tm")
    n_chan = lax.axis_size("chan")
    reach = partner_flags.shape[1]
    per_device = visibilities.shape[1] // (n_tm * n_chan)
    chan_total = visibilities.shape[3] * n_chan
    delay_matrix = delay_table(chan_total)
    ordered = jnp.take(visibilities, owner_order, axis=1)
    regrouped = lax.all_to_all(
        lax.all_to_all(ordered, "tm", split_axis=1, concat_axis=0, tiled=True),
        "chan",
        split_axis=1,
        concat_axis=3,
        tiled=True,
    )
    n_rows = regrouped.shape[0] * regrouped.shape[1]
    flat = regrouped.reshape(n_rows, 2 * chan_total)
    result = jnp.dot(flat, delay_matrix, preferred_element_type=jnp.float32).astype(jnp.bfloat16)
    spectra = result.reshape(regrouped.shape[0], regrouped.shape[1], 2 * chan_total)
    start = lax.axis_index(("tm", "chan")) * per_device
    padded_groups = jnp.pad(group_ids, (reach, reach), constant_values=-1)
    padded_flags = jnp.pad(partner_flags, ((reach, reach), (0, 0)))
    group_window = lax.dynamic_slice_in_dim(padded_groups, start, per_device + 2 * reach, 0)
    flag_window = lax.dynamic_slice_in_dim(padded_flags, start, per_device + 2 * reach, 0)
    own_group = group_window[reach : reach + per_device]
    extended = extended_2(spectra, ((("tm", "chan"), 1),), reach)
    columns = []
    for offset in range(1, reach + 1):
        power = pair_sum(spectra, extended[:, reach + offset : reach + offset + per_device])
        columns.append(
            jnp.where(
                (
                    (group_window[reach + offset : reach + offset + per_device] == own_group)
                    & (flag_window[reach : reach + per_device, offset - 1] == 1)
                )[:, None],
                power,
                0.0,
            )
        )
    for offset in range(1, reach + 1):
        valid = (group_window[reach - offset : reach - offset + per_device] == own_group) & (
            flag_window[reach - offset : reach - offset + per_device, offset - 1] == 1
        )
        power = pair_sum(spectra, extended[:, reach - offset : reach - offset + per_device])
        columns.append(jnp.where(valid[:, None], power, 0.0))
    return jnp.stack(columns, 1)


def solution(mesh):
    return jax.shard_map(
        body,
        mesh=mesh,
        in_specs=(P("tm", None, None, "chan"), P(), P(), P()),
        out_specs=P(("tm", "chan"), None, None),
        check_vma=False,
    )
```

profile of v0, /device:TPU:32, one launch (start us, length us, event | category | flops | bytes accessed | tf_op | source)
XLA Modules:
  0.0 477.3 jit_solution(8379851959030169122)
XLA Ops:
  0.0 0.7 fusion.129
  0.7 0.7 compare_and_fusion
  1.4 50.3 %gather_fusion = bf16[4096,4,2,128]{3,2,1,0:T(2,128)(2,1)} fusion(bf16[4,4096,2,128]{3,2,1,0:T(2,128)(2,1)} %param.4, s32[4096]{0:T(1024)S(1)} %fusion.129), kind=kCustom, calls=%fused_computation | custom fusion | bytes 16793600 | tf_op jit(solution)/shard_map/jit(_take)/gather | solution.py:60
  51.8 16.2 %fusion.54 = bf16[4,4096,2,128]{3,2,0,1:T(2,128)(2,1)S(1)} fusion(bf16[4096,4,2,128]{3,2,1,0:T(2,128)(2,1)} %gather_fusion, pred[4096]{0:T(1024)(128)(4,1)S(1)} %compare_and_fusion), kind=kLoop, calls=%fused_computation.103 | loop fusion | flops 4194304 | bytes 16781312 | tf_op jit(solution)/shard_map/jit(_take)/select_n | solution.py:60
  68.0 101.2 %all_to_all.33 = bf16[4,4096,2,128]{3,2,0,1:T(2,128)(2,1)} all-to-all(bf16[4,4096,2,128]{3,2,0,1:T(2,128)(2,1)S(1)} %fusion.54), channel_id=1, replica_groups=mesh['tm'=16,'chan'=8] {'tm'}, dimensions={1} | all-to-all | bytes 16777216 | tf_op jit(solution)/shard_map/all_to_all | solution.py:62
  169.2 7.7 %copy.29 = bf16[4,4096,2,128]{3,1,2,0:T(8,128)(2,1)} copy(bf16[4,4096,2,128]{3,2,0,1:T(2,128)(2,1)} %all_to_all.33) | data formatting | bytes 16777216 | tf_op jit(solution)/shard_map/all_to_all | solution.py:62
  176.9 7.7 %copy.30 = bf16[16,4,256,2,128]{4,2,3,1,0:T(8,128)(2,1)} copy(bf16[16,4,256,2,128]{4,2,0,3,1:T(8,128)(2,1)} %bitcast.211) | data formatting | bytes 16777216 | tf_op jit(solution)/shard_map/all_to_all | solution.py:62
  184.6 13.2 %copy.31 = bf16[64,256,2,128]{3,2,0,1:T(2,128)(2,1)} copy(bf16[64,256,2,128]{3,1,2,0:T(8,128)(2,1)} %bitcast.212) | data formatting | bytes 16777216 | tf_op jit(solution)/shard_map/all_to_all | solution.py:62
  197.8 5.1 %all-to-all-start.1 = ((bf16[64,256,2,128]{3,2,0,1:T(2,128)(2,1)}), bf16[64,256,2,128]{3,2,0,1:T(2,128)(2,1)}, u32[]{:S(2)}, u32[]{:S(2)}) async-start(bf16[64,256,2,128]{3,2,0,1:T(2,128)(2,1)} %copy.31), calls=%async_computation.1 | async-start | bytes 16777216 | tf_op jit(solution)/shard_map/all_to_all | solution.py:61
  202.9 0.7 multiply_reduce_fusion
  204.3 0.1 fusion.130
  204.3 18.4 %negate_convert_fusion = (bf16[1024,1024]{1,0:T(8,128)(2,1)S(1)}, bf16[1024,1024]{1,0:T(8,128)(2,1)}, bf16[1024,1024]{1,0:T(8,128)(2,1)}) fusion(f32[1024]{0:T(1024)S(1)} %fusion.130), kind=kLoop, calls=%fused_computation.111 | loop fusion | flops 20971520 | bytes 6295552 | tf_op jit(solution)/shard_map/convert.5
  222.7 74.6 %all-to-all-done.1 = bf16[64,256,2,128]{3,2,0,1:T(2,128)(2,1)} async-done(((bf16[64,256,2,128]{3,2,0,1:T(2,128)(2,1)}), bf16[64,256,2,128]{3,2,0,1:T(2,128)(2,1)}, u32[]{:S(2)}, u32[]{:S(2)}) %all-to-all-start.1) | async-done | bytes 8388640 | tf_op jit(solution)/shard_map/all_to_all | solution.py:61
  297.3 16.3 %copy.147 = bf16[64,8,32,2,128]{4,1,3,2,0:T(8,128)(2,1)} copy(bf16[64,8,32,2,128]{4,3,0,2,1:T(2,128)(2,1)} %bitcast.37) | data formatting | bytes 16777216 | tf_op jit(solution)/shard_map/all_to_all | solution.py:61
  313.7 13.3 %reshape.77 = bf16[2048,2048]{1,0:T(8,128)(2,1)} reshape(bf16[64,32,2,8,128]{4,3,2,1,0:T(8,128)(2,1)} %bitcast.213) | data formatting | bytes 16777216 | tf_op jit(solution)/shard_map/reshape | solution.py:69
  327.0 26.1 %fusion.55 = bf16[2048,2048]{1,0:T(8,128)(2,1)} fusion(bf16[2048,2048]{1,0:T(8,128)(2,1)} %reshape.77, bf16[1024,1024]{1,0:T(8,128)(2,1)} %get-tuple-element.41, bf16[1024,1024]{1,0:T(8,128)(2,1)} %get-tuple-element.40, bf16[1024,1024]{1,0:T(8,128)(2,1)S(1)} %get-tuple-element.39), kind=kOutput, calls=%fused_computation.104 | convolution fusion | flops 17217617920 | bytes 23068672 | tf_op jit(solution)/shard_map/dot_general | solution.py:70
  353.0 0.0 copy-start.1
  353.0 0.0 copy-start
  353.0 4.8 %fusion.132 = (bf16[64,8,2048]{2,1,0:T(8,128)(2,1)}, bf16[64,8,2048]{2,1,0:T(8,128)(2,1)}) fusion(bf16[64,32,2048]{2,1,0:T(8,128)(2,1)} %bitcast.206), kind=kLoop, calls=%fused_computation.223 | loop fusion | bytes 8388608 | tf_op jit(solution)/shard_map/slice | solution.py:14
  357.9 4.4 collective-permute-start
  362.3 0.0 copy-done.1
  362.3 0.1 pad_dynamic-slice_fusion.1
  362.4 0.0 copy-done
  362.4 0.1 pad_dynamic-slice_fusion
  362.4 0.1 bitcast_and_fusion.12
  362.5 0.1 bitcast_and_fusion.6
  362.6 0.1 bitcast_and_fusion
  362.7 1.9 collective-permute-start.1
  364.6 21.5 %collective-permute-done = bf16[64,8,2048]{2,1,0:T(8,128)(2,1)S(1)} collective-permute-done((bf16[64,8,2048]{2,1,0:T(8,128)(2,1)}, bf16[64,8,2048]{2,1,0:T(8,128)(2,1)S(1)}, u32[]{:S(2)}, u32[]{:S(2)}) %collective-permute-start) | collective-permute-done | bytes 2097184 | tf_op jit(solution)/shard_map/ppermute | solution.py:19
  386.1 46.3 %fusion.7 = (f32[32,2048]{1,0:T(8,128)S(1)}, f32[32,2048]{1,0:T(8,128)}, f32[32,2048]{1,0:T(8,128)}, f32[32,2048]{1,0:T(8,128)S(1)}, f32[32,2048]{1,0:T(8,128)S(...) fusion(bf16[32,2048,64]{1,0,2:T(8,128)(2,1)} %bitcast.207, ...), kind=kLoop, calls=%fused_computation.38 | loop fusion | flops 238551040 | bytes 20971520 | tf_op jit(solution)/shard_map/tbc,tbc->bc/dot_general | solution.py:46
  432.4 1.0 fusion.128
  433.4 1.0 fusion.124
  434.5 1.0 fusion.120
  435.5 0.1 fusion.116
  435.6 0.1 fusion.112
  435.7 0.1 fusion.108
  435.8 0.1 fusion.104
  435.9 0.1 fusion.100
  435.9 0.0 collective-permute-done.1
  435.9 38.1 %fusion.15 = (f32[32,2048]{1,0:T(8,128)S(1)}, f32[32,2048]{1,0:T(8,128)S(1)}, f32[32,2048]{1,0:T(8,128)S(1)}, f32[32,2048]{1,0:T(8,128)S(1)}, f32[32,2048]{1,0:T...) fusion(bf16[32,2048,64]{1,0,2:T(8,128)(2,1)} %bitcast.209, ...), kind=kLoop, calls=%fused_computation.46 | loop fusion | flops 238551040 | bytes 20971520 | tf_op jit(solution)/shard_map/tbc,tbc->bc/dot_general | solution.py:46
  474.1 0.1 fusion.96
  474.2 0.1 fusion.92
  474.2 0.1 fusion.88
  474.3 0.1 fusion.84
  474.4 0.1 fusion.80
  474.5 0.1 fusion.76
  474.6 0.1 fusion.72
  474.7 0.1 fusion.68
  474.8 2.5 copy.33
Async XLA Ops:
  197.8 99.6 %all-to-all-start.1 = ((bf16[64,256,2,128]{3,2,0,1:T(2,128)(2,1)}), bf16[64,256,2,128]{3,2,0,1:T(2,128)(2,1)}, u32[]{:S(2)}, u32[]{:S(2)}) async-start(bf16[64,256,2,128]{3,2,0,1:T(2,128)(2,1)} %copy.31), calls=%async_computation.1 | async-start | bytes 16777216 | tf_op jit(solution)/shard_map/all_to_all | solution.py:61
  353.0 9.2 %copy-start.1 = (s32[4096]{0:T(1024)S(1)}, s32[4096]{0:T(1024)}, u32[]{:S(2)}) copy-start(s32[4096]{0:T(1024)} %param.6) | copy-start | bytes 49156
  353.0 9.3 %copy-start = (s32[4096,8]{0,1:T(8,128)S(1)}, s32[4096,8]{0,1:T(8,128)}, u32[]{:S(2)}) copy-start(s32[4096,8]{0,1:T(8,128)} %param.7) | copy-start | bytes 393220
  357.9 28.2 %collective-permute-start = (bf16[64,8,2048]{2,1,0:T(8,128)(2,1)}, bf16[64,8,2048]{2,1,0:T(8,128)(2,1)S(1)}, u32[]{:S(2)}, u32[]{:S(2)}) collective-permute-start(bf16[64,8,2048]{2,1,0:T(8,128)(2,1)} %get-tuple-element.22), channel_id=1, source_target_pairs={{1,0},{2,1},{3,2},{4,3},{5,4},{6,5},{7,6},{8,7},{9,8},{10,9},{11,1... | collective-permute-start | bytes 6291464 | tf_op jit(solution)/shard_map/ppermute | solution.py:19
  362.7 73.2 %collective-permute-start.1 = (bf16[64,8,2048]{2,1,0:T(8,128)(2,1)}, bf16[64,8,2048]{2,1,0:T(8,128)(2,1)}, u32[]{:S(2)}, u32[]{:S(2)}) collective-permute-start(bf16[64,8,2048]{2,1,0:T(8,128)(2,1)} %get-tuple-element.21), channel_id=1, source_target_pairs={{0,1},{1,2},{2,3},{3,4},{4,5},{5,6},{6,7},{7,8},{8,9},{9,10},{10,1... | collective-permute-start | bytes 6291464 | tf_op jit(solution)/shard_map/ppermute | solution.py:17
where the time goes:
time: 481 us; the launch traced here: 477 us
  other arithmetic  126 us (26%)
  local copies, waits for them, and re-layouts  116 us (24%)
  blocking collectives  101 us (21%)
  waiting for transfers between devices  96.1 us (20%)
  matrix products  26.1 us (5%)
  starting transfers between devices  11.4 us (2%)
    all_to_all x1, blocking collectives, body(): lax.all_to_all(ordered, 'tm', split_axis=1, concat_axis=0, tiled=True)  101 us
    dot_general x2, other arithmetic, pair_sum(): jnp.einsum('tbc,tbc->bc', row_spectra, partner_rows, preferred_element_ty...  84.4 us
    all_to_all x1, waiting for transfers between devices, body(): lax.all_to_all(lax.all_to_all(ordered, 'tm', split_axis=1, concat_axis=0,...  74.6 us
    gather x1, local copies, waits for them, and re-layouts, body(): ordered = jnp.take(visibilities, owner_order, axis=1)  50.3 us
    all_to_all x3, local copies, waits for them, and re-layouts, body(): lax.all_to_all(ordered, 'tm', split_axis=1, concat_axis=0, tiled=True)  28.6 us
    dot_general x1, matrix products, body(): jnp.dot(flat, delay_matrix, preferred_element_type=jnp.float32)  26.1 us
    ppermute x1, waiting for transfers between devices, extended_2(): lax.ppermute(head, axis, [((i + 1) % count, i) for i in range(ends)])  21.5 us
    another operation x1, other arithmetic  18.4 us
  transfers between devices with their start and end apart: 3, of which 2 were waited for; matrix products, arithmetic and copies ran while one was open for 15% of the time, Pallas kernels for 0%

commit v1 on v0

v1 whole, which is shorter than its diff:
```python
import functools
import math

import jax
import jax.numpy as jnp
from jax import lax
from jax.experimental import pallas as pl
from jax.experimental.pallas import tpu as pltpu
from jax.sharding import PartitionSpec as P

AXES = ("tm", "chan")
MIB = 2**20
LANES = 128
PARTS = (3, 1)


def delay_table(n_chan):
    channel_index = jnp.arange(n_chan, dtype=jnp.int32)
    phase_index = channel_index[:, None] * channel_index[None, :] % n_chan
    phase_angle = 2.0 * math.pi / n_chan * phase_index.astype(jnp.float32)
    base_angle = 2.0 * math.pi / n_chan * channel_index.astype(jnp.float32)
    window_taper = (
        0.35875
        - 0.48829 * jnp.cos(base_angle)
        + 0.14128 * jnp.cos(2.0 * base_angle)
        - 0.01168 * jnp.cos(3.0 * base_angle)
    )
    weights_norm = window_taper / jnp.sqrt(jnp.sum(window_taper * window_taper))
    cosine = weights_norm[:, None] * jnp.cos(phase_angle)
    sine_part = weights_norm[:, None] * jnp.sin(phase_angle)
    upper_half = jnp.concatenate([cosine, -sine_part], 1)
    bottom = jnp.concatenate([sine_part, cosine], 1)
    return jnp.concatenate([upper_half, bottom], 0).astype(jnp.bfloat16)


def gather_kernel(order_ref, vis_ref, out_ref):
    owners, count, per = out_ref.shape[:3]
    first = pl.program_id(0) * owners

    def one_owner(owner, carry):
        base = (first + owner) * per
        for j in range(per):
            source = order_ref[base + j]
            for t in range(count):
                out_ref[owner, t, j] = vis_ref[t, source]
        return carry

    lax.fori_loop(0, owners, one_owner, 0)


def gather(visibilities, order, first, count, n_dev):
    n_base = visibilities.shape[1]
    per = n_base // n_dev
    tail = visibilities.shape[2:]
    steps = 8
    part = lax.slice_in_dim(visibilities, first, first + count, axis=0)
    return pl.pallas_call(
        gather_kernel,
        grid_spec=pltpu.PrefetchScalarGridSpec(
            num_scalar_prefetch=1,
            grid=(steps,),
            in_specs=[pl.BlockSpec((count, n_base) + tail, lambda i, o: (0, 0, 0, 0))],
            out_specs=pl.BlockSpec(
                (n_dev // steps, count, per) + tail, lambda i, o: (i, 0, 0, 0, 0)
            ),
        ),
        out_shape=jax.ShapeDtypeStruct((n_dev, count, per) + tail, visibilities.dtype),
        compiler_params=pltpu.CompilerParams(vmem_limit_bytes=40 * MIB),
        cost_estimate=pl.CostEstimate(
            flops=0, bytes_accessed=2 * count * n_base * 512, transcendentals=0
        ),
        name="slot_gather",
    )(order, part)


def spectra_kernel(received_ref, order_ref, table_ref, out_ref, rows_ref):
    sources, n_chan, _, pairs = received_ref.shape[:4]
    half = table_ref.shape[0] // 2
    group = order_ref.shape[0] // 2
    for b in range(pairs // 16):
        block = jnp.concatenate(
            [
                received_ref[:, c, 0, pl.ds(16 * b, 16), :].reshape(2 * group, LANES)
                for c in range(n_chan)
            ],
            axis=1,
        )
        sorted_rows = jnp.dot(
            order_ref[...], block, preferred_element_type=jnp.float32
        ).astype(jnp.bfloat16)
        rows_ref[pl.ds(b * group, group), pl.ds(0, half)] = sorted_rows[:group]
        rows_ref[pl.ds(b * group, group), pl.ds(half, half)] = sorted_rows[group:]
    width = 512
    for n in range(2 * half // width):
        part = jnp.dot(
            rows_ref[...],
            table_ref[:, pl.ds(n * width, width)],
            preferred_element_type=jnp.float32,
        ).astype(jnp.bfloat16)
        out_ref[0, :, :, pl.ds(n * width, width)] = part.reshape(
            pairs // 2, sources, width
        )


def spectra(received, row_order, table, n_tm, n_chan):
    _, count, pairs, lanes = received.shape
    rows = n_tm * pairs // 2
    width = table.shape[1]
    return pl.pallas_call(
        spectra_kernel,
        grid=(count,),
        in_specs=[
            pl.BlockSpec((n_tm, n_chan, 1, pairs, lanes), lambda t: (0, 0, t, 0, 0)),
            pl.BlockSpec(row_order.shape, lambda t: (0, 0)),
            pl.BlockSpec(table.shape, lambda t: (0, 0), pipeline_mode=pl.Buffered(1)),
        ],
        out_specs=pl.BlockSpec((1, pairs // 2, n_tm, width), lambda t: (t, 0, 0, 0)),
        out_shape=jax.ShapeDtypeStruct((count, pairs // 2, n_tm, width), jnp.bfloat16),
        scratch_shapes=[pltpu.VMEM((rows, width), jnp.bfloat16)],
        compiler_params=pltpu.CompilerParams(vmem_limit_bytes=40 * MIB),
        cost_estimate=pl.CostEstimate(
            flops=2 * count * rows * width * width,
            bytes_accessed=4 * count * rows * width + 2 * width * width,
            transcendentals=0,
        ),
        name="delay_spectra",
    )(received.reshape(n_tm, n_chan, count, pairs, lanes), row_order, table)


def pair_kernel(last, refs_in, refs_out, scratch):
    real_ref, imag_ref = scratch[:2]
    reach, per = 8, 32
    count = refs_in[0].shape[0]
    times = refs_in[0].shape[2]
    for which, target in ((0, real_ref), (1, imag_ref)):
        before, own, after = refs_in[3 * which : 3 * which + 3]
        for t in range(count):
            span = pl.ds(t * times, times)
            target[pl.ds(0, reach), span] = before[t].astype(jnp.float32)
            target[pl.ds(reach, per), span] = own[t].astype(jnp.float32)
            target[pl.ds(reach + per, reach), span] = after[t].astype(jnp.float32)
    column = lax.broadcasted_iota(jnp.int32, (reach, LANES), 0)
    power_ref = scratch[2] if last else refs_out[0]

    def one_slot(s, carry):
        real, imag = real_ref[s], imag_ref[s]
        powers = jnp.zeros((reach, LANES), jnp.float32)
        for k in range(1, reach + 1):
            product = real * real_ref[s + k] + imag * imag_ref[s + k]
            powers = jnp.where(
                column == k - 1, jnp.sum(product, axis=0, keepdims=True), powers
            )
        if last:
            powers = (powers + refs_in[6][s]) * (1.0 / 64.0)
            powers = jnp.where(refs_in[7][s] > 0.0, powers, 0.0)
        power_ref[s] = powers
        return carry

    lax.fori_loop(0, reach + per, one_slot, 0)
    if last:
        out_ref = refs_out[0]

        def one_output(s, carry):
            out_ref[s, pl.ds(0, reach), :] = power_ref[s + reach]
            backward = power_ref[s + reach - 1]
            for k in range(2, reach + 1):
                backward = jnp.where(column == k - 1, power_ref[s + reach - k], backward)
            out_ref[s, pl.ds(reach, reach), :] = backward
            return carry

        lax.fori_loop(0, per, one_output, 0)


def pair_powers(own, before, after, total=None, valid=None):
    count, per, times, width = own.shape
    reach = before.shape[1]
    chunks = width // 2 // LANES
    last = total is not None
    specs, operands = [], []
    for which in range(2):
        for array in (before, own, after):
            specs.append(
                pl.BlockSpec(
                    array.shape[:3] + (LANES,),
                    functools.partial(lambda w, j: (0, 0, 0, w * chunks + j), which),
                )
            )
            operands.append(array)
    power_spec = pl.BlockSpec((reach + per, reach, LANES), lambda j: (0, 0, j))
    power_shape = (reach + per, reach, width // 2)
    scratch = [pltpu.VMEM((per + 2 * reach, count * times, LANES), jnp.float32)] * 2
    if last:
        specs += [power_spec, pl.BlockSpec(valid.shape, lambda j: (0, 0, 0))]
        operands += [total, valid]
        scratch.append(pltpu.VMEM((reach + per, reach, LANES), jnp.float32))
        out_spec = pl.BlockSpec((per, 2 * reach, LANES), lambda j: (0, 0, j))
        out_shape = (per, 2 * reach, width // 2)
    else:
        out_spec, out_shape = power_spec, power_shape
    n_in = len(operands)

    def kernel(*refs):
        pair_kernel(last, refs[:n_in], refs[n_in : n_in + 1], refs[n_in + 1 :])

    return pl.pallas_call(
        kernel,
        grid=(chunks,),
        in_specs=specs,
        out_specs=out_spec,
        out_shape=jax.ShapeDtypeStruct(out_shape, jnp.float32),
        scratch_shapes=scratch,
        compiler_params=pltpu.CompilerParams(vmem_limit_bytes=40 * MIB),
        cost_estimate=pl.CostEstimate(
            flops=2 * (per + reach) * reach * count * times * width,
            bytes_accessed=2 * count * times * (per + 2 * reach) * width,
            transcendentals=0,
        ),
        name="pair_powers",
    )(*operands)


def body(visibilities, owner_order, group_ids, partner_flags):
    n_tm = lax.axis_size("tm")
    n_chan = lax.axis_size("chan")
    n_dev = n_tm * n_chan
    n_base = visibilities.shape[1]
    reach = partner_flags.shape[1]
    per = n_base // n_dev
    chan_total = visibilities.shape[3] * n_chan

    place = jnp.arange(n_tm * 16, dtype=jnp.int32)
    wanted = (place % n_tm) * 16 + (place // n_tm % 8) * 2 + place // (n_tm * 8)
    row_order = (wanted[:, None] == place[None, :]).astype(jnp.bfloat16)
    table = delay_table(chan_total)

    start = lax.axis_index(AXES) * per
    groups = lax.dynamic_slice_in_dim(
        jnp.pad(group_ids, (reach, reach), constant_values=-1), start, per + 2 * reach, 0
    )
    flags = lax.dynamic_slice_in_dim(
        jnp.pad(partner_flags, ((reach, reach), (0, 0))), start, per + reach, 0
    )
    own_group = groups[: per + reach]
    same = jnp.stack([groups[k : k + per + reach] == own_group for k in range(1, reach + 1)], 1)
    valid = jnp.broadcast_to(
        (same & (flags == 1)).astype(jnp.float32)[:, :, None], (per + reach, reach, LANES)
    )

    total = None
    first = 0
    up = [(i, i + 1) for i in range(n_dev - 1)]
    down = [(i + 1, i) for i in range(n_dev - 1)]
    for number, count in enumerate(PARTS):
        send = gather(visibilities, owner_order, first, count, n_dev)
        send = send.reshape(n_dev, count, 2 * per, visibilities.shape[3])
        received = lax.all_to_all(send, AXES, 0, 0, tiled=True)
        own = spectra(received, row_order, table, n_tm, n_chan)
        before = lax.ppermute(own[:, per - reach :], AXES, up)
        after = lax.ppermute(own[:, :reach], AXES, down)
        if number + 1 < len(PARTS):
            total = pair_powers(own, before, after)
        else:
            total = pair_powers(own, before, after, total, valid)
        first += count
    return total


def solution(mesh):
    return jax.shard_map(
        body,
        mesh=mesh,
        in_specs=(P("tm", None, None, "chan"), P(), P(), P()),
        out_specs=P(AXES, None, None),
        check_vma=False,
    )
```

time: 481 us -> 199 us (0.41)
  blocking collectives: 101 us -> 0 us
  local copies, waits for them, and re-layouts: 116 us -> 26.6 us
  waiting for transfers between devices: 96.1 us -> 8.86 us
  other arithmetic: 126 us -> 55.3 us
  Pallas kernels: 0 us -> 69.5 us
  matrix products: 26.1 us -> 0 us
  starting transfers between devices: 11.4 us -> 37.1 us
    all_to_all x1 -> x0, blocking collectives: 101 us -> none  [body(): lax.all_to_all(ordered, 'tm', split_axis=1, concat_axis=0, tiled=True)]
    dot_general x2 -> x0, other arithmetic: 84.4 us -> none  [pair_sum(): jnp.einsum('tbc,tbc->bc', row_spectra, partner_rows, preferred_element_ty...]
    pallas_call x0 -> x6, Pallas kernels: none -> 69.5 us  [the longest x2 31.1 us: pair_powers(): pl.pallas_call(kernel, grid=(chunks,), in_specs=specs, out_specs=out_spec...]
    all_to_all x1 -> x2, waiting for transfers between devices: 74.6 us -> 8.85 us  [body(): received = lax.all_to_all(send, AXES, 0, 0, tiled=True)]
    gather x1 -> x0, local copies, waits for them, and re-layouts: 50.3 us -> none  [body(): ordered = jnp.take(visibilities, owner_order, axis=1)]
    all_to_all x4 -> x0, local copies, waits for them, and re-layouts: 44.9 us -> none  [the longest x3 28.6 us: body(): lax.all_to_all(ordered, 'tm', split_axis=1, concat_axis=0, tiled=True)]
    concatenate x0 -> x1, other arithmetic: none -> 36.7 us  [delay_table(): return jnp.concatenate([upper_half, bottom], 0).astype(jnp.bfloat16)]
    dot_general x1 -> x0, matrix products: 26.1 us -> none  [body(): jnp.dot(flat, delay_matrix, preferred_element_type=jnp.float32)]
  transfers between devices with their start and end apart: 3 -> 6, of which waited for: 2 -> 1; matrix products, arithmetic and copies ran while one was open for 15% -> 31% of each run, Pallas kernels for 0% -> 24%
where the time goes in v1:
time: 199 us; the launch traced here: 198 us
  Pallas kernels  69.5 us (35%)
  other arithmetic  55.3 us (28%)
  starting transfers between devices  37.1 us (19%)
  local copies, waits for them, and re-layouts  26.6 us (13%)
  waiting for transfers between devices  8.86 us (4%)
    concatenate x1, other arithmetic, delay_table(): return jnp.concatenate([upper_half, bottom], 0).astype(jnp.bfloat16)  36.7 us
    pallas_call x2, Pallas kernels, pair_powers(): pl.pallas_call(kernel, grid=(chunks,), in_specs=specs, out_specs=out_spec...  31.1 us
    pallas_call x2, Pallas kernels, spectra(): pl.pallas_call(spectra_kernel, grid=(count,), in_specs=[pl.BlockSpec((n_t...  24.3 us
    all_to_all x2, starting transfers between devices, body(): received = lax.all_to_all(send, AXES, 0, 0, tiled=True)  17.6 us
    another operation x1, other arithmetic  17.6 us
    ppermute x2, starting transfers between devices, body(): after = lax.ppermute(own[:, :reach], AXES, down)  15.6 us
    unnamed x18, local copies, waits for them, and re-layouts  14.4 us
    pallas_call x2, Pallas kernels, gather(): pl.pallas_call(gather_kernel, grid_spec=pltpu.PrefetchScalarGridSpec(num_...  14.2 us
  transfers between devices with their start and end apart: 6, of which 1 were waited for; matrix products, arithmetic and copies ran while one was open for 31% of the time, Pallas kernels for 24%

profile of v1, /device:TPU:32, one launch (start us, length us, event | category | flops | bytes accessed | tf_op | source)
XLA Modules:
  0.0 198.3 jit_solution(9259892012942625177)
XLA Ops:
  0.0 0.0 copy-start.6
  0.0 5.6 %slice.48.vis_ref = bf16[3,4096,2,128]{3,2,1,0:T(2,128)(2,1)S(1)} slice(bf16[4,4096,2,128]{3,2,1,0:T(2,128)(2,1)} %param.4), slice={[0:3], [0:4096], [0:2], [0:128]} | slice | bytes 12582912 | tf_op jit(solution)/shard_map/slice | solution.py:56
  5.6 0.0 copy-done.6
  5.7 8.1 %slot_gather.3 = bf16[128,3,32,2,128]{4,3,2,1,0:T(2,128)(2,1)S(1)} custom-call(s32[4096]{0:T(1024)S(1)} %copy-done.6, bf16[3,4096,2,128]{3,2,1,0:T(2,128)(2,1)S(1)} %slice.48.vis_ref), custom_call_target="tpu_custom_call" | custom-call | bytes 12582912 | tf_op jit(solution)/shard_map/slot_gather/pallas_call | solution.py:57
  13.7 0.0 copy-start.2
  13.7 2.6 %copy-done.2 = bf16[128,3,32,2,128]{4,3,2,1,0:T(2,128)(2,1)} copy-done((bf16[128,3,32,2,128]{4,3,2,1,0:T(2,128)(2,1)}, bf16[128,3,32,2,128]{4,3,2,1,0:T(2,128)(2,1)S(1)}, u32[]{:S(2)}) %copy-start.2) | copy-done | bytes 6291480
  16.3 10.6 %all-to-all-start.1 = ((bf16[128,3,64,128]{3,2,1,0:T(8,128)(2,1)}), bf16[128,3,64,128]{3,2,1,0:T(8,128)(2,1)}, u32[]{:S(2)}, u32[]{:S(2)}) async-start(bf16[128,3,64,128]{3,2,1,0:T(8,128)(2,1)} %bitcast.22), calls=%async_computation.1 | async-start | bytes 12582912 | tf_op jit(solution)/shard_map/all_to_all | solution.py:256
  26.9 3.2 %slice.45.vis_ref = bf16[1,4096,2,128]{3,2,1,0:T(2,128)(2,1)S(1)} slice(bf16[4,4096,2,128]{3,2,1,0:T(2,128)(2,1)} %param.4), slice={[3:4], [0:4096], [0:2], [0:128]} | slice | bytes 4194304 | tf_op jit(solution)/shard_map/slice | solution.py:56
  30.2 0.7 multiply_reduce_fusion
  31.5 6.1 %slot_gather.2 = bf16[128,1,32,2,128]{4,3,2,1,0:T(2,128)(2,1)} custom-call(s32[4096]{0:T(1024)S(1)} %copy-done.6, bf16[1,4096,2,128]{3,2,1,0:T(2,128)(2,1)S(1)} %slice.45.vis_ref), custom_call_target="tpu_custom_call" | custom-call | bytes 4194304 | tf_op jit(solution)/shard_map/slot_gather/pallas_call | solution.py:57
  37.7 0.1 fusion.9
  37.7 17.6 %negate_convert_fusion = (bf16[1024,1024]{1,0:T(8,128)(2,1)S(1)}, bf16[1024,1024]{1,0:T(8,128)(2,1)S(1)}, bf16[1024,1024]{1,0:T(8,128)(2,1)S(1)}) fusion(f32[1024]{0:T(1024)S(1)} %fusion.9), kind=kLoop, calls=%fused_computation.7 | loop fusion | flops 20971520 | bytes 6295552 | tf_op jit(solution)/shard_map/convert.5
  55.3 36.7 %maximum_maximum_fusion.table_ref = bf16[2048,2048]{1,0:T(8,128)(2,1)} fusion(bf16[1024,1024]{1,0:T(8,128)(2,1)S(1)} %get-tuple-element.11, bf16[1024,1024]{1,0:T(8,128)(2,1)S(1)} %get-tuple-element.10, bf16[1024,1024]{1,0:T(8,128)(2,1)S(1)} %get-tuple-element.9), kind=kLoop, calls=%fused_computation | loop fusion | flops 33554432 | bytes 14680064 | tf_op jit(solution)/shard_map/concatenate | solution.py:33
  92.0 8.8 %all-to-all-done.1 = bf16[128,3,64,128]{3,2,1,0:T(8,128)(2,1)} async-done(((bf16[128,3,64,128]{3,2,1,0:T(8,128)(2,1)}), bf16[128,3,64,128]{3,2,1,0:T(8,128)(2,1)}, u32[]{:S(2)}, u32[]{:S(2)}) %all-to-all-start.1) | async-done | bytes 6291488 | tf_op jit(solution)/shard_map/all_to_all | solution.py:256
  100.8 7.0 %all-to-all-start = ((bf16[128,1,64,128]{3,2,1,0:T(8,128)(2,1)}), bf16[128,1,64,128]{3,2,1,0:T(8,128)(2,1)S(1)}, u32[]{:S(2)}, u32[]{:S(2)}) async-start(bf16[128,1,64,128]{3,2,1,0:T(8,128)(2,1)} %bitcast.1), calls=%async_computation | async-start | bytes 4194304 | tf_op jit(solution)/shard_map/all_to_all | solution.py:256
  107.8 0.1 fusion.7.order_ref
  107.9 19.2 %delay_spectra.3.refs_1_.refs_4_ = bf16[3,32,16,2048]{3,2,1,0:T(8,128)(2,1)S(1)} custom-call(bf16[16,8,3,64,128]{4,3,2,1,0:T(8,128)(2,1)} %bitcast.4.received_ref, bf16[256,256]{1,0:T(8,128)(2,1)S(1)} %fusion.7.order_ref, bf16[2048,2048]{1,0:T(8,128)(2,1)} %maximum_maximum_fusion.table_ref), custom_call_target="tpu_custom_call" | custom-call | flops 12884901888 | bytes 20971520 | tf_op jit(solution)/shard_map/delay_spectra/pallas_call | solution.py:109
  127.2 2.1 %fusion.18 = (bf16[3,8,16,2048]{3,2,1,0:T(8,128)(2,1)}, bf16[3,8,16,2048]{3,2,1,0:T(8,128)(2,1)}) fusion(bf16[3,32,16,2048]{3,2,1,0:T(8,128)(2,1)S(1)} %delay_spectra.3.refs_1_.refs_4_), kind=kLoop, calls=%fused_computation.50 | loop fusion | bytes 6291456 | tf_op jit(solution)/shard_map/slice | solution.py:259
  129.2 0.0 copy-start
  129.2 2.7 %copy-done = bf16[3,32,16,2048]{3,2,1,0:T(8,128)(2,1)} copy-done((bf16[3,32,16,2048]{3,2,1,0:T(8,128)(2,1)}, bf16[3,32,16,2048]{3,2,1,0:T(8,128)(2,1)S(1)}, u32[]{:S(2)}) %copy-start) | copy-done | bytes 6291480
  131.9 2.0 %collective-permute-start.2 = (bf16[3,8,16,2048]{3,2,1,0:T(8,128)(2,1)}, bf16[3,8,16,2048]{3,2,1,0:T(8,128)(2,1)}, u32[]{:S(2)}, u32[]{:S(2)}) collective-permute-start(bf16[3,8,16,2048]{3,2,1,0:T(8,128)(2,1)} %get-tuple-element.6), channel_id=1, source_target_pairs={{0,1},{1,2},{2,3},{3,4},{4,5},{5,6},{6,7},{7,8},{8,9},{9,10},{10,1... | collective-permute-start | bytes 4718600 | tf_op jit(solution)/shard_map/ppermute | solution.py:258
  134.0 7.7 %collective-permute-start.3 = (bf16[3,8,16,2048]{3,2,1,0:T(8,128)(2,1)}, bf16[3,8,16,2048]{3,2,1,0:T(8,128)(2,1)}, u32[]{:S(2)}, u32[]{:S(2)}) collective-permute-start(bf16[3,8,16,2048]{3,2,1,0:T(8,128)(2,1)} %get-tuple-element.5), channel_id=1, source_target_pairs={{1,0},{2,1},{3,2},{4,3},{5,4},{6,5},{7,6},{8,7},{9,8},{10,9},{11,1... | collective-permute-start | bytes 4718600 | tf_op jit(solution)/shard_map/ppermute | solution.py:259
  141.7 0.0 all-to-all-done
  141.7 0.0 copy-start.4
  141.7 1.3 copy-done.4
  143.1 0.0 copy-start.3
  143.1 3.4 %copy-done.3 = bf16[2048,2048]{1,0:T(8,128)(2,1)S(1)} copy-done((bf16[2048,2048]{1,0:T(8,128)(2,1)S(1)}, bf16[2048,2048]{1,0:T(8,128)(2,1)}, u32[]{:S(2)}) %copy-start.3) | copy-done | bytes 8388632
  146.4 0.0 copy-start.5
  146.4 1.6 copy-done.5
  148.0 0.0 copy-start.8
  148.0 0.0 copy-start.7
  148.0 5.0 %delay_spectra.2.refs_1_.refs_4_ = bf16[1,32,16,2048]{3,2,1,0:T(8,128)(2,1)S(1)} custom-call(bf16[16,8,1,64,128]{4,3,2,1,0:T(8,128)(2,1)S(1)} %bitcast.23, bf16[256,256]{1,0:T(8,128)(2,1)S(1)} %fusion.7.order_ref, bf16[2048,2048]{1,0:T(8,128)(2,1)S(1)} %copy-done.3), custom_call_target="tpu_custom_call" | custom-call | flops 4294967296 | bytes 12582912 | tf_op jit(solution)/shard_map/delay_spectra/pallas_call | solution.py:109
  153.1 1.0 fusion.19
  154.1 1.9 collective-permute-start
  156.0 7.9 %collective-permute-start.1 = (bf16[1,8,16,2048]{3,2,1,0:T(8,128)(2,1)}, bf16[1,8,16,2048]{3,2,1,0:T(8,128)(2,1)S(1)}, u32[]{:S(2)}, u32[]{:S(2)}) collective-permute-start(bf16[1,8,16,2048]{3,2,1,0:T(8,128)(2,1)} %get-tuple-element.7), channel_id=1, source_target_pairs={{1,0},{2,1},{3,2},{4,3},{5,4},{6,5},{7,6},{8,7},{9,8},{10,9},{11,1... | collective-permute-start | bytes 1572872 | tf_op jit(solution)/shard_map/ppermute | solution.py:259
  163.9 0.0 copy-done.8
  163.9 0.1 pad_dynamic-slice_fusion.1
  164.0 0.1 compare_bitcast_fusion
  164.1 0.0 copy-done.7
  164.1 0.1 and_convert_fusion
  164.2 0.1 copy.7
  164.3 0.0 collective-permute-done.2.refs_0_.refs_3_
  164.3 0.0 collective-permute-done.3.refs_2_.refs_5_
  164.3 0.0 copy-start.1
  164.3 2.8 %copy-done.1 = bf16[3,32,16,2048]{3,2,1,0:T(8,128)(2,1)S(1)} copy-done((bf16[3,32,16,2048]{3,2,1,0:T(8,128)(2,1)S(1)}, bf16[3,32,16,2048]{3,2,1,0:T(8,128)(2,1)}, u32[]{:S(2)}) %copy-start.1) | copy-done | bytes 6291480
  167.1 18.0 %pair_powers.2.refs_6_ = f32[40,8,1024]{2,1,0:T(8,128)S(1)} custom-call(bf16[3,8,16,2048]{3,2,1,0:T(8,128)(2,1)} %collective-permute-done.2.refs_0_.refs_3_, bf16[3,32,16,2048]{3,2,1,0:T(8,128)(2,1)S(1)} %copy-done.1, bf16[3,8,16,2048]{3,2,1,0:T(8,128)(2,1)} %collective-permute-done.3.refs_2_.refs_5_, ...), custom_call_target="tpu_custom_call" | custom-call | flops 62914560 | bytes 9437184 | tf_op jit(solution)/shard_map/pair_powers/pallas_call | solution.py:205
  185.1 0.0 collective-permute-done.refs_0_.refs_3_
  185.1 0.0 collective-permute-done.1.refs_2_.refs_5_
  185.1 0.1 broadcast_in_dim.2.refs_7_
  185.2 13.1 %pair_powers.3 = f32[32,16,1024]{2,1,0:T(8,128)} custom-call(bf16[1,8,16,2048]{3,2,1,0:T(8,128)(2,1)S(1)} %collective-permute-done.refs_0_.refs_3_, bf16[1,32,16,2048]{3,2,1,0:T(8,128)(2,1)S(1)} %delay_spectra.2.refs_1_.refs_4_, bf16[1,8,16,2048]{3,2,1,0:T(8,128)(2,1)S(1)} %collective-permute-done.1.refs_2_.refs_5_, ...), custom_call_target="tpu_custom_call" | custom-call | flops 20971520 | bytes 3145728 | tf_op jit(solution)/shard_map/pair_powers/pallas_call | solution.py:205
  (2 shorter events, 0.0 us)
Async XLA Ops:
  0.0 5.6 %copy-start.6 = (s32[4096]{0:T(1024)S(1)}, s32[4096]{0:T(1024)}, u32[]{:S(2)}) copy-start(s32[4096]{0:T(1024)} %order_ref.3) | copy-start | bytes 49156
  13.7 2.6 %copy-start.2 = (bf16[128,3,32,2,128]{4,3,2,1,0:T(2,128)(2,1)}, bf16[128,3,32,2,128]{4,3,2,1,0:T(2,128)(2,1)S(1)}, u32[]{:S(2)}) copy-start(bf16[128,3,32,2,128]{4,3,2,1,0:T(2,128)(2,1)S(1)} %slot_gather.3) | copy-start | bytes 18874372
  16.3 84.5 %all-to-all-start.1 = ((bf16[128,3,64,128]{3,2,1,0:T(8,128)(2,1)}), bf16[128,3,64,128]{3,2,1,0:T(8,128)(2,1)}, u32[]{:S(2)}, u32[]{:S(2)}) async-start(bf16[128,3,64,128]{3,2,1,0:T(8,128)(2,1)} %bitcast.22), calls=%async_computation.1 | async-start | bytes 12582912 | tf_op jit(solution)/shard_map/all_to_all | solution.py:256
  100.8 40.9 %all-to-all-start = ((bf16[128,1,64,128]{3,2,1,0:T(8,128)(2,1)}), bf16[128,1,64,128]{3,2,1,0:T(8,128)(2,1)S(1)}, u32[]{:S(2)}, u32[]{:S(2)}) async-start(bf16[128,1,64,128]{3,2,1,0:T(8,128)(2,1)} %bitcast.1), calls=%async_computation | async-start | bytes 4194304 | tf_op jit(solution)/shard_map/all_to_all | solution.py:256
  129.2 2.7 %copy-start = (bf16[3,32,16,2048]{3,2,1,0:T(8,128)(2,1)}, bf16[3,32,16,2048]{3,2,1,0:T(8,128)(2,1)S(1)}, u32[]{:S(2)}) copy-start(bf16[3,32,16,2048]{3,2,1,0:T(8,128)(2,1)S(1)} %delay_spectra.3.refs_1_.refs_4_) | copy-start | bytes 18874372
  131.9 32.4 %collective-permute-start.2 = (bf16[3,8,16,2048]{3,2,1,0:T(8,128)(2,1)}, bf16[3,8,16,2048]{3,2,1,0:T(8,128)(2,1)}, u32[]{:S(2)}, u32[]{:S(2)}) collective-permute-start(bf16[3,8,16,2048]{3,2,1,0:T(8,128)(2,1)} %get-tuple-element.6), channel_id=1, source_target_pairs={{0,1},{1,2},{2,3},{3,4},{4,5},{5,6},{6,7},{7,8},{8,9},{9,10},{10,1... | collective-permute-start | bytes 4718600 | tf_op jit(solution)/shard_map/ppermute | solution.py:258
  134.0 30.3 %collective-permute-start.3 = (bf16[3,8,16,2048]{3,2,1,0:T(8,128)(2,1)}, bf16[3,8,16,2048]{3,2,1,0:T(8,128)(2,1)}, u32[]{:S(2)}, u32[]{:S(2)}) collective-permute-start(bf16[3,8,16,2048]{3,2,1,0:T(8,128)(2,1)} %get-tuple-element.5), channel_id=1, source_target_pairs={{1,0},{2,1},{3,2},{4,3},{5,4},{6,5},{7,6},{8,7},{9,8},{10,9},{11,1... | collective-permute-start | bytes 4718600 | tf_op jit(solution)/shard_map/ppermute | solution.py:259
  141.7 1.3 copy-start.4
  143.1 3.4 %copy-start.3 = (bf16[2048,2048]{1,0:T(8,128)(2,1)S(1)}, bf16[2048,2048]{1,0:T(8,128)(2,1)}, u32[]{:S(2)}) copy-start(bf16[2048,2048]{1,0:T(8,128)(2,1)} %maximum_maximum_fusion.table_ref) | copy-start | bytes 25165828
  146.4 1.6 copy-start.5
  148.0 15.9 %copy-start.8 = (s32[4096]{0:T(1024)S(1)}, s32[4096]{0:T(1024)}, u32[]{:S(2)}) copy-start(s32[4096]{0:T(1024)} %param.6) | copy-start | bytes 49156
  148.0 16.1 %copy-start.7 = (s32[4096,8]{0,1:T(8,128)S(1)}, s32[4096,8]{0,1:T(8,128)}, u32[]{:S(2)}) copy-start(s32[4096,8]{0,1:T(8,128)} %param.7) | copy-start | bytes 393220
  154.1 31.0 %collective-permute-start = (bf16[1,8,16,2048]{3,2,1,0:T(8,128)(2,1)}, bf16[1,8,16,2048]{3,2,1,0:T(8,128)(2,1)S(1)}, u32[]{:S(2)}, u32[]{:S(2)}) collective-permute-start(bf16[1,8,16,2048]{3,2,1,0:T(8,128)(2,1)} %get-tuple-element.8), channel_id=1, source_target_pairs={{0,1},{1,2},{2,3},{3,4},{4,5},{5,6},{6,7},{7,8},{8,9},{9,10},{10,1... | collective-permute-start | bytes 1572872 | tf_op jit(solution)/shard_map/ppermute | solution.py:258
  156.0 29.1 %collective-permute-start.1 = (bf16[1,8,16,2048]{3,2,1,0:T(8,128)(2,1)}, bf16[1,8,16,2048]{3,2,1,0:T(8,128)(2,1)S(1)}, u32[]{:S(2)}, u32[]{:S(2)}) collective-permute-start(bf16[1,8,16,2048]{3,2,1,0:T(8,128)(2,1)} %get-tuple-element.7), channel_id=1, source_target_pairs={{1,0},{2,1},{3,2},{4,3},{5,4},{6,5},{7,6},{8,7},{9,8},{10,9},{11,1... | collective-permute-start | bytes 1572872 | tf_op jit(solution)/shard_map/ppermute | solution.py:259
  164.3 2.8 %copy-start.1 = (bf16[3,32,16,2048]{3,2,1,0:T(8,128)(2,1)S(1)}, bf16[3,32,16,2048]{3,2,1,0:T(8,128)(2,1)}, u32[]{:S(2)}) copy-start(bf16[3,32,16,2048]{3,2,1,0:T(8,128)(2,1)} %copy-done) | copy-start | bytes 18874372

commit v2 on v0

v2 whole, which is shorter than its diff:
```python
import functools
import math

import jax
import jax.numpy as jnp
from jax import lax
from jax.experimental import pallas as pl
from jax.experimental.pallas import tpu as pltpu
from jax.sharding import PartitionSpec as P

AXES = ("tm", "chan")
MIB = 2**20
LANES = 128
REACH = 8
OUTER = tuple(range(8)) + tuple(range(24, 32))
INNER = tuple(range(8, 24))


def in_hbm(array):
    return pltpu.with_memory_space_constraint(array, pltpu.HBM)


def half_table(n_chan):
    channel_index = jnp.arange(n_chan, dtype=jnp.int32)
    place = jnp.arange(n_chan, dtype=jnp.int32)
    delay_index = place // (2 * LANES) * LANES + place % LANES
    is_sine = place % (2 * LANES) >= LANES
    middle = is_sine & (delay_index == 0)
    delay_index = jnp.where(middle, n_chan // 2, delay_index)
    turn = jnp.where(is_sine & ~middle, 3 * n_chan // 4, 0)
    phase_index = (channel_index[:, None] * delay_index[None, :] + turn[None, :]) % n_chan
    phase_angle = 2.0 * math.pi / n_chan * phase_index.astype(jnp.float32)
    base_angle = 2.0 * math.pi / n_chan * channel_index.astype(jnp.float32)
    window_taper = (
        0.35875
        - 0.48829 * jnp.cos(base_angle)
        + 0.14128 * jnp.cos(2.0 * base_angle)
        - 0.01168 * jnp.cos(3.0 * base_angle)
    )
    weights_norm = window_taper / jnp.sqrt(jnp.sum(window_taper * window_taper))
    return (weights_norm[:, None] * jnp.cos(phase_angle)).astype(jnp.bfloat16)


def gather_kernel(slots, per, order_ref, vis_ref, _, out_ref):
    owners, count = out_ref.shape[0], out_ref.shape[2]
    first = pl.program_id(0) * owners

    def one_owner(owner, carry):
        base = (first + owner) * per
        for j, slot in enumerate(slots):
            source = order_ref[base + slot]
            for t in range(count):
                out_ref[owner, j, t] = vis_ref[t, source]
        return carry

    lax.fori_loop(0, owners, one_owner, 0)


def gather(visibilities, order, slots, n_dev, earlier):
    count, n_base = visibilities.shape[:2]
    tail = visibilities.shape[2:]
    steps = 8
    return pl.pallas_call(
        functools.partial(gather_kernel, slots, n_base // n_dev),
        grid_spec=pltpu.PrefetchScalarGridSpec(
            num_scalar_prefetch=1,
            grid=(steps,),
            in_specs=[
                pl.BlockSpec(memory_space=pltpu.VMEM),
                pl.BlockSpec(memory_space=pl.ANY),
            ],
            out_specs=pl.BlockSpec(
                (n_dev // steps, len(slots), count) + tail, lambda i, o: (i, 0, 0, 0, 0)
            ),
        ),
        out_shape=pltpu.HBM((n_dev, len(slots), count) + tail, visibilities.dtype),
        compiler_params=pltpu.CompilerParams(vmem_limit_bytes=24 * MIB),
        cost_estimate=pl.CostEstimate(
            flops=0, bytes_accessed=2 * count * n_dev * len(slots) * 512, transcendentals=0
        ),
        name="slot_gather",
    )(in_hbm(order), visibilities, in_hbm(earlier))


def spectra_kernel(received_ref, table_ref, out_ref):
    sources, n_chan, rows = received_ref.shape[:3]
    slots = out_ref.shape[2]
    n_rows = sources * rows
    block = jnp.concatenate(
        [received_ref[:, c].reshape(n_rows, LANES) for c in range(n_chan)], axis=1
    )
    chunks = table_ref.shape[1] // (2 * LANES)
    shape = (n_rows // 8, 8, LANES)
    first = lax.broadcasted_iota(jnp.int32, shape, 2) == 0
    is_real = lax.broadcasted_iota(jnp.int32, shape, 1) % 2 == 0

    def store(sign, c, value):
        value = jnp.swapaxes(value.reshape(sources, slots, 8, LANES), 0, 1)
        value = value.reshape(slots, sources * 8, LANES).astype(jnp.bfloat16)
        out_ref[sign, c] = value

    minus = []
    for c in range(chunks):
        both = jnp.dot(
            block, table_ref[:, pl.ds(2 * c * LANES, 2 * LANES)], preferred_element_type=jnp.float32
        )
        cosine, sine = both[:, :LANES].reshape(shape), both[:, LANES:].reshape(shape)
        other = jnp.where(is_real, pltpu.roll(sine, 7, 1), -pltpu.roll(sine, 1, 1))
        ahead, back = cosine + other, cosine - other
        if c == 0:
            ahead, back = jnp.where(first, cosine, ahead), jnp.where(first, sine, back)
        store(0, c, ahead)
        minus.append(back)
        if c > 0:
            store(1, c - 1, jnp.where(first, back, minus[c - 1]))
    store(1, chunks - 1, jnp.where(first, minus[0], minus[-1]))


def spectra(received, table, n_tm, n_chan):
    _, pairs, lanes = received.shape
    slots = pairs // 8
    step = REACH
    width = table.shape[1]
    rows = n_tm * 8
    chunks = width // (2 * LANES)
    return pl.pallas_call(
        spectra_kernel,
        grid=(slots // step,),
        in_specs=[
            pl.BlockSpec((n_tm, n_chan, 8 * step, lanes), lambda t: (0, 0, t, 0)),
            pl.BlockSpec(table.shape, lambda t: (0, 0), pipeline_mode=pl.Buffered(1)),
        ],
        out_specs=pl.BlockSpec((2, chunks, step, rows, LANES), lambda t: (0, 0, t, 0, 0)),
        out_shape=pltpu.HBM((2, chunks, slots, rows, LANES), jnp.bfloat16),
        compiler_params=pltpu.CompilerParams(vmem_limit_bytes=32 * MIB),
        cost_estimate=pl.CostEstimate(
            flops=2 * pairs * n_tm * width * width,
            bytes_accessed=8 * pairs * n_tm * width,
            transcendentals=0,
        ),
        name="delay_spectra",
    )(in_hbm(received.reshape(n_tm, n_chan, pairs, lanes)), in_hbm(table))


def fold_rows(sums):
    row = lax.broadcasted_iota(jnp.int32, sums[0].shape, 0)
    for bit in (1, 2, 4):
        low = (row & bit) == 0
        merged = []
        for i in range(0, len(sums), 2):
            a, b = sums[i], sums[i + 1]
            kept, moved = jnp.where(low, a, b), jnp.where(low, b, a)
            merged.append(kept + pltpu.roll(moved, 8 - bit, 0))
        sums = merged
    return sums[0]


def cross_tile(rows_ref, s, offsets):
    spans = [pl.ds(8 * g, 8) for g in range(rows_ref.shape[1] // 8)]
    own = [rows_ref[s, span] for span in spans]
    sums = []
    for k in range(1, REACH + 1):
        if k not in offsets:
            sums.append(jnp.zeros((8, LANES), jnp.float32))
            continue
        total = None
        for g, span in enumerate(spans):
            term = own[g] * rows_ref[s + k, span]
            total = term if total is None else total + term
        sums.append(total)
    return fold_rows(sums)


def load_rows(target, at, source):
    target[pl.ds(at, source.shape[0])] = source[...].astype(jnp.float32)


def outer_kernel(rows_in, out_ref, rows_ref):
    load_rows(rows_ref, 0, rows_in.at[0, 0])
    run = out_ref.shape[1] // 2

    def one_run(i, carry):
        for j in range(run):
            s = i * run + j
            out_ref[0, s] = cross_tile(rows_ref, s, range(1, run - j))
        return carry

    lax.fori_loop(0, 2, one_run, 0)


def edge_kernel(own, after, before, _, plus_ref, minus_ref, rows_ref):
    sign = pl.program_id(0)

    @pl.when(sign == 0)
    def _():
        load_rows(rows_ref, 0, own.at[0, 0])
        load_rows(rows_ref, REACH, after.at[0])

    @pl.when(sign == 1)
    def _():
        load_rows(rows_ref, 0, before.at[0])
        load_rows(rows_ref, REACH, own.at[0, 0])

    tiles = [cross_tile(rows_ref, j, range(REACH - j, REACH + 1)) for j in range(REACH)]

    @pl.when(sign == 0)
    def _():
        for j in range(REACH):
            plus_ref[0, j] = tiles[j]

    @pl.when(sign == 1)
    def _():
        for j in range(REACH):
            minus_ref[0, j] = tiles[j]


def final_kernel(
    outer, inner, sums_ref, plus_ref, minus_ref, left_ref, right_ref, valid_ref,
    out_ref, rows_ref,
):
    shape = (REACH, LANES)
    lane = lax.broadcasted_iota(jnp.int32, shape, 1)
    row = lax.broadcasted_iota(jnp.int32, shape, 0)
    mirror = pl.program_id(0) == 1
    order = jnp.where(mirror, (LANES - lane) % LANES, lane)
    slots = out_ref.shape[0]
    load_rows(rows_ref, 0, outer.at[0, 0, pl.ds(0, REACH)])
    load_rows(rows_ref, REACH, inner.at[0, 0])
    load_rows(rows_ref, slots - REACH, outer.at[0, 0, pl.ds(REACH, REACH)])
    powers = {}
    for s in range(-REACH, slots):
        terms = []
        if s < 0:
            terms.append(jnp.where(mirror, minus_ref[0, s + REACH], left_ref[0, s + REACH]))
        if s in OUTER:
            terms.append(sums_ref[0, OUTER.index(s)])
        if 0 <= s < slots - REACH:
            terms.append(cross_tile(rows_ref, s, range(max(1, REACH - s), REACH + 1)))
        if s >= slots - REACH:
            j = s - (slots - REACH)
            terms.append(jnp.where(mirror, right_ref[0, j], plus_ref[0, j]))
        value = jnp.take_along_axis(sum(terms[1:], terms[0]), order, axis=1)
        powers[s] = jnp.where(valid_ref[s + REACH] > 0.0, value * (1.0 / 64.0), 0.0)
        if s >= 0:
            out_ref[s, pl.ds(0, REACH), :] = powers[s]
            backward = powers[s - 1]
            for k in range(2, REACH + 1):
                backward = jnp.where(row == k - 1, powers[s - k], backward)
            out_ref[s, pl.ds(REACH, REACH), :] = backward


CHUNKS = 4


def cross_call(kernel, name, operands, specs, out_specs, out_shape, held, pairs):
    rows = 128
    return pl.pallas_call(
        kernel,
        grid=(2, CHUNKS),
        in_specs=specs,
        out_specs=out_specs,
        out_shape=out_shape,
        scratch_shapes=[pltpu.VMEM((held, rows, LANES), jnp.float32)],
        compiler_params=pltpu.CompilerParams(vmem_limit_bytes=24 * MIB),
        cost_estimate=pl.CostEstimate(
            flops=2 * pairs * rows * 1024,
            bytes_accessed=2 * held * rows * 1024,
            transcendentals=0,
        ),
        name=name,
    )(*operands)


def spectra_spec(slots, rows, place=lambda i: 0):
    return pl.BlockSpec((1, 1, slots, rows, LANES), lambda i, j: (i, j, place(i), 0, 0))


def sums_spec(slots):
    return pl.BlockSpec((1, slots, REACH, LANES), lambda i, j: (i * CHUNKS + j, 0, 0, 0))


def plus_spec(rows=REACH):
    return pl.BlockSpec(
        (1, REACH, rows, LANES), lambda i, j: (jnp.where(i == 0, j, CHUNKS - 1), 0, 0, 0)
    )


def minus_spec(rows=REACH):
    return pl.BlockSpec((1, REACH, rows, LANES), lambda i, j: (jnp.where(i == 0, 0, j), 0, 0, 0))


def outer_powers(outer):
    slots, rows = outer.shape[2:4]
    shape = jax.ShapeDtypeStruct((2 * CHUNKS, slots, REACH, LANES), jnp.float32)
    return cross_call(
        outer_kernel,
        "outer_pairs",
        [in_hbm(outer)],
        [spectra_spec(slots, rows)],
        sums_spec(slots),
        shape,
        slots,
        56,
    )


def edge_powers(outer, after, before, outer_sums):
    slots, rows = outer.shape[2:4]
    last = slots // REACH - 1
    shape = jax.ShapeDtypeStruct((CHUNKS, REACH, REACH, LANES), jnp.float32)
    return cross_call(
        edge_kernel,
        "edge_pairs",
        [in_hbm(outer), after, before, outer_sums],
        [
            spectra_spec(REACH, rows, lambda i: (1 - i) * last),
            plus_spec(rows),
            minus_spec(rows),
            pl.BlockSpec(memory_space=pl.ANY),
        ],
        [plus_spec(), minus_spec()],
        [shape, shape],
        2 * REACH,
        36,
    )


def final_powers(outer, inner, outer_sums, plus, minus, left, right, valid):
    rows = outer.shape[3]
    slots = 4 * REACH
    return cross_call(
        final_kernel,
        "pair_power",
        [in_hbm(outer), in_hbm(inner), outer_sums, plus, minus, left, right, valid],
        [
            spectra_spec(outer.shape[2], rows),
            spectra_spec(inner.shape[2], rows),
            sums_spec(outer_sums.shape[1]),
            plus_spec(),
            minus_spec(),
            plus_spec(),
            minus_spec(),
            pl.BlockSpec(valid.shape, lambda i, j: (0, 0, 0)),
        ],
        pl.BlockSpec(
            (slots, 2 * REACH, LANES),
            lambda i, j: (0, 0, jnp.where(i == 0, j, 2 * CHUNKS - 1 - j)),
        ),
        jax.ShapeDtypeStruct((slots, 2 * REACH, 2 * CHUNKS * LANES), jnp.float32),
        slots,
        164,
    )


def body(visibilities, owner_order, group_ids, partner_flags):
    n_tm = lax.axis_size("tm")
    n_chan = lax.axis_size("chan")
    n_dev = n_tm * n_chan
    count, n_base, _, width = visibilities.shape
    per = n_base // n_dev

    table = half_table(width * n_chan)

    start = lax.axis_index(AXES) * per
    groups = lax.dynamic_slice_in_dim(
        jnp.pad(group_ids, (REACH, REACH), constant_values=-1), start, per + 2 * REACH, 0
    )
    flags = lax.dynamic_slice_in_dim(
        jnp.pad(partner_flags, ((REACH, REACH), (0, 0))), start, per + REACH, 0
    )
    own_group = groups[: per + REACH]
    same = jnp.stack([groups[k : k + per + REACH] == own_group for k in range(1, REACH + 1)], 1)
    valid = jnp.broadcast_to(
        (same & (flags == 1)).astype(jnp.float32)[:, :, None], (per + REACH, REACH, LANES)
    )

    def exchange(slots, earlier):
        send = gather(visibilities, owner_order, slots, n_dev, earlier)
        send = send.reshape(n_dev, 2 * count * len(slots), width)
        return lax.all_to_all(send, AXES, 0, 0, tiled=True)

    up = [(i, i + 1) for i in range(n_dev - 1)]
    down = [(i + 1, i) for i in range(n_dev - 1)]
    received_outer = exchange(OUTER, group_ids)
    received_inner = exchange(INNER, table)
    outer = spectra(received_outer, table, n_tm, n_chan)
    after = lax.ppermute(outer[0, :, :REACH], AXES, down)
    before = lax.ppermute(outer[1, :, REACH:], AXES, up)
    outer_sums = outer_powers(outer)
    plus, minus = edge_powers(outer, after, before, outer_sums)
    left = lax.ppermute(plus, AXES, up)
    right = lax.ppermute(minus, AXES, down)
    inner = spectra(received_inner, table, n_tm, n_chan)
    return final_powers(outer, inner, outer_sums, plus, minus, left, right, valid)


def solution(mesh):
    return jax.shard_map(
        body,
        mesh=mesh,
        in_specs=(P("tm", None, None, "chan"), P(), P(), P()),
        out_specs=P(AXES, None, None),
        check_vma=False,
    )
```

time: 481 us -> 176 us (0.37)
  other arithmetic: 126 us -> 17.4 us
  local copies, waits for them, and re-layouts: 116 us -> 10.2 us
  blocking collectives: 101 us -> 0 us
  Pallas kernels: 0 us -> 53.7 us
  waiting for transfers between devices: 96.1 us -> 57.4 us
  matrix products: 26.1 us -> 0 us
  starting transfers between devices: 11.4 us -> 35.3 us
    all_to_all x1 -> x0, blocking collectives: 101 us -> none  [body(): lax.all_to_all(ordered, 'tm', split_axis=1, concat_axis=0, tiled=True)]
    dot_general x2 -> x0, other arithmetic: 84.4 us -> none  [pair_sum(): jnp.einsum('tbc,tbc->bc', row_spectra, partner_rows, preferred_element_ty...]
    pallas_call x0 -> x7, Pallas kernels: none -> 53.7 us  [the longest x3 22.3 us: cross_call(): pl.pallas_call(kernel, grid=(2, CHUNKS), in_specs=specs, out_specs=out_sp...]
    all_to_all x1 -> x2, waiting for transfers between devices: 74.6 us -> 23 us  [exchange(): return lax.all_to_all(send, AXES, 0, 0, tiled=True)]
    gather x1 -> x0, local copies, waits for them, and re-layouts: 50.3 us -> none  [body(): ordered = jnp.take(visibilities, owner_order, axis=1)]
    all_to_all x4 -> x0, local copies, waits for them, and re-layouts: 44.9 us -> none  [the longest x3 28.6 us: body(): lax.all_to_all(ordered, 'tm', split_axis=1, concat_axis=0, tiled=True)]
    dot_general x1 -> x0, matrix products: 26.1 us -> none  [body(): jnp.dot(flat, delay_matrix, preferred_element_type=jnp.float32)]
    another operation x2 -> x1, other arithmetic: 18.5 us -> 0.08 us  [body(): jnp.stack([groups[k:k + per + REACH] == own_group for k in range(1, REACH...]
  transfers between devices with their start and end apart: 3 -> 6, of which waited for: 2 -> 3; matrix products, arithmetic and copies ran while one was open for 15% -> 12% of each run, Pallas kernels for 0% -> 20%
where the time goes in v2:
time: 176 us; the launch traced here: 175 us
  waiting for transfers between devices  57.4 us (33%)
  Pallas kernels  53.7 us (31%)
  starting transfers between devices  35.3 us (20%)
  other arithmetic  17.4 us (10%)
  local copies, waits for them, and re-layouts  10.2 us (6%)
    ppermute x1, waiting for transfers between devices, body(): after = lax.ppermute(outer[0, :, :REACH], AXES, down)  30.1 us
    all_to_all x2, waiting for transfers between devices, exchange(): return lax.all_to_all(send, AXES, 0, 0, tiled=True)  23 us
    pallas_call x3, Pallas kernels, cross_call(): pl.pallas_call(kernel, grid=(2, CHUNKS), in_specs=specs, out_specs=out_sp...  22.3 us
    all_to_all x2, starting transfers between devices, exchange(): return lax.all_to_all(send, AXES, 0, 0, tiled=True)  17.2 us
    pallas_call x2, Pallas kernels, spectra(): pl.pallas_call(spectra_kernel, grid=(slots // step,), in_specs=[pl.BlockS...  16.8 us
    convert_element_type x1, other arithmetic, half_table(): return (weights_norm[:, None] * jnp.cos(phase_angle)).astype(jnp.bfloat16)  16.5 us
    pallas_call x2, Pallas kernels, gather(): pl.pallas_call(functools.partial(gather_kernel, slots, n_base // n_dev),...  14.7 us
    ppermute x1, starting transfers between devices, body(): right = lax.ppermute(minus, AXES, down)  7.86 us
  transfers between devices with their start and end apart: 6, of which 3 were waited for; matrix products, arithmetic and copies ran while one was open for 12% of the time, Pallas kernels for 20%

profile of v2, /device:TPU:32, one launch (start us, length us, event | category | flops | bytes accessed | tf_op | source)
XLA Modules:
  0.0 175.0 jit_solution(9184951303497698172)
XLA Ops:
  0.0 0.0 copy-start
  0.0 3.4 %copy-done = bf16[4,4096,2,128]{3,2,1,0:T(2,128)(2,1)S(1)} copy-done((bf16[4,4096,2,128]{3,2,1,0:T(2,128)(2,1)S(1)}, bf16[4,4096,2,128]{3,2,1,0:T(2,128)(2,1)}, u32[]{:S(2)}) %copy-start) | copy-done | bytes 8388632
  3.4 7.3 %slot_gather.2 = bf16[128,16,4,2,128]{4,3,2,1,0:T(2,128)(2,1)} custom-call(s32[4096]{0:T(1024)} %order_ref.3, bf16[4,4096,2,128]{3,2,1,0:T(2,128)(2,1)S(1)} %copy-done, s32[4096]{0:T(1024)} %_.1), custom_call_target="tpu_custom_call" | custom-call | bytes 8388608 | tf_op jit(solution)/shard_map/slot_gather/pallas_call | solution.py:63
  10.7 10.7 %all-to-all-start = ((bf16[128,128,128]{2,1,0:T(8,128)(2,1)}), bf16[128,128,128]{2,1,0:T(8,128)(2,1)}, u32[]{:S(2)}, u32[]{:S(2)}) async-start(bf16[128,128,128]{2,1,0:T(8,128)(2,1)} %bitcast.24), calls=%async_computation | async-start | bytes 8388608 | tf_op jit(solution)/shard_map/all_to_all | solution.py:380
  21.4 0.7 multiply_reduce_fusion
  22.7 0.1 fusion.23
  22.8 16.5 %fusion.5.table_ref._ = bf16[1024,1024]{1,0:T(8,128)(2,1)} fusion(s32[1024]{0:T(1024)S(1)} %get-tuple-element.19, s32[1024]{0:T(1024)S(1)} %get-tuple-element.20, f32[1024]{0:T(1024)S(1)} %fusion.23), kind=kLoop, calls=%fused_computation.8 | loop fusion | flops 17825792 | bytes 2109440 | tf_op jit(solution)/shard_map/convert_element_type | solution.py:41
  39.3 0.0 copy-start.1
  39.3 3.4 %copy-done.1 = bf16[4,4096,2,128]{3,2,1,0:T(2,128)(2,1)S(1)} copy-done((bf16[4,4096,2,128]{3,2,1,0:T(2,128)(2,1)S(1)}, bf16[4,4096,2,128]{3,2,1,0:T(2,128)(2,1)}, u32[]{:S(2)}) %copy-start.1) | copy-done | bytes 8388632
  42.7 7.4 %slot_gather.3 = bf16[128,16,4,2,128]{4,3,2,1,0:T(2,128)(2,1)} custom-call(s32[4096]{0:T(1024)} %order_ref.3, bf16[4,4096,2,128]{3,2,1,0:T(2,128)(2,1)S(1)} %copy-done.1, bf16[1024,1024]{1,0:T(8,128)(2,1)} %fusion.5.table_ref._), custom_call_target="tpu_custom_call" | custom-call | bytes 8388608 | tf_op jit(solution)/shard_map/slot_gather/pallas_call | solution.py:63
  50.1 23.0 %all-to-all-done = bf16[128,128,128]{2,1,0:T(8,128)(2,1)} async-done(((bf16[128,128,128]{2,1,0:T(8,128)(2,1)}), bf16[128,128,128]{2,1,0:T(8,128)(2,1)}, u32[]{:S(2)}, u32[]{:S(2)}) %all-to-all-start) | async-done | bytes 4194336 | tf_op jit(solution)/shard_map/all_to_all | solution.py:380
  73.1 6.5 %all-to-all-start.1 = ((bf16[128,128,128]{2,1,0:T(8,128)(2,1)}), bf16[128,128,128]{2,1,0:T(8,128)(2,1)}, u32[]{:S(2)}, u32[]{:S(2)}) async-start(bf16[128,128,128]{2,1,0:T(8,128)(2,1)} %bitcast.25), calls=%async_computation.1 | async-start | bytes 8388608 | tf_op jit(solution)/shard_map/all_to_all | solution.py:380
  79.6 8.4 %delay_spectra.2.rows_in.own.outer = bf16[2,4,16,128,128]{4,3,2,1,0:T(8,128)(2,1)} custom-call(bf16[16,8,128,128]{3,2,1,0:T(8,128)(2,1)} %bitcast.1.received_ref, bf16[1024,1024]{1,0:T(8,128)(2,1)} %fusion.5.table_ref._), custom_call_target="tpu_custom_call" | custom-call | flops 4294967296 | bytes 16777216 | tf_op jit(solution)/shard_map/delay_spectra/pallas_call | solution.py:126
  88.0 0.0 copy-start.3
  88.0 0.0 copy-start.2
  88.0 3.2 %slice_bitcast_fusion = (bf16[4,8,128,128]{3,2,1,0:T(8,128)(2,1)}, bf16[4,8,128,128]{3,2,1,0:T(8,128)(2,1)}) fusion(bf16[2,4,16,128,128]{4,3,2,1,0:T(8,128)(2,1)} %delay_spectra.2.rows_in.own.outer), kind=kLoop, calls=%fused_computation.9 | loop fusion | bytes 4194304 | tf_op jit(solution)/shard_map/squeeze | solution.py:388
  91.2 6.4 %collective-permute-start = (bf16[4,8,128,128]{3,2,1,0:T(8,128)(2,1)}, bf16[4,8,128,128]{3,2,1,0:T(8,128)(2,1)S(1)}, u32[]{:S(2)}, u32[]{:S(2)}) collective-permute-start(bf16[4,8,128,128]{3,2,1,0:T(8,128)(2,1)} %get-tuple-element.10), channel_id=1, source_target_pairs={{1,0},{2,1},{3,2},{4,3},{5,4},{6,5},{7,6},{8,7},{9,8},{10,9},{11,1... | collective-permute-start | bytes 3145736 | tf_op jit(solution)/shard_map/ppermute | solution.py:387
  97.6 1.9 %collective-permute-start.1 = (bf16[4,8,128,128]{3,2,1,0:T(8,128)(2,1)}, bf16[4,8,128,128]{3,2,1,0:T(8,128)(2,1)S(1)}, u32[]{:S(2)}, u32[]{:S(2)}) collective-permute-start(bf16[4,8,128,128]{3,2,1,0:T(8,128)(2,1)} %get-tuple-element.9), channel_id=1, source_target_pairs={{0,1},{1,2},{2,3},{3,4},{4,5},{5,6},{6,7},{7,8},{8,9},{9,10},{10,1... | collective-permute-start | bytes 3145736 | tf_op jit(solution)/shard_map/ppermute | solution.py:388
  99.5 0.0 copy-done.3
  99.6 0.1 pad_dynamic-slice_fusion.1
  99.6 0.1 compare_bitcast_fusion
  99.8 0.0 copy-done.2
  99.8 0.1 and_convert_fusion
  99.8 0.1 copy.5
  99.9 6.2 %outer_pairs.1._.sums_ref = f32[8,16,8,128]{3,2,1,0:T(8,128)S(1)} custom-call(bf16[2,4,16,128,128]{4,3,2,1,0:T(8,128)(2,1)} %delay_spectra.2.rows_in.own.outer), custom_call_target="tpu_custom_call" | custom-call | flops 14680064 | bytes 4194304 | tf_op jit(solution)/shard_map/outer_pairs/pallas_call | solution.py:257
  106.1 30.1 %collective-permute-done.after = bf16[4,8,128,128]{3,2,1,0:T(8,128)(2,1)S(1)} collective-permute-done((bf16[4,8,128,128]{3,2,1,0:T(8,128)(2,1)}, bf16[4,8,128,128]{3,2,1,0:T(8,128)(2,1)S(1)}, u32[]{:S(2)}, u32[]{:S(2)}) %collective-permute-start) | collective-permute-done | bytes 1048608 | tf_op jit(solution)/shard_map/ppermute | solution.py:387
  136.2 4.3 %collective-permute-done.1.before = bf16[4,8,128,128]{3,2,1,0:T(8,128)(2,1)S(1)} collective-permute-done((bf16[4,8,128,128]{3,2,1,0:T(8,128)(2,1)}, bf16[4,8,128,128]{3,2,1,0:T(8,128)(2,1)S(1)}, u32[]{:S(2)}, u32[]{:S(2)}) %collective-permute-start.1) | collective-permute-done | bytes 1048608 | tf_op jit(solution)/shard_map/ppermute | solution.py:388
  140.6 5.2 %edge_pairs.1 = (f32[4,8,8,128]{3,2,1,0:T(8,128)S(1)}, f32[4,8,8,128]{3,2,1,0:T(8,128)S(1)}) custom-call(bf16[2,4,16,128,128]{4,3,2,1,0:T(8,128)(2,1)} %delay_spectra.2.rows_in.own.outer, bf16[4,8,128,128]{3,2,1,0:T(8,128)(2,1)S(1)} %collective-permute-done.after, bf16[4,8,128,128]{3,2,1,0:T(8,128)(2,1)S(1)} %collective-permute-done.1.before, ...), custom_call_target="tpu_custom_call" | custom-call | flops 9437184 | bytes 4194304 | tf_op jit(solution)/shard_map/edge_pairs/pallas_call | solution.py:257
  145.8 1.9 %collective-permute-start.2 = (f32[4,8,8,128]{3,2,1,0:T(8,128)S(1)}, f32[4,8,8,128]{3,2,1,0:T(8,128)S(1)}, u32[]{:S(2)}, u32[]{:S(2)}) collective-permute-start(f32[4,8,8,128]{3,2,1,0:T(8,128)S(1)} %get-tuple-element.7.plus_ref), channel_id=1, source_target_pairs={{0,1},{1,2},{2,3},{3,4},{4,5},{5,6},{6,7},{7,8},{8,9},{9,10},{10,1... | collective-permute-start | bytes 393224 | tf_op jit(solution)/shard_map/ppermute | solution.py:391
  147.7 7.9 %collective-permute-start.3 = (f32[4,8,8,128]{3,2,1,0:T(8,128)S(1)}, f32[4,8,8,128]{3,2,1,0:T(8,128)S(1)}, u32[]{:S(2)}, u32[]{:S(2)}) collective-permute-start(f32[4,8,8,128]{3,2,1,0:T(8,128)S(1)} %get-tuple-element.8.minus_ref), channel_id=1, source_target_pairs={{1,0},{2,1},{3,2},{4,3},{5,4},{6,5},{7,6},{8,7},{9,8},{10,9},{11,1... | collective-permute-start | bytes 393224 | tf_op jit(solution)/shard_map/ppermute | solution.py:392
  155.6 0.0 all-to-all-done.1
  155.6 8.4 %delay_spectra.3.inner = bf16[2,4,16,128,128]{4,3,2,1,0:T(8,128)(2,1)} custom-call(bf16[16,8,128,128]{3,2,1,0:T(8,128)(2,1)} %bitcast.3.received_ref, bf16[1024,1024]{1,0:T(8,128)(2,1)} %fusion.5.table_ref._), custom_call_target="tpu_custom_call" | custom-call | flops 4294967296 | bytes 16777216 | tf_op jit(solution)/shard_map/delay_spectra/pallas_call | solution.py:126
  164.0 0.0 collective-permute-done.2.left_ref
  164.0 0.0 collective-permute-done.3.right_ref
  164.0 0.1 broadcast_in_dim.22.valid_ref
  164.1 10.8 %pair_power.1 = f32[32,16,1024]{2,1,0:T(8,128)} custom-call(bf16[2,4,16,128,128]{4,3,2,1,0:T(8,128)(2,1)} %delay_spectra.2.rows_in.own.outer, bf16[2,4,16,128,128]{4,3,2,1,0:T(8,128)(2,1)} %delay_spectra.3.inner, f32[8,16,8,128]{3,2,1,0:T(8,128)S(1)} %outer_pairs.1._.sums_ref, f32[4,8,8,128]{3,2,1,0:T(8,128)S(1)} %get-tuple-element.7.plus_ref, ...), custom_call_target="tpu_custom_call" | custom-call | flops 42991616 | bytes 8388608 | tf_op jit(solution)/shard_map/pair_power/pallas_call | solution.py:257
  (2 shorter events, 0.0 us)
Async XLA Ops:
  0.0 3.4 %copy-start = (bf16[4,4096,2,128]{3,2,1,0:T(2,128)(2,1)S(1)}, bf16[4,4096,2,128]{3,2,1,0:T(2,128)(2,1)}, u32[]{:S(2)}) copy-start(bf16[4,4096,2,128]{3,2,1,0:T(2,128)(2,1)} %vis_ref.3) | copy-start | bytes 25165828
  10.7 62.4 %all-to-all-start = ((bf16[128,128,128]{2,1,0:T(8,128)(2,1)}), bf16[128,128,128]{2,1,0:T(8,128)(2,1)}, u32[]{:S(2)}, u32[]{:S(2)}) async-start(bf16[128,128,128]{2,1,0:T(8,128)(2,1)} %bitcast.24), calls=%async_computation | async-start | bytes 8388608 | tf_op jit(solution)/shard_map/all_to_all | solution.py:380
  39.3 3.4 %copy-start.1 = (bf16[4,4096,2,128]{3,2,1,0:T(2,128)(2,1)S(1)}, bf16[4,4096,2,128]{3,2,1,0:T(2,128)(2,1)}, u32[]{:S(2)}) copy-start(bf16[4,4096,2,128]{3,2,1,0:T(2,128)(2,1)} %vis_ref.3) | copy-start | bytes 25165828
  73.1 82.5 %all-to-all-start.1 = ((bf16[128,128,128]{2,1,0:T(8,128)(2,1)}), bf16[128,128,128]{2,1,0:T(8,128)(2,1)}, u32[]{:S(2)}, u32[]{:S(2)}) async-start(bf16[128,128,128]{2,1,0:T(8,128)(2,1)} %bitcast.25), calls=%async_computation.1 | async-start | bytes 8388608 | tf_op jit(solution)/shard_map/all_to_all | solution.py:380
  88.0 11.5 %copy-start.3 = (s32[4096]{0:T(1024)S(1)}, s32[4096]{0:T(1024)}, u32[]{:S(2)}) copy-start(s32[4096]{0:T(1024)} %_.1) | copy-start | bytes 49156
  88.0 11.7 %copy-start.2 = (s32[4096,8]{0,1:T(8,128)S(1)}, s32[4096,8]{0,1:T(8,128)}, u32[]{:S(2)}) copy-start(s32[4096,8]{0,1:T(8,128)} %param.7) | copy-start | bytes 393220
  91.2 45.1 %collective-permute-start = (bf16[4,8,128,128]{3,2,1,0:T(8,128)(2,1)}, bf16[4,8,128,128]{3,2,1,0:T(8,128)(2,1)S(1)}, u32[]{:S(2)}, u32[]{:S(2)}) collective-permute-start(bf16[4,8,128,128]{3,2,1,0:T(8,128)(2,1)} %get-tuple-element.10), channel_id=1, source_target_pairs={{1,0},{2,1},{3,2},{4,3},{5,4},{6,5},{7,6},{8,7},{9,8},{10,9},{11,1... | collective-permute-start | bytes 3145736 | tf_op jit(solution)/shard_map/ppermute | solution.py:387
  97.6 43.0 %collective-permute-start.1 = (bf16[4,8,128,128]{3,2,1,0:T(8,128)(2,1)}, bf16[4,8,128,128]{3,2,1,0:T(8,128)(2,1)S(1)}, u32[]{:S(2)}, u32[]{:S(2)}) collective-permute-start(bf16[4,8,128,128]{3,2,1,0:T(8,128)(2,1)} %get-tuple-element.9), channel_id=1, source_target_pairs={{0,1},{1,2},{2,3},{3,4},{4,5},{5,6},{6,7},{7,8},{8,9},{9,10},{10,1... | collective-permute-start | bytes 3145736 | tf_op jit(solution)/shard_map/ppermute | solution.py:388
  145.8 18.2 %collective-permute-start.2 = (f32[4,8,8,128]{3,2,1,0:T(8,128)S(1)}, f32[4,8,8,128]{3,2,1,0:T(8,128)S(1)}, u32[]{:S(2)}, u32[]{:S(2)}) collective-permute-start(f32[4,8,8,128]{3,2,1,0:T(8,128)S(1)} %get-tuple-element.7.plus_ref), channel_id=1, source_target_pairs={{0,1},{1,2},{2,3},{3,4},{4,5},{5,6},{6,7},{7,8},{8,9},{9,10},{10,1... | collective-permute-start | bytes 393224 | tf_op jit(solution)/shard_map/ppermute | solution.py:391
  147.7 16.3 %collective-permute-start.3 = (f32[4,8,8,128]{3,2,1,0:T(8,128)S(1)}, f32[4,8,8,128]{3,2,1,0:T(8,128)S(1)}, u32[]{:S(2)}, u32[]{:S(2)}) collective-permute-start(f32[4,8,8,128]{3,2,1,0:T(8,128)S(1)} %get-tuple-element.8.minus_ref), channel_id=1, source_target_pairs={{1,0},{2,1},{3,2},{4,3},{5,4},{6,5},{7,6},{8,7},{9,8},{10,9},{11,1... | collective-permute-start | bytes 393224 | tf_op jit(solution)/shard_map/ppermute | solution.py:392

commit v3 on v2

--- a/solution.py
+++ b/solution.py
@@ -82,7 +82,7 @@
     )(in_hbm(order), visibilities, in_hbm(earlier))
 
 
-def spectra_kernel(received_ref, table_ref, out_ref):
+def spectra_kernel(received_ref, table_ref, _, out_ref):
     sources, n_chan, rows = received_ref.shape[:3]
     slots = out_ref.shape[2]
     n_rows = sources * rows
@@ -116,9 +116,8 @@
     store(1, chunks - 1, jnp.where(first, minus[0], minus[-1]))
 
 
-def spectra(received, table, n_tm, n_chan):
+def spectra(received, table, n_tm, n_chan, first, slots, earlier):
     _, pairs, lanes = received.shape
-    slots = pairs // 8
     step = REACH
     width = table.shape[1]
     rows = n_tm * 8
@@ -127,19 +126,22 @@
         spectra_kernel,
         grid=(slots // step,),
         in_specs=[
-            pl.BlockSpec((n_tm, n_chan, 8 * step, lanes), lambda t: (0, 0, t, 0)),
+            pl.BlockSpec(
+                (n_tm, n_chan, 8 * step, lanes), lambda t: (0, 0, first // step + t, 0)
+            ),
             pl.BlockSpec(table.shape, lambda t: (0, 0), pipeline_mode=pl.Buffered(1)),
+            pl.BlockSpec(memory_space=pl.ANY),
         ],
         out_specs=pl.BlockSpec((2, chunks, step, rows, LANES), lambda t: (0, 0, t, 0, 0)),
         out_shape=pltpu.HBM((2, chunks, slots, rows, LANES), jnp.bfloat16),
         compiler_params=pltpu.CompilerParams(vmem_limit_bytes=32 * MIB),
         cost_estimate=pl.CostEstimate(
-            flops=2 * pairs * n_tm * width * width,
-            bytes_accessed=8 * pairs * n_tm * width,
+            flops=16 * slots * n_tm * width * width,
+            bytes_accessed=64 * slots * n_tm * width,
             transcendentals=0,
         ),
         name="delay_spectra",
-    )(in_hbm(received.reshape(n_tm, n_chan, pairs, lanes)), in_hbm(table))
+    )(in_hbm(received.reshape(n_tm, n_chan, pairs, lanes)), in_hbm(table), earlier)
 
 
 def fold_rows(sums):
@@ -175,70 +177,47 @@
     target[pl.ds(at, source.shape[0])] = source[...].astype(jnp.float32)
 
 
-def outer_kernel(rows_in, out_ref, rows_ref):
-    load_rows(rows_ref, 0, rows_in.at[0, 0])
-    run = out_ref.shape[1] // 2
+def outer_kernel(head, tail, out_ref, rows_ref):
+    load_rows(rows_ref, 0, head.at[0, 0])
+    load_rows(rows_ref, REACH, tail.at[0, 0])
 
     def one_run(i, carry):
-        for j in range(run):
-            s = i * run + j
-            out_ref[0, s] = cross_tile(rows_ref, s, range(1, run - j))
+        for j in range(REACH):
+            s = i * REACH + j
+            out_ref[0, s] = cross_tile(rows_ref, s, range(1, REACH - j))
         return carry
 
     lax.fori_loop(0, 2, one_run, 0)
 
 
-def edge_kernel(own, after, before, _, plus_ref, minus_ref, rows_ref):
-    sign = pl.program_id(0)
-
-    @pl.when(sign == 0)
-    def _():
-        load_rows(rows_ref, 0, own.at[0, 0])
-        load_rows(rows_ref, REACH, after.at[0])
-
-    @pl.when(sign == 1)
-    def _():
-        load_rows(rows_ref, 0, before.at[0])
-        load_rows(rows_ref, REACH, own.at[0, 0])
-
-    tiles = [cross_tile(rows_ref, j, range(REACH - j, REACH + 1)) for j in range(REACH)]
-
-    @pl.when(sign == 0)
-    def _():
-        for j in range(REACH):
-            plus_ref[0, j] = tiles[j]
-
-    @pl.when(sign == 1)
-    def _():
-        for j in range(REACH):
-            minus_ref[0, j] = tiles[j]
-
-
-def final_kernel(
-    outer, inner, sums_ref, plus_ref, minus_ref, left_ref, right_ref, valid_ref,
-    out_ref, rows_ref,
-):
+def inner_kernel(head, inner, tail, out_ref, rows_ref):
+    load_rows(rows_ref, 0, head.at[0, 0])
+    load_rows(rows_ref, REACH, inner.at[0, 0])
+    load_rows(rows_ref, 3 * REACH, tail.at[0, 0])
+    for s in range(3 * REACH):
+        out_ref[0, s] = cross_tile(rows_ref, s, range(max(1, REACH - s), REACH + 1))
+
+
+def final_kernel(before, head, tail, after, outer_ref, inner_ref, valid_ref, out_ref, rows_ref):
     shape = (REACH, LANES)
     lane = lax.broadcasted_iota(jnp.int32, shape, 1)
     row = lax.broadcasted_iota(jnp.int32, shape, 0)
     mirror = pl.program_id(0) == 1
     order = jnp.where(mirror, (LANES - lane) % LANES, lane)
     slots = out_ref.shape[0]
-    load_rows(rows_ref, 0, outer.at[0, 0, pl.ds(0, REACH)])
-    load_rows(rows_ref, REACH, inner.at[0, 0])
-    load_rows(rows_ref, slots - REACH, outer.at[0, 0, pl.ds(REACH, REACH)])
+    for i, source in enumerate((before, head, tail, after)):
+        load_rows(rows_ref, i * REACH, source.at[0, 0])
     powers = {}
     for s in range(-REACH, slots):
         terms = []
-        if s < 0:
-            terms.append(jnp.where(mirror, minus_ref[0, s + REACH], left_ref[0, s + REACH]))
+        if s < 0 or s >= slots - REACH:
+            j = s % REACH
+            at = j if s < 0 else 2 * REACH + j
+            terms.append(cross_tile(rows_ref, at, range(REACH - j, REACH + 1)))
         if s in OUTER:
-            terms.append(sums_ref[0, OUTER.index(s)])
+            terms.append(outer_ref[0, OUTER.index(s)])
         if 0 <= s < slots - REACH:
-            terms.append(cross_tile(rows_ref, s, range(max(1, REACH - s), REACH + 1)))
-        if s >= slots - REACH:
-            j = s - (slots - REACH)
-            terms.append(jnp.where(mirror, right_ref[0, j], plus_ref[0, j]))
+            terms.append(inner_ref[0, s])
         value = jnp.take_along_axis(sum(terms[1:], terms[0]), order, axis=1)
         powers[s] = jnp.where(valid_ref[s + REACH] > 0.0, value * (1.0 / 64.0), 0.0)
         if s >= 0:
@@ -271,75 +250,53 @@
     )(*operands)
 
 
-def spectra_spec(slots, rows, place=lambda i: 0):
-    return pl.BlockSpec((1, 1, slots, rows, LANES), lambda i, j: (i, j, place(i), 0, 0))
+def spectra_spec(array):
+    return pl.BlockSpec((1, 1) + array.shape[2:], lambda i, j: (i, j, 0, 0, 0))
 
 
 def sums_spec(slots):
     return pl.BlockSpec((1, slots, REACH, LANES), lambda i, j: (i * CHUNKS + j, 0, 0, 0))
 
 
-def plus_spec(rows=REACH):
-    return pl.BlockSpec(
-        (1, REACH, rows, LANES), lambda i, j: (jnp.where(i == 0, j, CHUNKS - 1), 0, 0, 0)
-    )
-
-
-def minus_spec(rows=REACH):
-    return pl.BlockSpec((1, REACH, rows, LANES), lambda i, j: (jnp.where(i == 0, 0, j), 0, 0, 0))
-
-
-def outer_powers(outer):
-    slots, rows = outer.shape[2:4]
-    shape = jax.ShapeDtypeStruct((2 * CHUNKS, slots, REACH, LANES), jnp.float32)
+def outer_powers(head, tail):
+    slots = 2 * REACH
     return cross_call(
         outer_kernel,
         "outer_pairs",
-        [in_hbm(outer)],
-        [spectra_spec(slots, rows)],
+        [in_hbm(head), in_hbm(tail)],
+        [spectra_spec(head)] * 2,
         sums_spec(slots),
-        shape,
+        jax.ShapeDtypeStruct((2 * CHUNKS, slots, REACH, LANES), jnp.float32),
         slots,
         56,
     )
 
 
-def edge_powers(outer, after, before, outer_sums):
-    slots, rows = outer.shape[2:4]
-    last = slots // REACH - 1
-    shape = jax.ShapeDtypeStruct((CHUNKS, REACH, REACH, LANES), jnp.float32)
+def inner_powers(head, inner, tail):
+    slots = 3 * REACH
     return cross_call(
-        edge_kernel,
-        "edge_pairs",
-        [in_hbm(outer), after, before, outer_sums],
-        [
-            spectra_spec(REACH, rows, lambda i: (1 - i) * last),
-            plus_spec(rows),
-            minus_spec(rows),
-            pl.BlockSpec(memory_space=pl.ANY),
-        ],
-        [plus_spec(), minus_spec()],
-        [shape, shape],
-        2 * REACH,
-        36,
-    )
-
-
-def final_powers(outer, inner, outer_sums, plus, minus, left, right, valid):
-    rows = outer.shape[3]
+        inner_kernel,
+        "inner_pairs",
+        [in_hbm(head), in_hbm(inner), in_hbm(tail)],
+        [spectra_spec(array) for array in (head, inner, tail)],
+        sums_spec(slots),
+        jax.ShapeDtypeStruct((2 * CHUNKS, slots, REACH, LANES), jnp.float32),
+        4 * REACH,
+        164,
+    )
+
+
+def final_powers(before, head, tail, after, outer_sums, inner_sums, valid):
     slots = 4 * REACH
+    spectra_specs = [spectra_spec(array) for array in (before, head, tail, after)]
     return cross_call(
         final_kernel,
         "pair_power",
-        [in_hbm(outer), in_hbm(inner), outer_sums, plus, minus, left, right, valid],
-        [
-            spectra_spec(outer.shape[2], rows),
-            spectra_spec(inner.shape[2], rows),
+        [before, in_hbm(head), in_hbm(tail), after, outer_sums, inner_sums, valid],
+        spectra_specs
+        + [
             sums_spec(outer_sums.shape[1]),
-            plus_spec(),
-            minus_spec(),
-            plus_spec(),
-            minus_spec(),
+            sums_spec(inner_sums.shape[1]),
             pl.BlockSpec(valid.shape, lambda i, j: (0, 0, 0)),
         ],
         pl.BlockSpec(
@@ -348,7 +305,7 @@
         ),
         jax.ShapeDtypeStruct((slots, 2 * REACH, 2 * CHUNKS * LANES), jnp.float32),
         slots,
-        164,
+        72,
     )
 
 
@@ -383,15 +340,14 @@
     down = [(i + 1, i) for i in range(n_dev - 1)]
     received_outer = exchange(OUTER, group_ids)
     received_inner = exchange(INNER, table)
-    outer = spectra(received_outer, table, n_tm, n_chan)
-    after = lax.ppermute(outer[0, :, :REACH], AXES, down)
-    before = lax.ppermute(outer[1, :, REACH:], AXES, up)
-    outer_sums = outer_powers(outer)
-    plus, minus = edge_powers(outer, after, before, outer_sums)
-    left = lax.ppermute(plus, AXES, up)
-    right = lax.ppermute(minus, AXES, down)
-    inner = spectra(received_inner, table, n_tm, n_chan)
-    return final_powers(outer, inner, outer_sums, plus, minus, left, right, valid)
+    head = spectra(received_outer, table, n_tm, n_chan, 0, REACH, group_ids)
+    tail = spectra(received_outer, table, n_tm, n_chan, REACH, REACH, group_ids)
+    after = lax.ppermute(head, AXES, down)
+    before = lax.ppermute(tail, AXES, up)
+    outer_sums = outer_powers(head, tail)
+    inner = spectra(received_inner, table, n_tm, n_chan, 0, 2 * REACH, outer_sums)
+    inner_sums = inner_powers(head, inner, tail)
+    return final_powers(before, head, tail, after, outer_sums, inner_sums, valid)
 
 
 def solution(mesh):

time: 176 us -> 178 us (1.011)
  the two profiles are of different devices: /device:TPU:32 before, /device:TPU:46 now
where the time goes in v3:
time: 178 us; the launch traced here: 177 us
  waiting for transfers between devices  66.2 us (37%)
  Pallas kernels  58.8 us (33%)
  starting transfers between devices  26.2 us (15%)
  other arithmetic  17.4 us (10%)
  local copies, waits for them, and re-layouts  7.07 us (4%)
    all_to_all x2, waiting for transfers between devices, exchange(): return lax.all_to_all(send, AXES, 0, 0, tiled=True)  66.2 us
    pallas_call x3, Pallas kernels, cross_call(): pl.pallas_call(kernel, grid=(2, CHUNKS), in_specs=specs, out_specs=out_sp...  23.7 us
    all_to_all x2, starting transfers between devices, exchange(): return lax.all_to_all(send, AXES, 0, 0, tiled=True)  20.7 us
    pallas_call x3, Pallas kernels, spectra(): pl.pallas_call(spectra_kernel, grid=(slots // step,), in_specs=[pl.BlockS...  20.3 us
    convert_element_type x1, other arithmetic, half_table(): return (weights_norm[:, None] * jnp.cos(phase_angle)).astype(jnp.bfloat16)  16.5 us
    pallas_call x2, Pallas kernels, gather(): pl.pallas_call(functools.partial(gather_kernel, slots, n_base // n_dev),...  14.8 us
    unnamed x8, local copies, waits for them, and re-layouts  6.77 us
  transfers between devices with their start and end apart: 4, of which 2 were waited for; matrix products, arithmetic and copies ran while one was open for 10% of the time, Pallas kernels for 24%

profile of v3, /device:TPU:46, one launch (start us, length us, event | category | flops | bytes accessed | tf_op | source)
XLA Modules:
  0.0 176.5 jit_solution(327893730566698314)
XLA Ops:
  0.0 0.0 copy-start
  0.0 3.4 %copy-done = bf16[4,4096,2,128]{3,2,1,0:T(2,128)(2,1)S(1)} copy-done((bf16[4,4096,2,128]{3,2,1,0:T(2,128)(2,1)S(1)}, bf16[4,4096,2,128]{3,2,1,0:T(2,128)(2,1)}, u32[]{:S(2)}) %copy-start) | copy-done | bytes 8388632
  3.4 7.3 %slot_gather.2 = bf16[128,16,4,2,128]{4,3,2,1,0:T(2,128)(2,1)} custom-call(s32[4096]{0:T(1024)} %order_ref.3, bf16[4,4096,2,128]{3,2,1,0:T(2,128)(2,1)S(1)} %copy-done, s32[4096]{0:T(1024)} %_.5), custom_call_target="tpu_custom_call" | custom-call | bytes 8388608 | tf_op jit(solution)/shard_map/slot_gather/pallas_call | solution.py:63
  10.7 10.6 %all-to-all-start = ((bf16[128,128,128]{2,1,0:T(8,128)(2,1)}), bf16[128,128,128]{2,1,0:T(8,128)(2,1)}, u32[]{:S(2)}, u32[]{:S(2)}) async-start(bf16[128,128,128]{2,1,0:T(8,128)(2,1)} %bitcast.20), calls=%async_computation | async-start | bytes 8388608 | tf_op jit(solution)/shard_map/all_to_all | solution.py:337
  21.3 0.7 multiply_reduce_fusion
  22.6 0.1 fusion.23
  22.7 16.5 %fusion.5.table_ref._ = bf16[1024,1024]{1,0:T(8,128)(2,1)} fusion(s32[1024]{0:T(1024)S(1)} %get-tuple-element.13, s32[1024]{0:T(1024)S(1)} %get-tuple-element.14, f32[1024]{0:T(1024)S(1)} %fusion.23), kind=kLoop, calls=%fused_computation.8 | loop fusion | flops 17825792 | bytes 2109440 | tf_op jit(solution)/shard_map/convert_element_type | solution.py:41
  39.2 0.0 copy-start.1
  39.2 3.4 %copy-done.1 = bf16[4,4096,2,128]{3,2,1,0:T(2,128)(2,1)S(1)} copy-done((bf16[4,4096,2,128]{3,2,1,0:T(2,128)(2,1)S(1)}, bf16[4,4096,2,128]{3,2,1,0:T(2,128)(2,1)}, u32[]{:S(2)}) %copy-start.1) | copy-done | bytes 8388632
  42.6 7.5 %slot_gather.3 = bf16[128,16,4,2,128]{4,3,2,1,0:T(2,128)(2,1)} custom-call(s32[4096]{0:T(1024)} %order_ref.3, bf16[4,4096,2,128]{3,2,1,0:T(2,128)(2,1)S(1)} %copy-done.1, bf16[1024,1024]{1,0:T(8,128)(2,1)} %fusion.5.table_ref._), custom_call_target="tpu_custom_call" | custom-call | bytes 8388608 | tf_op jit(solution)/shard_map/slot_gather/pallas_call | solution.py:63
  50.1 19.5 %all-to-all-done = bf16[128,128,128]{2,1,0:T(8,128)(2,1)} async-done(((bf16[128,128,128]{2,1,0:T(8,128)(2,1)}), bf16[128,128,128]{2,1,0:T(8,128)(2,1)}, u32[]{:S(2)}, u32[]{:S(2)}) %all-to-all-start) | async-done | bytes 4194336 | tf_op jit(solution)/shard_map/all_to_all | solution.py:337
  69.6 0.0 copy-start.2
  69.6 10.1 %all-to-all-start.1 = ((bf16[128,128,128]{2,1,0:T(8,128)(2,1)}), bf16[128,128,128]{2,1,0:T(8,128)(2,1)}, u32[]{:S(2)}, u32[]{:S(2)}) async-start(bf16[128,128,128]{2,1,0:T(8,128)(2,1)} %bitcast.21), calls=%async_computation.1 | async-start | bytes 8388608 | tf_op jit(solution)/shard_map/all_to_all | solution.py:337
  79.7 0.0 copy-done.2
  79.7 5.9 %delay_spectra.4.head = bf16[2,4,8,128,128]{4,3,2,1,0:T(8,128)(2,1)} custom-call(bf16[16,8,128,128]{3,2,1,0:T(8,128)(2,1)} %bitcast.1.received_ref, bf16[1024,1024]{1,0:T(8,128)(2,1)} %fusion.5.table_ref._, s32[4096]{0:T(1024)S(1)} %copy-done.2), custom_call_target="tpu_custom_call" | custom-call | flops 2147483648 | bytes 8388608 | tf_op jit(solution)/shard_map/delay_spectra/pallas_call | solution.py:125
  85.6 0.0 copy-start.3
  85.6 6.0 %delay_spectra.3.tail = bf16[2,4,8,128,128]{4,3,2,1,0:T(8,128)(2,1)} custom-call(bf16[16,8,128,128]{3,2,1,0:T(8,128)(2,1)} %bitcast.1.received_ref, bf16[1024,1024]{1,0:T(8,128)(2,1)} %fusion.5.table_ref._, s32[4096]{0:T(1024)S(1)} %copy-done.2), custom_call_target="tpu_custom_call" | custom-call | flops 2147483648 | bytes 8388608 | tf_op jit(solution)/shard_map/delay_spectra/pallas_call | solution.py:125
  91.7 2.0 %collective-permute-start = (bf16[2,4,8,128,128]{4,3,2,1,0:T(8,128)(2,1)}, bf16[2,4,8,128,128]{4,3,2,1,0:T(8,128)(2,1)S(1)}, u32[]{:S(2)}, u32[]{:S(2)}) collective-permute-start(bf16[2,4,8,128,128]{4,3,2,1,0:T(8,128)(2,1)} %delay_spectra.3.tail), channel_id=1, source_target_pairs={{0,1},{1,2},{2,3},{3,4},{4,5},{5,6},{6,7},{7,8},{8,9},{9,10},{10,1... | collective-permute-start | bytes 6291464 | tf_op jit(solution)/shard_map/ppermute | solution.py:346
  93.7 3.5 %collective-permute-start.1 = (bf16[2,4,8,128,128]{4,3,2,1,0:T(8,128)(2,1)}, bf16[2,4,8,128,128]{4,3,2,1,0:T(8,128)(2,1)}, u32[]{:S(2)}, u32[]{:S(2)}) collective-permute-start(bf16[2,4,8,128,128]{4,3,2,1,0:T(8,128)(2,1)} %delay_spectra.4.head), channel_id=1, source_target_pairs={{1,0},{2,1},{3,2},{4,3},{5,4},{6,5},{7,6},{8,7},{9,8},{10,9},{11,1... | collective-permute-start | bytes 6291464 | tf_op jit(solution)/shard_map/ppermute | solution.py:345
  97.2 0.1 pad_dynamic-slice_fusion.1
  97.3 0.1 compare_bitcast_fusion
  97.4 0.0 copy-done.3
  97.4 0.1 and_convert_fusion
  97.5 0.1 copy.5
  97.6 6.2 %outer_pairs.1._.outer_ref = f32[8,16,8,128]{3,2,1,0:T(8,128)S(1)} custom-call(bf16[2,4,8,128,128]{4,3,2,1,0:T(8,128)(2,1)} %delay_spectra.4.head, bf16[2,4,8,128,128]{4,3,2,1,0:T(8,128)(2,1)} %delay_spectra.3.tail), custom_call_target="tpu_custom_call" | custom-call | flops 14680064 | bytes 4194304 | tf_op jit(solution)/shard_map/outer_pairs/pallas_call | solution.py:236
  103.8 46.7 %all-to-all-done.1 = bf16[128,128,128]{2,1,0:T(8,128)(2,1)} async-done(((bf16[128,128,128]{2,1,0:T(8,128)(2,1)}), bf16[128,128,128]{2,1,0:T(8,128)(2,1)}, u32[]{:S(2)}, u32[]{:S(2)}) %all-to-all-start.1) | async-done | bytes 4194336 | tf_op jit(solution)/shard_map/all_to_all | solution.py:337
  150.4 8.4 %delay_spectra.5.inner = bf16[2,4,16,128,128]{4,3,2,1,0:T(8,128)(2,1)} custom-call(bf16[16,8,128,128]{3,2,1,0:T(8,128)(2,1)} %bitcast.3.received_ref, bf16[1024,1024]{1,0:T(8,128)(2,1)} %fusion.5.table_ref._, f32[8,16,8,128]{3,2,1,0:T(8,128)S(1)} %outer_pairs.1._.outer_ref), custom_call_target="tpu_custom_call" | custom-call | flops 4294967296 | bytes 16777216 | tf_op jit(solution)/shard_map/delay_spectra/pallas_call | solution.py:125
  158.8 9.2 %inner_pairs.1.inner_ref = f32[8,24,8,128]{3,2,1,0:T(8,128)S(1)} custom-call(bf16[2,4,8,128,128]{4,3,2,1,0:T(8,128)(2,1)} %delay_spectra.4.head, bf16[2,4,16,128,128]{4,3,2,1,0:T(8,128)(2,1)} %delay_spectra.5.inner, bf16[2,4,8,128,128]{4,3,2,1,0:T(8,128)(2,1)} %delay_spectra.3.tail), custom_call_target="tpu_custom_call" | custom-call | flops 42991616 | bytes 8388608 | tf_op jit(solution)/shard_map/inner_pairs/pallas_call | solution.py:236
  168.0 0.0 collective-permute-done.before
  168.0 0.0 collective-permute-done.1.after
  168.1 0.1 broadcast_in_dim.22.valid_ref
  168.2 8.3 %pair_power.1 = f32[32,16,1024]{2,1,0:T(8,128)} custom-call(bf16[2,4,8,128,128]{4,3,2,1,0:T(8,128)(2,1)S(1)} %collective-permute-done.before, bf16[2,4,8,128,128]{4,3,2,1,0:T(8,128)(2,1)} %delay_spectra.4.head, bf16[2,4,8,128,128]{4,3,2,1,0:T(8,128)(2,1)} %delay_spectra.3.tail, bf16[2,4,8,128,128]{4,3,2,1,0:T(8,128)(2,1)} %collective-permute-done.1.after, ...), custom_call_target="tpu_custom_call" | custom-call | flops 18874368 | bytes 8388608 | tf_op jit(solution)/shard_map/pair_power/pallas_call | solution.py:236
  (2 shorter events, 0.0 us)
Async XLA Ops:
  0.0 3.4 %copy-start = (bf16[4,4096,2,128]{3,2,1,0:T(2,128)(2,1)S(1)}, bf16[4,4096,2,128]{3,2,1,0:T(2,128)(2,1)}, u32[]{:S(2)}) copy-start(bf16[4,4096,2,128]{3,2,1,0:T(2,128)(2,1)} %vis_ref.3) | copy-start | bytes 25165828
  10.7 58.9 %all-to-all-start = ((bf16[128,128,128]{2,1,0:T(8,128)(2,1)}), bf16[128,128,128]{2,1,0:T(8,128)(2,1)}, u32[]{:S(2)}, u32[]{:S(2)}) async-start(bf16[128,128,128]{2,1,0:T(8,128)(2,1)} %bitcast.20), calls=%async_computation | async-start | bytes 8388608 | tf_op jit(solution)/shard_map/all_to_all | solution.py:337
  39.2 3.4 %copy-start.1 = (bf16[4,4096,2,128]{3,2,1,0:T(2,128)(2,1)S(1)}, bf16[4,4096,2,128]{3,2,1,0:T(2,128)(2,1)}, u32[]{:S(2)}) copy-start(bf16[4,4096,2,128]{3,2,1,0:T(2,128)(2,1)} %vis_ref.3) | copy-start | bytes 25165828
  69.6 10.1 %copy-start.2 = (s32[4096]{0:T(1024)S(1)}, s32[4096]{0:T(1024)}, u32[]{:S(2)}) copy-start(s32[4096]{0:T(1024)} %_.5) | copy-start | bytes 49156
  69.6 80.8 %all-to-all-start.1 = ((bf16[128,128,128]{2,1,0:T(8,128)(2,1)}), bf16[128,128,128]{2,1,0:T(8,128)(2,1)}, u32[]{:S(2)}, u32[]{:S(2)}) async-start(bf16[128,128,128]{2,1,0:T(8,128)(2,1)} %bitcast.21), calls=%async_computation.1 | async-start | bytes 8388608 | tf_op jit(solution)/shard_map/all_to_all | solution.py:337
  85.6 11.8 %copy-start.3 = (s32[4096,8]{0,1:T(8,128)S(1)}, s32[4096,8]{0,1:T(8,128)}, u32[]{:S(2)}) copy-start(s32[4096,8]{0,1:T(8,128)} %param.7) | copy-start | bytes 393220
  91.7 76.4 %collective-permute-start = (bf16[2,4,8,128,128]{4,3,2,1,0:T(8,128)(2,1)}, bf16[2,4,8,128,128]{4,3,2,1,0:T(8,128)(2,1)S(1)}, u32[]{:S(2)}, u32[]{:S(2)}) collective-permute-start(bf16[2,4,8,128,128]{4,3,2,1,0:T(8,128)(2,1)} %delay_spectra.3.tail), channel_id=1, source_target_pairs={{0,1},{1,2},{2,3},{3,4},{4,5},{5,6},{6,7},{7,8},{8,9},{9,10},{10,1... | collective-permute-start | bytes 6291464 | tf_op jit(solution)/shard_map/ppermute | solution.py:346
  93.7 74.3 %collective-permute-start.1 = (bf16[2,4,8,128,128]{4,3,2,1,0:T(8,128)(2,1)}, bf16[2,4,8,128,128]{4,3,2,1,0:T(8,128)(2,1)}, u32[]{:S(2)}, u32[]{:S(2)}) collective-permute-start(bf16[2,4,8,128,128]{4,3,2,1,0:T(8,128)(2,1)} %delay_spectra.4.head), channel_id=1, source_target_pairs={{1,0},{2,1},{3,2},{4,3},{5,4},{6,5},{7,6},{8,7},{9,8},{10,9},{11,1... | collective-permute-start | bytes 6291464 | tf_op jit(solution)/shard_map/ppermute | solution.py:345

commit v4 on v3

--- a/solution.py
+++ b/solution.py
@@ -190,34 +190,38 @@
     lax.fori_loop(0, 2, one_run, 0)
 
 
-def inner_kernel(head, inner, tail, out_ref, rows_ref):
-    load_rows(rows_ref, 0, head.at[0, 0])
-    load_rows(rows_ref, REACH, inner.at[0, 0])
-    load_rows(rows_ref, 3 * REACH, tail.at[0, 0])
-    for s in range(3 * REACH):
-        out_ref[0, s] = cross_tile(rows_ref, s, range(max(1, REACH - s), REACH + 1))
-
-
-def final_kernel(before, head, tail, after, outer_ref, inner_ref, valid_ref, out_ref, rows_ref):
+def edge_kernel(tail, after, before, head, _, next_ref, prev_ref, rows_ref):
+    for left, right, out_ref in ((tail, after, next_ref), (before, head, prev_ref)):
+        load_rows(rows_ref, 0, left.at[0, 0])
+        load_rows(rows_ref, REACH, right.at[0, 0])
+        for j in range(REACH):
+            out_ref[0, j] = cross_tile(rows_ref, j, range(REACH - j, REACH + 1))
+
+
+def final_kernel(
+    head, inner, tail, outer_ref, next_a, next_b, prev_a, prev_b, valid_ref, out_ref, rows_ref
+):
     shape = (REACH, LANES)
     lane = lax.broadcasted_iota(jnp.int32, shape, 1)
     row = lax.broadcasted_iota(jnp.int32, shape, 0)
     mirror = pl.program_id(0) == 1
     order = jnp.where(mirror, (LANES - lane) % LANES, lane)
     slots = out_ref.shape[0]
-    for i, source in enumerate((before, head, tail, after)):
-        load_rows(rows_ref, i * REACH, source.at[0, 0])
+    load_rows(rows_ref, 0, head.at[0, 0])
+    load_rows(rows_ref, REACH, inner.at[0, 0])
+    load_rows(rows_ref, 3 * REACH, tail.at[0, 0])
     powers = {}
     for s in range(-REACH, slots):
         terms = []
-        if s < 0 or s >= slots - REACH:
-            j = s % REACH
-            at = j if s < 0 else 2 * REACH + j
-            terms.append(cross_tile(rows_ref, at, range(REACH - j, REACH + 1)))
+        if s < 0:
+            terms += [prev_a[0, s + REACH], prev_b[0, s + REACH]]
         if s in OUTER:
             terms.append(outer_ref[0, OUTER.index(s)])
         if 0 <= s < slots - REACH:
-            terms.append(inner_ref[0, s])
+            terms.append(cross_tile(rows_ref, s, range(max(1, REACH - s), REACH + 1)))
+        if s >= slots - REACH:
+            j = s - (slots - REACH)
+            terms += [next_a[0, j], next_b[0, j]]
         value = jnp.take_along_axis(sum(terms[1:], terms[0]), order, axis=1)
         powers[s] = jnp.where(valid_ref[s + REACH] > 0.0, value * (1.0 / 64.0), 0.0)
         if s >= 0:
@@ -231,8 +235,7 @@
 CHUNKS = 4
 
 
-def cross_call(kernel, name, operands, specs, out_specs, out_shape, held, pairs):
-    rows = 128
+def cross_call(kernel, name, operands, specs, out_specs, out_shape, held, pairs, rows=128):
     return pl.pallas_call(
         kernel,
         grid=(2, CHUNKS),
@@ -272,41 +275,72 @@
     )
 
 
-def inner_powers(head, inner, tail):
-    slots = 3 * REACH
+def edge_powers(tail, after, before, head, earlier):
+    rows = after.shape[3]
+    shape = jax.ShapeDtypeStruct((2 * CHUNKS, REACH, REACH, LANES), jnp.float32)
+
+    def half(which):
+        return pl.BlockSpec((1, 1, REACH, rows, LANES), lambda i, j: (i, j, 0, which, 0))
+
     return cross_call(
-        inner_kernel,
-        "inner_pairs",
-        [in_hbm(head), in_hbm(inner), in_hbm(tail)],
-        [spectra_spec(array) for array in (head, inner, tail)],
-        sums_spec(slots),
-        jax.ShapeDtypeStruct((2 * CHUNKS, slots, REACH, LANES), jnp.float32),
-        4 * REACH,
-        164,
-    )
-
-
-def final_powers(before, head, tail, after, outer_sums, inner_sums, valid):
+        edge_kernel,
+        "edge_pairs",
+        [in_hbm(tail), in_hbm(after), in_hbm(before), in_hbm(head), earlier],
+        [half(0), half(0), half(0), half(1), pl.BlockSpec(memory_space=pl.ANY)],
+        [sums_spec(REACH)] * 2,
+        [shape, shape],
+        2 * REACH,
+        36 * 100000,
+        rows,
+    )
+
+
+def final_powers(head, inner, tail, outer_sums, following, preceding, valid):
     slots = 4 * REACH
-    spectra_specs = [spectra_spec(array) for array in (before, head, tail, after)]
+    edges = [*following, *preceding]
     return cross_call(
         final_kernel,
         "pair_power",
-        [before, in_hbm(head), in_hbm(tail), after, outer_sums, inner_sums, valid],
-        spectra_specs
-        + [
-            sums_spec(outer_sums.shape[1]),
-            sums_spec(inner_sums.shape[1]),
-            pl.BlockSpec(valid.shape, lambda i, j: (0, 0, 0)),
-        ],
+        [in_hbm(head), in_hbm(inner), in_hbm(tail), outer_sums, *edges, valid],
+        [spectra_spec(array) for array in (head, inner, tail)]
+        + [sums_spec(outer_sums.shape[1])]
+        + [sums_spec(REACH)] * len(edges)
+        + [pl.BlockSpec(valid.shape, lambda i, j: (0, 0, 0))],
         pl.BlockSpec(
             (slots, 2 * REACH, LANES),
             lambda i, j: (0, 0, jnp.where(i == 0, j, 2 * CHUNKS - 1 - j)),
         ),
         jax.ShapeDtypeStruct((slots, 2 * REACH, 2 * CHUNKS * LANES), jnp.float32),
         slots,
-        72,
-    )
+        164,
+    )
+
+
+def edge_rows_kernel(received, _, head, tail, __, sems):
+    near, edge = head.shape[:2]
+    copies = [
+        pltpu.make_async_copy(received.at[pl.ds(0, near), pl.ds(0, edge)], head, sems.at[0]),
+        pltpu.make_async_copy(received.at[pl.ds(near, near), pl.ds(edge, edge)], tail, sems.at[1]),
+    ]
+    for copy in copies:
+        copy.start()
+    for copy in copies:
+        copy.wait()
+
+
+def edge_rows(received, send):
+    sources, rows, lanes = received.shape
+    part = pltpu.HBM((sources // 2, rows // 2, lanes), received.dtype)
+    anywhere = pl.BlockSpec(memory_space=pl.ANY)
+    return pl.pallas_call(
+        edge_rows_kernel,
+        in_specs=[anywhere] * 2,
+        out_specs=[anywhere] * 3,
+        out_shape=[part, part, pltpu.HBM(send.shape, send.dtype)],
+        scratch_shapes=[pltpu.SemaphoreType.DMA((2,))],
+        input_output_aliases={1: 2},
+        name="edge_rows",
+    )(in_hbm(received), in_hbm(send))
 
 
 def body(visibilities, owner_order, group_ids, partner_flags):
@@ -331,23 +365,33 @@
         (same & (flags == 1)).astype(jnp.float32)[:, :, None], (per + REACH, REACH, LANES)
     )
 
-    def exchange(slots, earlier):
+    def rows_for_owners(slots, earlier):
         send = gather(visibilities, owner_order, slots, n_dev, earlier)
-        send = send.reshape(n_dev, 2 * count * len(slots), width)
+        return send.reshape(n_dev, 2 * count * len(slots), width)
+
+    def exchange(send):
         return lax.all_to_all(send, AXES, 0, 0, tiled=True)
 
     up = [(i, i + 1) for i in range(n_dev - 1)]
     down = [(i + 1, i) for i in range(n_dev - 1)]
-    received_outer = exchange(OUTER, group_ids)
-    received_inner = exchange(INNER, table)
+    received_outer = exchange(rows_for_owners(OUTER, group_ids))
+    send_inner = rows_for_owners(INNER, table)
+    head_rows, tail_rows, send_inner = edge_rows(received_outer, send_inner)
+    after_rows = lax.ppermute(head_rows, AXES, down)
+    before_rows = lax.ppermute(tail_rows, AXES, up)
+    received_inner = exchange(send_inner)
     head = spectra(received_outer, table, n_tm, n_chan, 0, REACH, group_ids)
     tail = spectra(received_outer, table, n_tm, n_chan, REACH, REACH, group_ids)
-    after = lax.ppermute(head, AXES, down)
-    before = lax.ppermute(tail, AXES, up)
     outer_sums = outer_powers(head, tail)
-    inner = spectra(received_inner, table, n_tm, n_chan, 0, 2 * REACH, outer_sums)
-    inner_sums = inner_powers(head, inner, tail)
-    return final_powers(before, head, tail, after, outer_sums, inner_sums, valid)
+    after = spectra(after_rows, table, n_tm // 2, n_chan, 0, REACH, outer_sums)
+    before = spectra(before_rows, table, n_tm // 2, n_chan, 0, REACH, outer_sums)
+    next_sums, prev_sums = edge_powers(tail, after, before, head, outer_sums)
+    prev_other = lax.ppermute(next_sums, AXES, up)
+    next_other = lax.ppermute(prev_sums, AXES, down)
+    inner = spectra(received_inner, table, n_tm, n_chan, 0, 2 * REACH, next_sums)
+    return final_powers(
+        head, inner, tail, outer_sums, (next_sums, next_other), (prev_sums, prev_other), valid
+    )
 
 
 def solution(mesh):

time: 178 us -> 234 us (1.31)
  the two profiles are of different devices: /device:TPU:46 before, /device:TPU:32 now
where the time goes in v4:
time: 234 us; the launch traced here: 230 us
  Pallas kernels  131 us (56%)
  waiting for transfers between devices  38.9 us (17%)
  starting transfers between devices  32.9 us (14%)
  other arithmetic  17.4 us (7%)
  local copies, waits for them, and re-layouts  9.67 us (4%)
    pallas_call x1, Pallas kernels, edge_rows(): pl.pallas_call(edge_rows_kernel, in_specs=[anywhere] * 2, out_specs=[anyw...  64.6 us
    all_to_all x2, waiting for transfers between devices, exchange(): return lax.all_to_all(send, AXES, 0, 0, tiled=True)  38.6 us
    pallas_call x5, Pallas kernels, spectra(): pl.pallas_call(spectra_kernel, grid=(slots // step,), in_specs=[pl.BlockS...  28.8 us
    pallas_call x3, Pallas kernels, cross_call(): pl.pallas_call(kernel, grid=(2, CHUNKS), in_specs=specs, out_specs=out_sp...  22.6 us
    all_to_all x2, starting transfers between devices, exchange(): return lax.all_to_all(send, AXES, 0, 0, tiled=True)  18.9 us
    convert_element_type x1, other arithmetic, half_table(): return (weights_norm[:, None] * jnp.cos(phase_angle)).astype(jnp.bfloat16)  16.5 us
    pallas_call x2, Pallas kernels, gather(): pl.pallas_call(functools.partial(gather_kernel, slots, n_base // n_dev),...  14.7 us
    unnamed x14, local copies, waits for them, and re-layouts  8.77 us
  transfers between devices with their start and end apart: 6, of which 3 were waited for; matrix products, arithmetic and copies ran while one was open for 8% of the time, Pallas kernels for 21%

profile of v4, /device:TPU:32, one launch (start us, length us, event | category | flops | bytes accessed | tf_op | source)
XLA Modules:
  0.0 230.4 jit_solution(4305278618791429331)
XLA Ops:
  0.0 0.0 copy-start
  0.0 3.4 %copy-done = bf16[4,4096,2,128]{3,2,1,0:T(2,128)(2,1)S(1)} copy-done((bf16[4,4096,2,128]{3,2,1,0:T(2,128)(2,1)S(1)}, bf16[4,4096,2,128]{3,2,1,0:T(2,128)(2,1)}, u32[]{:S(2)}) %copy-start) | copy-done | bytes 8388632
  3.4 7.3 %slot_gather.2 = bf16[128,16,4,2,128]{4,3,2,1,0:T(2,128)(2,1)} custom-call(s32[4096]{0:T(1024)} %order_ref.3, bf16[4,4096,2,128]{3,2,1,0:T(2,128)(2,1)S(1)} %copy-done, s32[4096]{0:T(1024)} %_.5), custom_call_target="tpu_custom_call" | custom-call | bytes 8388608 | tf_op jit(solution)/shard_map/slot_gather/pallas_call | solution.py:63
  10.7 10.7 %all-to-all-start = ((bf16[128,128,128]{2,1,0:T(8,128)(2,1)}), bf16[128,128,128]{2,1,0:T(8,128)(2,1)}, u32[]{:S(2)}, u32[]{:S(2)}) async-start(bf16[128,128,128]{2,1,0:T(8,128)(2,1)} %bitcast.23), calls=%async_computation | async-start | bytes 8388608 | tf_op jit(solution)/shard_map/all_to_all | solution.py:373
  21.4 0.7 multiply_reduce_fusion
  22.8 0.1 fusion.23
  22.8 16.5 %fusion.5.table_ref._ = bf16[1024,1024]{1,0:T(8,128)(2,1)} fusion(s32[1024]{0:T(1024)S(1)} %get-tuple-element.23, s32[1024]{0:T(1024)S(1)} %get-tuple-element.24, f32[1024]{0:T(1024)S(1)} %fusion.23), kind=kLoop, calls=%fused_computation.8 | loop fusion | flops 17825792 | bytes 2109440 | tf_op jit(solution)/shard_map/convert_element_type | solution.py:41
  39.4 0.0 copy-start.1
  39.4 3.4 %copy-done.1 = bf16[4,4096,2,128]{3,2,1,0:T(2,128)(2,1)S(1)} copy-done((bf16[4,4096,2,128]{3,2,1,0:T(2,128)(2,1)S(1)}, bf16[4,4096,2,128]{3,2,1,0:T(2,128)(2,1)}, u32[]{:S(2)}) %copy-start.1) | copy-done | bytes 8388632
  42.7 7.4 %slot_gather.3 = bf16[128,16,4,2,128]{4,3,2,1,0:T(2,128)(2,1)} custom-call(s32[4096]{0:T(1024)} %order_ref.3, bf16[4,4096,2,128]{3,2,1,0:T(2,128)(2,1)S(1)} %copy-done.1, bf16[1024,1024]{1,0:T(8,128)(2,1)} %fusion.5.table_ref._), custom_call_target="tpu_custom_call" | custom-call | bytes 8388608 | tf_op jit(solution)/shard_map/slot_gather/pallas_call | solution.py:63
  50.1 23.0 %all-to-all-done.received = bf16[128,128,128]{2,1,0:T(8,128)(2,1)} async-done(((bf16[128,128,128]{2,1,0:T(8,128)(2,1)}), bf16[128,128,128]{2,1,0:T(8,128)(2,1)}, u32[]{:S(2)}, u32[]{:S(2)}) %all-to-all-start) | async-done | bytes 4194336 | tf_op jit(solution)/shard_map/all_to_all | solution.py:373
  73.1 0.0 copy-start.2
  73.1 0.0 copy-start.5
  73.1 64.6 %edge_rows.1 = (bf16[64,64,128]{2,1,0:T(8,128)(2,1)}, bf16[64,64,128]{2,1,0:T(8,128)(2,1)}, bf16[128,128,128]{2,1,0:T(8,128)(2,1)}) custom-call(bf16[128,128,128]{2,1,0:T(8,128)(2,1)} %all-to-all-done.received, bf16[128,128,128]{2,1,0:T(8,128)(2,1)} %bitcast.22), custom_call_target="tpu_custom_call", output_to_operand_aliasing={{2}: (1, {})} | custom-call | tf_op jit(solution)/shard_map/edge_rows/pallas_call | solution.py:335
  137.8 3.7 %collective-permute-start = (bf16[64,64,128]{2,1,0:T(8,128)(2,1)}, bf16[64,64,128]{2,1,0:T(8,128)(2,1)S(1)}, u32[]{:S(2)}, u32[]{:S(2)}) collective-permute-start(bf16[64,64,128]{2,1,0:T(8,128)(2,1)} %get-tuple-element.11), channel_id=1, source_target_pairs={{1,0},{2,1},{3,2},{4,3},{5,4},{6,5},{7,6},{8,7},{9,8},{10,9},{11,1... | collective-permute-start | bytes 3145736 | tf_op jit(solution)/shard_map/ppermute | solution.py:380
  141.5 1.9 collective-permute-start.1
  143.5 0.0 copy-done.2
  143.5 0.1 pad_dynamic-slice_fusion.1
  143.5 0.1 compare_bitcast_fusion
  143.7 0.0 copy-done.5
  143.7 0.1 and_convert_fusion
  143.8 0.7 copy.6
  144.4 8.2 %all-to-all-start.1 = ((bf16[128,128,128]{2,1,0:T(8,128)(2,1)}), bf16[128,128,128]{2,1,0:T(8,128)(2,1)}, u32[]{:S(2)}, u32[]{:S(2)}) async-start(bf16[128,128,128]{2,1,0:T(8,128)(2,1)} %get-tuple-element.10), calls=%async_computation.1 | async-start | bytes 8388608 | tf_op jit(solution)/shard_map/all_to_all | solution.py:373
  152.7 6.0 %delay_spectra.5.head = bf16[2,4,8,128,128]{4,3,2,1,0:T(8,128)(2,1)} custom-call(bf16[16,8,128,128]{3,2,1,0:T(8,128)(2,1)} %bitcast.1.received_ref, bf16[1024,1024]{1,0:T(8,128)(2,1)} %fusion.5.table_ref._, s32[4096]{0:T(1024)S(1)} %copy-done.2), custom_call_target="tpu_custom_call" | custom-call | flops 2147483648 | bytes 8388608 | tf_op jit(solution)/shard_map/delay_spectra/pallas_call | solution.py:125
  158.7 5.9 %delay_spectra.6.tail = bf16[2,4,8,128,128]{4,3,2,1,0:T(8,128)(2,1)} custom-call(bf16[16,8,128,128]{3,2,1,0:T(8,128)(2,1)} %bitcast.1.received_ref, bf16[1024,1024]{1,0:T(8,128)(2,1)} %fusion.5.table_ref._, s32[4096]{0:T(1024)S(1)} %copy-done.2), custom_call_target="tpu_custom_call" | custom-call | flops 2147483648 | bytes 8388608 | tf_op jit(solution)/shard_map/delay_spectra/pallas_call | solution.py:125
  164.6 6.2 %outer_pairs.1._.outer_ref = f32[8,16,8,128]{3,2,1,0:T(8,128)S(1)} custom-call(bf16[2,4,8,128,128]{4,3,2,1,0:T(8,128)(2,1)} %delay_spectra.5.head, bf16[2,4,8,128,128]{4,3,2,1,0:T(8,128)(2,1)} %delay_spectra.6.tail), custom_call_target="tpu_custom_call" | custom-call | flops 14680064 | bytes 4194304 | tf_op jit(solution)/shard_map/outer_pairs/pallas_call | solution.py:239
  170.8 0.0 collective-permute-done
  170.8 0.0 copy-start.3
  170.8 1.0 copy-done.3
  171.8 4.2 %delay_spectra.7.after = bf16[2,4,8,64,128]{4,3,2,1,0:T(8,128)(2,1)} custom-call(bf16[8,8,64,128]{3,2,1,0:T(8,128)(2,1)} %bitcast.24, bf16[1024,1024]{1,0:T(8,128)(2,1)} %fusion.5.table_ref._, f32[8,16,8,128]{3,2,1,0:T(8,128)S(1)} %outer_pairs.1._.outer_ref), custom_call_target="tpu_custom_call" | custom-call | flops 1073741824 | bytes 4194304 | tf_op jit(solution)/shard_map/delay_spectra/pallas_call | solution.py:125
  176.0 0.2 collective-permute-done.1
  176.2 0.0 copy-start.4
  176.2 1.0 copy-done.4
  177.2 4.2 %delay_spectra.8.before = bf16[2,4,8,64,128]{4,3,2,1,0:T(8,128)(2,1)} custom-call(bf16[8,8,64,128]{3,2,1,0:T(8,128)(2,1)} %bitcast.25, bf16[1024,1024]{1,0:T(8,128)(2,1)} %fusion.5.table_ref._, f32[8,16,8,128]{3,2,1,0:T(8,128)S(1)} %outer_pairs.1._.outer_ref), custom_call_target="tpu_custom_call" | custom-call | flops 1073741824 | bytes 4194304 | tf_op jit(solution)/shard_map/delay_spectra/pallas_call | solution.py:125
  181.4 5.6 %edge_pairs.1 = (f32[8,8,8,128]{3,2,1,0:T(8,128)S(1)}, f32[8,8,8,128]{3,2,1,0:T(8,128)S(1)}) custom-call(bf16[2,4,8,128,128]{4,3,2,1,0:T(8,128)(2,1)} %delay_spectra.6.tail, bf16[2,4,8,64,128]{4,3,2,1,0:T(8,128)(2,1)} %delay_spectra.7.after, bf16[2,4,8,64,128]{4,3,2,1,0:T(8,128)(2,1)} %delay_spectra.8.before, ...), custom_call_target="tpu_custom_call" | custom-call | flops 471859200000 | bytes 2097152 | tf_op jit(solution)/shard_map/edge_pairs/pallas_call | solution.py:239
  187.1 6.2 %collective-permute-start.2 = (f32[8,8,8,128]{3,2,1,0:T(8,128)S(1)}, f32[8,8,8,128]{3,2,1,0:T(8,128)S(1)}, u32[]{:S(2)}, u32[]{:S(2)}) collective-permute-start(f32[8,8,8,128]{3,2,1,0:T(8,128)S(1)} %get-tuple-element.14.prev_a), channel_id=1, source_target_pairs={{1,0},{2,1},{3,2},{4,3},{5,4},{6,5},{7,6},{8,7},{9,8},{10,9},{11,1... | collective-permute-start | bytes 786440 | tf_op jit(solution)/shard_map/ppermute | solution.py:390
  193.3 2.1 collective-permute-start.3
  195.4 15.7 %all-to-all-done.1 = bf16[128,128,128]{2,1,0:T(8,128)(2,1)} async-done(((bf16[128,128,128]{2,1,0:T(8,128)(2,1)}), bf16[128,128,128]{2,1,0:T(8,128)(2,1)}, u32[]{:S(2)}, u32[]{:S(2)}) %all-to-all-start.1) | async-done | bytes 4194336 | tf_op jit(solution)/shard_map/all_to_all | solution.py:373
  211.1 0.0 copy-start.6
  211.1 8.4 %delay_spectra.9.inner = bf16[2,4,16,128,128]{4,3,2,1,0:T(8,128)(2,1)} custom-call(bf16[16,8,128,128]{3,2,1,0:T(8,128)(2,1)} %bitcast.3.received_ref, bf16[1024,1024]{1,0:T(8,128)(2,1)} %fusion.5.table_ref._, f32[8,8,8,128]{3,2,1,0:T(8,128)S(1)} %get-tuple-element.13._.next_a), custom_call_target="tpu_custom_call" | custom-call | flops 4294967296 | bytes 16777216 | tf_op jit(solution)/shard_map/delay_spectra/pallas_call | solution.py:125
  219.5 0.0 collective-permute-done.2.next_b
  219.5 0.0 collective-permute-done.3.prev_b
  219.5 0.0 copy-done.6
  219.5 0.1 broadcast_in_dim.22.valid_ref
  219.6 10.8 %pair_power.1 = f32[32,16,1024]{2,1,0:T(8,128)} custom-call(bf16[2,4,8,128,128]{4,3,2,1,0:T(8,128)(2,1)} %delay_spectra.5.head, bf16[2,4,16,128,128]{4,3,2,1,0:T(8,128)(2,1)} %delay_spectra.9.inner, bf16[2,4,8,128,128]{4,3,2,1,0:T(8,128)(2,1)} %delay_spectra.6.tail, f32[8,16,8,128]{3,2,1,0:T(8,128)S(1)} %outer_pairs.1._.outer_ref, ...), custom_call_target="tpu_custom_call" | custom-call | flops 42991616 | bytes 8388608 | tf_op jit(solution)/shard_map/pair_power/pallas_call | solution.py:239
  (2 shorter events, 0.0 us)
Async XLA Ops:
  0.0 3.4 %copy-start = (bf16[4,4096,2,128]{3,2,1,0:T(2,128)(2,1)S(1)}, bf16[4,4096,2,128]{3,2,1,0:T(2,128)(2,1)}, u32[]{:S(2)}) copy-start(bf16[4,4096,2,128]{3,2,1,0:T(2,128)(2,1)} %vis_ref.3) | copy-start | bytes 25165828
  10.7 62.4 %all-to-all-start = ((bf16[128,128,128]{2,1,0:T(8,128)(2,1)}), bf16[128,128,128]{2,1,0:T(8,128)(2,1)}, u32[]{:S(2)}, u32[]{:S(2)}) async-start(bf16[128,128,128]{2,1,0:T(8,128)(2,1)} %bitcast.23), calls=%async_computation | async-start | bytes 8388608 | tf_op jit(solution)/shard_map/all_to_all | solution.py:373
  39.4 3.4 %copy-start.1 = (bf16[4,4096,2,128]{3,2,1,0:T(2,128)(2,1)S(1)}, bf16[4,4096,2,128]{3,2,1,0:T(2,128)(2,1)}, u32[]{:S(2)}) copy-start(bf16[4,4096,2,128]{3,2,1,0:T(2,128)(2,1)} %vis_ref.3) | copy-start | bytes 25165828
  73.1 70.3 %copy-start.2 = (s32[4096]{0:T(1024)S(1)}, s32[4096]{0:T(1024)}, u32[]{:S(2)}) copy-start(s32[4096]{0:T(1024)} %_.5) | copy-start | bytes 49156
  73.1 70.5 %copy-start.5 = (s32[4096,8]{0,1:T(8,128)S(1)}, s32[4096,8]{0,1:T(8,128)}, u32[]{:S(2)}) copy-start(s32[4096,8]{0,1:T(8,128)} %param.7) | copy-start | bytes 393220
  137.8 33.0 %collective-permute-start = (bf16[64,64,128]{2,1,0:T(8,128)(2,1)}, bf16[64,64,128]{2,1,0:T(8,128)(2,1)S(1)}, u32[]{:S(2)}, u32[]{:S(2)}) collective-permute-start(bf16[64,64,128]{2,1,0:T(8,128)(2,1)} %get-tuple-element.11), channel_id=1, source_target_pairs={{1,0},{2,1},{3,2},{4,3},{5,4},{6,5},{7,6},{8,7},{9,8},{10,9},{11,1... | collective-permute-start | bytes 3145736 | tf_op jit(solution)/shard_map/ppermute | solution.py:380
  141.5 34.7 %collective-permute-start.1 = (bf16[64,64,128]{2,1,0:T(8,128)(2,1)}, bf16[64,64,128]{2,1,0:T(8,128)(2,1)S(1)}, u32[]{:S(2)}, u32[]{:S(2)}) collective-permute-start(bf16[64,64,128]{2,1,0:T(8,128)(2,1)} %get-tuple-element.12), channel_id=1, source_target_pairs={{0,1},{1,2},{2,3},{3,4},{4,5},{5,6},{6,7},{7,8},{8,9},{9,10},{10,1... | collective-permute-start | bytes 3145736 | tf_op jit(solution)/shard_map/ppermute | solution.py:381
  144.4 66.6 %all-to-all-start.1 = ((bf16[128,128,128]{2,1,0:T(8,128)(2,1)}), bf16[128,128,128]{2,1,0:T(8,128)(2,1)}, u32[]{:S(2)}, u32[]{:S(2)}) async-start(bf16[128,128,128]{2,1,0:T(8,128)(2,1)} %get-tuple-element.10), calls=%async_computation.1 | async-start | bytes 8388608 | tf_op jit(solution)/shard_map/all_to_all | solution.py:373
  170.8 1.0 copy-start.3
  176.2 1.0 copy-start.4
  187.1 32.4 %collective-permute-start.2 = (f32[8,8,8,128]{3,2,1,0:T(8,128)S(1)}, f32[8,8,8,128]{3,2,1,0:T(8,128)S(1)}, u32[]{:S(2)}, u32[]{:S(2)}) collective-permute-start(f32[8,8,8,128]{3,2,1,0:T(8,128)S(1)} %get-tuple-element.14.prev_a), channel_id=1, source_target_pairs={{1,0},{2,1},{3,2},{4,3},{5,4},{6,5},{7,6},{8,7},{9,8},{10,9},{11,1... | collective-permute-start | bytes 786440 | tf_op jit(solution)/shard_map/ppermute | solution.py:390
  193.3 26.2 %collective-permute-start.3 = (f32[8,8,8,128]{3,2,1,0:T(8,128)S(1)}, f32[8,8,8,128]{3,2,1,0:T(8,128)S(1)}, u32[]{:S(2)}, u32[]{:S(2)}) collective-permute-start(f32[8,8,8,128]{3,2,1,0:T(8,128)S(1)} %get-tuple-element.13._.next_a), channel_id=1, source_target_pairs={{0,1},{1,2},{2,3},{3,4},{4,5},{5,6},{6,7},{7,8},{8,9},{9,10},{10,1... | collective-permute-start | bytes 786440 | tf_op jit(solution)/shard_map/ppermute | solution.py:389
  211.1 8.4 %copy-start.6 = (f32[40,8]{1,0:T(8,128)S(1)}, f32[40,8]{1,0:T(8,128)}, u32[]{:S(2)}) copy-start(f32[40,8]{1,0:T(8,128)} %copy.6) | copy-start | bytes 3844

commit v5 on v3

--- a/solution.py
+++ b/solution.py
@@ -309,6 +309,22 @@
     )
 
 
+def after_those(arrays, *earlier):
+    def kernel(*refs):
+        pass
+
+    count = len(arrays)
+    anywhere = pl.BlockSpec(memory_space=pl.ANY)
+    return pl.pallas_call(
+        kernel,
+        in_specs=[anywhere] * (count + len(earlier)),
+        out_specs=[anywhere] * count,
+        out_shape=[pltpu.HBM(array.shape, array.dtype) for array in arrays],
+        input_output_aliases={i: i for i in range(count)},
+        name="in_order",
+    )(*[in_hbm(array) for array in arrays], *earlier)
+
+
 def body(visibilities, owner_order, group_ids, partner_flags):
     n_tm = lax.axis_size("tm")
     n_chan = lax.axis_size("chan")
@@ -339,15 +355,16 @@
     up = [(i, i + 1) for i in range(n_dev - 1)]
     down = [(i + 1, i) for i in range(n_dev - 1)]
     received_outer = exchange(OUTER, group_ids)
-    received_inner = exchange(INNER, table)
+    received_inner = exchange(INNER, group_ids)
     head = spectra(received_outer, table, n_tm, n_chan, 0, REACH, group_ids)
     tail = spectra(received_outer, table, n_tm, n_chan, REACH, REACH, group_ids)
-    after = lax.ppermute(head, AXES, down)
-    before = lax.ppermute(tail, AXES, up)
     outer_sums = outer_powers(head, tail)
+    head_sent, tail_sent = after_those((head, tail), outer_sums)
+    after = lax.ppermute(head_sent, AXES, down)
+    before = lax.ppermute(tail_sent, AXES, up)
     inner = spectra(received_inner, table, n_tm, n_chan, 0, 2 * REACH, outer_sums)
-    inner_sums = inner_powers(head, inner, tail)
-    return final_powers(before, head, tail, after, outer_sums, inner_sums, valid)
+    inner_sums = inner_powers(head_sent, inner, tail_sent)
+    return final_powers(before, head_sent, tail_sent, after, outer_sums, inner_sums, valid)
 
 
 def solution(mesh):

time: 178 us -> 162 us (0.910)
  the two profiles are of different devices: /device:TPU:46 before, /device:TPU:32 now
where the time goes in v5:
time: 162 us; the launch traced here: 160 us
  Pallas kernels  58.8 us (36%)
  waiting for transfers between devices  47.4 us (29%)
  starting transfers between devices  27.1 us (17%)
  other arithmetic  17.4 us (11%)
  local copies, waits for them, and re-layouts  8.9 us (5%)
    all_to_all x2, waiting for transfers between devices, exchange(): return lax.all_to_all(send, AXES, 0, 0, tiled=True)  46.3 us
    pallas_call x3, Pallas kernels, cross_call(): pl.pallas_call(kernel, grid=(2, CHUNKS), in_specs=specs, out_specs=out_sp...  23.7 us
    pallas_call x3, Pallas kernels, spectra(): pl.pallas_call(spectra_kernel, grid=(slots // step,), in_specs=[pl.BlockS...  20.3 us
    all_to_all x2, starting transfers between devices, exchange(): return lax.all_to_all(send, AXES, 0, 0, tiled=True)  17.4 us
    convert_element_type x1, other arithmetic, half_table(): return (weights_norm[:, None] * jnp.cos(phase_angle)).astype(jnp.bfloat16)  16.5 us
    pallas_call x2, Pallas kernels, gather(): pl.pallas_call(functools.partial(gather_kernel, slots, n_base // n_dev),...  14.8 us
    unnamed x12, local copies, waits for them, and re-layouts  8.61 us
    ppermute x1, starting transfers between devices, body(): after = lax.ppermute(head_sent, AXES, down)  7.73 us
  transfers between devices with their start and end apart: 4, of which 3 were waited for; matrix products, arithmetic and copies ran while one was open for 11% of the time, Pallas kernels for 27%

profile of v5, /device:TPU:32, one launch (start us, length us, event | category | flops | bytes accessed | tf_op | source)
XLA Modules:
  0.0 160.4 jit_solution(14843950609567633497)
XLA Ops:
  0.0 0.0 copy-start
  0.0 3.4 %copy-done = bf16[4,4096,2,128]{3,2,1,0:T(2,128)(2,1)S(1)} copy-done((bf16[4,4096,2,128]{3,2,1,0:T(2,128)(2,1)S(1)}, bf16[4,4096,2,128]{3,2,1,0:T(2,128)(2,1)}, u32[]{:S(2)}) %copy-start) | copy-done | bytes 8388632
  3.4 7.3 %slot_gather.2 = bf16[128,16,4,2,128]{4,3,2,1,0:T(2,128)(2,1)} custom-call(s32[4096]{0:T(1024)} %order_ref.3, bf16[4,4096,2,128]{3,2,1,0:T(2,128)(2,1)S(1)} %copy-done, s32[4096]{0:T(1024)} %_.7), custom_call_target="tpu_custom_call" | custom-call | bytes 8388608 | tf_op jit(solution)/shard_map/slot_gather/pallas_call | solution.py:63
  10.7 10.7 %all-to-all-start = ((bf16[128,128,128]{2,1,0:T(8,128)(2,1)}), bf16[128,128,128]{2,1,0:T(8,128)(2,1)}, u32[]{:S(2)}, u32[]{:S(2)}) async-start(bf16[128,128,128]{2,1,0:T(8,128)(2,1)} %bitcast.21), calls=%async_computation | async-start | bytes 8388608 | tf_op jit(solution)/shard_map/all_to_all | solution.py:353
  21.4 0.0 copy-start.1
  21.4 3.4 %copy-done.1 = bf16[4,4096,2,128]{3,2,1,0:T(2,128)(2,1)S(1)} copy-done((bf16[4,4096,2,128]{3,2,1,0:T(2,128)(2,1)S(1)}, bf16[4,4096,2,128]{3,2,1,0:T(2,128)(2,1)}, u32[]{:S(2)}) %copy-start.1) | copy-done | bytes 8388632
  24.8 7.5 %slot_gather.3 = bf16[128,16,4,2,128]{4,3,2,1,0:T(2,128)(2,1)} custom-call(s32[4096]{0:T(1024)} %order_ref.3, bf16[4,4096,2,128]{3,2,1,0:T(2,128)(2,1)S(1)} %copy-done.1, s32[4096]{0:T(1024)} %_.7), custom_call_target="tpu_custom_call" | custom-call | bytes 8388608 | tf_op jit(solution)/shard_map/slot_gather/pallas_call | solution.py:63
  32.2 40.9 %all-to-all-done = bf16[128,128,128]{2,1,0:T(8,128)(2,1)} async-done(((bf16[128,128,128]{2,1,0:T(8,128)(2,1)}), bf16[128,128,128]{2,1,0:T(8,128)(2,1)}, u32[]{:S(2)}, u32[]{:S(2)}) %all-to-all-start) | async-done | bytes 4194336 | tf_op jit(solution)/shard_map/all_to_all | solution.py:353
  73.1 0.0 copy-start.4
  73.1 6.7 %all-to-all-start.1 = ((bf16[128,128,128]{2,1,0:T(8,128)(2,1)}), bf16[128,128,128]{2,1,0:T(8,128)(2,1)}, u32[]{:S(2)}, u32[]{:S(2)}) async-start(bf16[128,128,128]{2,1,0:T(8,128)(2,1)} %bitcast.20), calls=%async_computation.1 | async-start | bytes 8388608 | tf_op jit(solution)/shard_map/all_to_all | solution.py:353
  79.8 0.7 multiply_reduce_fusion
  81.1 0.1 fusion.23
  81.2 16.5 %fusion.5.table_ref = bf16[1024,1024]{1,0:T(8,128)(2,1)} fusion(s32[1024]{0:T(1024)S(1)} %get-tuple-element.17, s32[1024]{0:T(1024)S(1)} %get-tuple-element.18, f32[1024]{0:T(1024)S(1)} %fusion.23), kind=kLoop, calls=%fused_computation.8 | loop fusion | flops 17825792 | bytes 2109440 | tf_op jit(solution)/shard_map/convert_element_type | solution.py:41
  97.7 0.0 copy-done.4
  97.7 5.9 %delay_spectra.4.tail.refs_1_ = bf16[2,4,8,128,128]{4,3,2,1,0:T(8,128)(2,1)} custom-call(bf16[16,8,128,128]{3,2,1,0:T(8,128)(2,1)} %bitcast.1.received_ref, bf16[1024,1024]{1,0:T(8,128)(2,1)} %fusion.5.table_ref, s32[4096]{0:T(1024)S(1)} %copy-done.4), custom_call_target="tpu_custom_call" | custom-call | flops 2147483648 | bytes 8388608 | tf_op jit(solution)/shard_map/delay_spectra/pallas_call | solution.py:125
  103.7 5.9 %delay_spectra.3.head.refs_0_ = bf16[2,4,8,128,128]{4,3,2,1,0:T(8,128)(2,1)} custom-call(bf16[16,8,128,128]{3,2,1,0:T(8,128)(2,1)} %bitcast.1.received_ref, bf16[1024,1024]{1,0:T(8,128)(2,1)} %fusion.5.table_ref, s32[4096]{0:T(1024)S(1)} %copy-done.4), custom_call_target="tpu_custom_call" | custom-call | flops 2147483648 | bytes 8388608 | tf_op jit(solution)/shard_map/delay_spectra/pallas_call | solution.py:125
  109.6 0.0 copy-start.5
  109.6 6.2 %outer_pairs.1.refs_2_._.outer_ref = f32[8,16,8,128]{3,2,1,0:T(8,128)S(1)} custom-call(bf16[2,4,8,128,128]{4,3,2,1,0:T(8,128)(2,1)} %delay_spectra.3.head.refs_0_, bf16[2,4,8,128,128]{4,3,2,1,0:T(8,128)(2,1)} %delay_spectra.4.tail.refs_1_), custom_call_target="tpu_custom_call" | custom-call | flops 14680064 | bytes 4194304 | tf_op jit(solution)/shard_map/outer_pairs/pallas_call | solution.py:236
  115.8 0.0 copy-start.2
  115.8 0.8 copy-done.2
  116.6 2.0 %collective-permute-start = (bf16[2,4,8,128,128]{4,3,2,1,0:T(8,128)(2,1)}, bf16[2,4,8,128,128]{4,3,2,1,0:T(8,128)(2,1)S(1)}, u32[]{:S(2)}, u32[]{:S(2)}) collective-permute-start(bf16[2,4,8,128,128]{4,3,2,1,0:T(8,128)(2,1)} %get-tuple-element.7.tail), channel_id=1, source_target_pairs={{0,1},{1,2},{2,3},{3,4},{4,5},{5,6},{6,7},{7,8},{8,9},{9,10},{10,1... | collective-permute-start | bytes 6291464 | tf_op jit(solution)/shard_map/ppermute | solution.py:364
  118.7 7.7 %collective-permute-start.1 = (bf16[2,4,8,128,128]{4,3,2,1,0:T(8,128)(2,1)}, bf16[2,4,8,128,128]{4,3,2,1,0:T(8,128)(2,1)}, u32[]{:S(2)}, u32[]{:S(2)}) collective-permute-start(bf16[2,4,8,128,128]{4,3,2,1,0:T(8,128)(2,1)} %get-tuple-element.8.head), channel_id=1, source_target_pairs={{1,0},{2,1},{3,2},{4,3},{5,4},{6,5},{7,6},{8,7},{9,8},{10,9},{11,1... | collective-permute-start | bytes 6291464 | tf_op jit(solution)/shard_map/ppermute | solution.py:363
  126.4 0.1 pad_dynamic-slice_fusion.1
  126.5 0.1 compare_bitcast_fusion
  126.6 0.0 copy-done.5
  126.6 0.1 and_convert_fusion
  126.7 0.1 copy.7
  126.8 5.4 %all-to-all-done.1 = bf16[128,128,128]{2,1,0:T(8,128)(2,1)} async-done(((bf16[128,128,128]{2,1,0:T(8,128)(2,1)}), bf16[128,128,128]{2,1,0:T(8,128)(2,1)}, u32[]{:S(2)}, u32[]{:S(2)}) %all-to-all-start.1) | async-done | bytes 4194336 | tf_op jit(solution)/shard_map/all_to_all | solution.py:353
  132.2 0.0 copy-start.3
  132.2 1.0 copy-done.3
  133.2 8.4 %delay_spectra.5.inner = bf16[2,4,16,128,128]{4,3,2,1,0:T(8,128)(2,1)} custom-call(bf16[16,8,128,128]{3,2,1,0:T(8,128)(2,1)} %bitcast.3.received_ref, bf16[1024,1024]{1,0:T(8,128)(2,1)} %fusion.5.table_ref, f32[8,16,8,128]{3,2,1,0:T(8,128)S(1)} %copy-done.3), custom_call_target="tpu_custom_call" | custom-call | flops 4294967296 | bytes 16777216 | tf_op jit(solution)/shard_map/delay_spectra/pallas_call | solution.py:125
  141.7 9.2 %inner_pairs.1.inner_ref = f32[8,24,8,128]{3,2,1,0:T(8,128)S(1)} custom-call(bf16[2,4,8,128,128]{4,3,2,1,0:T(8,128)(2,1)} %get-tuple-element.8.head, bf16[2,4,16,128,128]{4,3,2,1,0:T(8,128)(2,1)} %delay_spectra.5.inner, bf16[2,4,8,128,128]{4,3,2,1,0:T(8,128)(2,1)} %get-tuple-element.7.tail), custom_call_target="tpu_custom_call" | custom-call | flops 42991616 | bytes 8388608 | tf_op jit(solution)/shard_map/inner_pairs/pallas_call | solution.py:236
  150.9 1.1 collective-permute-done.before
  152.0 0.0 collective-permute-done.1.after
  152.0 0.1 broadcast_in_dim.22.valid_ref
  152.1 8.3 %pair_power.1 = f32[32,16,1024]{2,1,0:T(8,128)} custom-call(bf16[2,4,8,128,128]{4,3,2,1,0:T(8,128)(2,1)S(1)} %collective-permute-done.before, bf16[2,4,8,128,128]{4,3,2,1,0:T(8,128)(2,1)} %get-tuple-element.8.head, bf16[2,4,8,128,128]{4,3,2,1,0:T(8,128)(2,1)} %get-tuple-element.7.tail, bf16[2,4,8,128,128]{4,3,2,1,0:T(8,128)(2,1)} %collective-permute-done.1.after, ...), custom_call_target="tpu_custom_call" | custom-call | flops 18874368 | bytes 8388608 | tf_op jit(solution)/shard_map/pair_power/pallas_call | solution.py:236
  (3 shorter events, 0.0 us)
Async XLA Ops:
  0.0 3.4 %copy-start = (bf16[4,4096,2,128]{3,2,1,0:T(2,128)(2,1)S(1)}, bf16[4,4096,2,128]{3,2,1,0:T(2,128)(2,1)}, u32[]{:S(2)}) copy-start(bf16[4,4096,2,128]{3,2,1,0:T(2,128)(2,1)} %vis_ref.3) | copy-start | bytes 25165828
  10.7 62.4 %all-to-all-start = ((bf16[128,128,128]{2,1,0:T(8,128)(2,1)}), bf16[128,128,128]{2,1,0:T(8,128)(2,1)}, u32[]{:S(2)}, u32[]{:S(2)}) async-start(bf16[128,128,128]{2,1,0:T(8,128)(2,1)} %bitcast.21), calls=%async_computation | async-start | bytes 8388608 | tf_op jit(solution)/shard_map/all_to_all | solution.py:353
  21.4 3.4 %copy-start.1 = (bf16[4,4096,2,128]{3,2,1,0:T(2,128)(2,1)S(1)}, bf16[4,4096,2,128]{3,2,1,0:T(2,128)(2,1)}, u32[]{:S(2)}) copy-start(bf16[4,4096,2,128]{3,2,1,0:T(2,128)(2,1)} %vis_ref.3) | copy-start | bytes 25165828
  73.1 24.6 %copy-start.4 = (s32[4096]{0:T(1024)S(1)}, s32[4096]{0:T(1024)}, u32[]{:S(2)}) copy-start(s32[4096]{0:T(1024)} %_.7) | copy-start | bytes 49156
  73.1 59.1 %all-to-all-start.1 = ((bf16[128,128,128]{2,1,0:T(8,128)(2,1)}), bf16[128,128,128]{2,1,0:T(8,128)(2,1)}, u32[]{:S(2)}, u32[]{:S(2)}) async-start(bf16[128,128,128]{2,1,0:T(8,128)(2,1)} %bitcast.20), calls=%async_computation.1 | async-start | bytes 8388608 | tf_op jit(solution)/shard_map/all_to_all | solution.py:353
  109.6 17.0 %copy-start.5 = (s32[4096,8]{0,1:T(8,128)S(1)}, s32[4096,8]{0,1:T(8,128)}, u32[]{:S(2)}) copy-start(s32[4096,8]{0,1:T(8,128)} %param.7) | copy-start | bytes 393220
  115.8 0.8 copy-start.2
  116.6 35.3 %collective-permute-start = (bf16[2,4,8,128,128]{4,3,2,1,0:T(8,128)(2,1)}, bf16[2,4,8,128,128]{4,3,2,1,0:T(8,128)(2,1)S(1)}, u32[]{:S(2)}, u32[]{:S(2)}) collective-permute-start(bf16[2,4,8,128,128]{4,3,2,1,0:T(8,128)(2,1)} %get-tuple-element.7.tail), channel_id=1, source_target_pairs={{0,1},{1,2},{2,3},{3,4},{4,5},{5,6},{6,7},{7,8},{8,9},{9,10},{10,1... | collective-permute-start | bytes 6291464 | tf_op jit(solution)/shard_map/ppermute | solution.py:364
  118.7 33.3 %collective-permute-start.1 = (bf16[2,4,8,128,128]{4,3,2,1,0:T(8,128)(2,1)}, bf16[2,4,8,128,128]{4,3,2,1,0:T(8,128)(2,1)}, u32[]{:S(2)}, u32[]{:S(2)}) collective-permute-start(bf16[2,4,8,128,128]{4,3,2,1,0:T(8,128)(2,1)} %get-tuple-element.8.head), channel_id=1, source_target_pairs={{1,0},{2,1},{3,2},{4,3},{5,4},{6,5},{7,6},{8,7},{9,8},{10,9},{11,1... | collective-permute-start | bytes 6291464 | tf_op jit(solution)/shard_map/ppermute | solution.py:363
  132.2 1.0 copy-start.3

commit v6 on v3

--- a/solution.py
+++ b/solution.py
@@ -12,8 +12,10 @@
 MIB = 2**20
 LANES = 128
 REACH = 8
-OUTER = tuple(range(8)) + tuple(range(24, 32))
-INNER = tuple(range(8, 24))
+HEAD, TAIL = tuple(range(8)), tuple(range(24, 32))
+MIDDLE = tuple(range(8, 12)) + tuple(range(20, 24))
+OUTER = HEAD + MIDDLE + TAIL
+INNER = tuple(range(12, 20))
 
 
 def in_hbm(array):
@@ -141,7 +143,7 @@
             transcendentals=0,
         ),
         name="delay_spectra",
-    )(in_hbm(received.reshape(n_tm, n_chan, pairs, lanes)), in_hbm(table), earlier)
+    )(in_hbm(received.reshape(n_tm, n_chan, pairs, lanes)), in_hbm(table), in_hbm(earlier))
 
 
 def fold_rows(sums):
@@ -177,25 +179,29 @@
     target[pl.ds(at, source.shape[0])] = source[...].astype(jnp.float32)
 
 
-def outer_kernel(head, tail, out_ref, rows_ref):
+def outer_kernel(head, middle, tail, out_ref, rows_ref):
     load_rows(rows_ref, 0, head.at[0, 0])
-    load_rows(rows_ref, REACH, tail.at[0, 0])
+    load_rows(rows_ref, REACH, middle.at[0, 0])
+    load_rows(rows_ref, 2 * REACH, tail.at[0, 0])
+    run = len(OUTER) // 2
 
     def one_run(i, carry):
-        for j in range(REACH):
-            s = i * REACH + j
-            out_ref[0, s] = cross_tile(rows_ref, s, range(1, REACH - j))
+        for j in range(run):
+            s = i * run + j
+            out_ref[0, s] = cross_tile(rows_ref, s, range(1, min(REACH, run - 1 - j) + 1))
         return carry
 
     lax.fori_loop(0, 2, one_run, 0)
 
 
-def inner_kernel(head, inner, tail, out_ref, rows_ref):
-    load_rows(rows_ref, 0, head.at[0, 0])
-    load_rows(rows_ref, REACH, inner.at[0, 0])
-    load_rows(rows_ref, 3 * REACH, tail.at[0, 0])
-    for s in range(3 * REACH):
-        out_ref[0, s] = cross_tile(rows_ref, s, range(max(1, REACH - s), REACH + 1))
+def inner_kernel(head, middle, inner, tail, out_ref, rows_ref):
+    load_rows(rows_ref, 0, head.at[0, 0, pl.ds(4, 4)])
+    load_rows(rows_ref, 4, middle.at[0, 0, pl.ds(0, 4)])
+    load_rows(rows_ref, 8, inner.at[0, 0])
+    load_rows(rows_ref, 16, middle.at[0, 0, pl.ds(4, 4)])
+    load_rows(rows_ref, 20, tail.at[0, 0, pl.ds(0, 4)])
+    for j in range(2 * REACH):
+        out_ref[0, j] = cross_tile(rows_ref, j, range(max(1, REACH - j), REACH + 1))
 
 
 def final_kernel(before, head, tail, after, outer_ref, inner_ref, valid_ref, out_ref, rows_ref):
@@ -216,8 +222,8 @@
             terms.append(cross_tile(rows_ref, at, range(REACH - j, REACH + 1)))
         if s in OUTER:
             terms.append(outer_ref[0, OUTER.index(s)])
-        if 0 <= s < slots - REACH:
-            terms.append(inner_ref[0, s])
+        if 4 <= s < 20:
+            terms.append(inner_ref[0, s - 4])
         value = jnp.take_along_axis(sum(terms[1:], terms[0]), order, axis=1)
         powers[s] = jnp.where(valid_ref[s + REACH] > 0.0, value * (1.0 / 64.0), 0.0)
         if s >= 0:
@@ -258,31 +264,30 @@
     return pl.BlockSpec((1, slots, REACH, LANES), lambda i, j: (i * CHUNKS + j, 0, 0, 0))
 
 
-def outer_powers(head, tail):
-    slots = 2 * REACH
+def outer_powers(head, middle, tail):
+    slots = len(OUTER)
     return cross_call(
         outer_kernel,
         "outer_pairs",
-        [in_hbm(head), in_hbm(tail)],
-        [spectra_spec(head)] * 2,
+        [in_hbm(head), in_hbm(middle), in_hbm(tail)],
+        [spectra_spec(head)] * 3,
         sums_spec(slots),
-        jax.ShapeDtypeStruct((2 * CHUNKS, slots, REACH, LANES), jnp.float32),
+        pltpu.HBM((2 * CHUNKS, slots, REACH, LANES), jnp.float32),
         slots,
-        56,
-    )
-
-
-def inner_powers(head, inner, tail):
-    slots = 3 * REACH
+        120,
+    )
+
+
+def inner_powers(head, middle, inner, tail):
     return cross_call(
         inner_kernel,
         "inner_pairs",
-        [in_hbm(head), in_hbm(inner), in_hbm(tail)],
-        [spectra_spec(array) for array in (head, inner, tail)],
-        sums_spec(slots),
-        jax.ShapeDtypeStruct((2 * CHUNKS, slots, REACH, LANES), jnp.float32),
-        4 * REACH,
-        164,
+        [in_hbm(head), in_hbm(middle), in_hbm(inner), in_hbm(tail)],
+        [spectra_spec(head)] * 4,
+        sums_spec(2 * REACH),
+        pltpu.HBM((2 * CHUNKS, 2 * REACH, REACH, LANES), jnp.float32),
+        3 * REACH,
+        100,
     )
 
 
@@ -292,7 +297,7 @@
     return cross_call(
         final_kernel,
         "pair_power",
-        [before, in_hbm(head), in_hbm(tail), after, outer_sums, inner_sums, valid],
+        [before, in_hbm(head), in_hbm(tail), after, in_hbm(outer_sums), in_hbm(inner_sums), valid],
         spectra_specs
         + [
             sums_spec(outer_sums.shape[1]),
@@ -341,12 +346,13 @@
     received_outer = exchange(OUTER, group_ids)
     received_inner = exchange(INNER, table)
     head = spectra(received_outer, table, n_tm, n_chan, 0, REACH, group_ids)
-    tail = spectra(received_outer, table, n_tm, n_chan, REACH, REACH, group_ids)
+    tail = spectra(received_outer, table, n_tm, n_chan, 2 * REACH, REACH, group_ids)
     after = lax.ppermute(head, AXES, down)
     before = lax.ppermute(tail, AXES, up)
-    outer_sums = outer_powers(head, tail)
-    inner = spectra(received_inner, table, n_tm, n_chan, 0, 2 * REACH, outer_sums)
-    inner_sums = inner_powers(head, inner, tail)
+    middle = spectra(received_outer, table, n_tm, n_chan, REACH, REACH, group_ids)
+    outer_sums = outer_powers(head, middle, tail)
+    inner = spectra(received_inner, table, n_tm, n_chan, 0, REACH, outer_sums)
+    inner_sums = inner_powers(head, middle, inner, tail)
     return final_powers(before, head, tail, after, outer_sums, inner_sums, valid)
 
 

time: 178 us -> 166 us (0.933)
  the two profiles are of different devices: /device:TPU:46 before, /device:TPU:32 now
where the time goes in v6:
time: 166 us; the launch traced here: 164 us
  Pallas kernels  64.7 us (39%)
  waiting for transfers between devices  47.3 us (28%)
  starting transfers between devices  26.4 us (16%)
  other arithmetic  17.4 us (10%)
  local copies, waits for them, and re-layouts  7.07 us (4%)
    all_to_all x2, waiting for transfers between devices, exchange(): return lax.all_to_all(send, AXES, 0, 0, tiled=True)  46.9 us
    pallas_call x3, Pallas kernels, cross_call(): pl.pallas_call(kernel, grid=(2, CHUNKS), in_specs=specs, out_specs=out_sp...  25.8 us
    pallas_call x4, Pallas kernels, spectra(): pl.pallas_call(spectra_kernel, grid=(slots // step,), in_specs=[pl.BlockS...  23.9 us
    all_to_all x2, starting transfers between devices, exchange(): return lax.all_to_all(send, AXES, 0, 0, tiled=True)  18 us
    convert_element_type x1, other arithmetic, half_table(): return (weights_norm[:, None] * jnp.cos(phase_angle)).astype(jnp.bfloat16)  16.5 us
    pallas_call x2, Pallas kernels, gather(): pl.pallas_call(functools.partial(gather_kernel, slots, n_base // n_dev),...  14.9 us
    unnamed x8, local copies, waits for them, and re-layouts  6.77 us
    ppermute x1, starting transfers between devices, body(): after = lax.ppermute(head, AXES, down)  6.41 us
  transfers between devices with their start and end apart: 4, of which 2 were waited for; matrix products, arithmetic and copies ran while one was open for 11% of the time, Pallas kernels for 29%

profile of v6, /device:TPU:32, one launch (start us, length us, event | category | flops | bytes accessed | tf_op | source)
XLA Modules:
  0.0 163.6 jit_solution(2549415712168846057)
XLA Ops:
  0.0 0.0 copy-start
  0.0 3.4 %copy-done = bf16[4,4096,2,128]{3,2,1,0:T(2,128)(2,1)S(1)} copy-done((bf16[4,4096,2,128]{3,2,1,0:T(2,128)(2,1)S(1)}, bf16[4,4096,2,128]{3,2,1,0:T(2,128)(2,1)}, u32[]{:S(2)}) %copy-start) | copy-done | bytes 8388632
  3.4 9.3 %slot_gather.2 = bf16[128,24,4,2,128]{4,3,2,1,0:T(2,128)(2,1)} custom-call(s32[4096]{0:T(1024)} %order_ref.3, bf16[4,4096,2,128]{3,2,1,0:T(2,128)(2,1)S(1)} %copy-done, s32[4096]{0:T(1024)} %_.7), custom_call_target="tpu_custom_call" | custom-call | bytes 12582912 | tf_op jit(solution)/shard_map/slot_gather/pallas_call | solution.py:65
  12.6 10.6 %all-to-all-start = ((bf16[128,192,128]{2,1,0:T(8,128)(2,1)}), bf16[128,192,128]{2,1,0:T(8,128)(2,1)}, u32[]{:S(2)}, u32[]{:S(2)}) async-start(bf16[128,192,128]{2,1,0:T(8,128)(2,1)} %bitcast.20), calls=%async_computation | async-start | bytes 12582912 | tf_op jit(solution)/shard_map/all_to_all | solution.py:342
  23.3 0.7 multiply_reduce_fusion
  24.6 0.1 fusion.23
  24.7 16.5 %fusion.5.table_ref._ = bf16[1024,1024]{1,0:T(8,128)(2,1)} fusion(s32[1024]{0:T(1024)S(1)} %get-tuple-element.13, s32[1024]{0:T(1024)S(1)} %get-tuple-element.14, f32[1024]{0:T(1024)S(1)} %fusion.23), kind=kLoop, calls=%fused_computation.8 | loop fusion | flops 17825792 | bytes 2109440 | tf_op jit(solution)/shard_map/convert_element_type | solution.py:43
  41.2 0.0 copy-start.1
  41.2 3.4 %copy-done.1 = bf16[4,4096,2,128]{3,2,1,0:T(2,128)(2,1)S(1)} copy-done((bf16[4,4096,2,128]{3,2,1,0:T(2,128)(2,1)S(1)}, bf16[4,4096,2,128]{3,2,1,0:T(2,128)(2,1)}, u32[]{:S(2)}) %copy-start.1) | copy-done | bytes 8388632
  44.6 5.6 %slot_gather.3 = bf16[128,8,4,2,128]{4,3,2,1,0:T(2,128)(2,1)} custom-call(s32[4096]{0:T(1024)} %order_ref.3, bf16[4,4096,2,128]{3,2,1,0:T(2,128)(2,1)S(1)} %copy-done.1, bf16[1024,1024]{1,0:T(8,128)(2,1)} %fusion.5.table_ref._), custom_call_target="tpu_custom_call" | custom-call | bytes 4194304 | tf_op jit(solution)/shard_map/slot_gather/pallas_call | solution.py:65
  50.3 46.9 %all-to-all-done = bf16[128,192,128]{2,1,0:T(8,128)(2,1)} async-done(((bf16[128,192,128]{2,1,0:T(8,128)(2,1)}), bf16[128,192,128]{2,1,0:T(8,128)(2,1)}, u32[]{:S(2)}, u32[]{:S(2)}) %all-to-all-start) | async-done | bytes 6291488 | tf_op jit(solution)/shard_map/all_to_all | solution.py:342
  97.2 7.4 %all-to-all-start.1 = ((bf16[128,64,128]{2,1,0:T(8,128)(2,1)}), bf16[128,64,128]{2,1,0:T(8,128)(2,1)}, u32[]{:S(2)}, u32[]{:S(2)}) async-start(bf16[128,64,128]{2,1,0:T(8,128)(2,1)} %bitcast.21), calls=%async_computation.1 | async-start | bytes 4194304 | tf_op jit(solution)/shard_map/all_to_all | solution.py:342
  104.6 6.0 %delay_spectra.5.head = bf16[2,4,8,128,128]{4,3,2,1,0:T(8,128)(2,1)} custom-call(bf16[16,8,192,128]{3,2,1,0:T(8,128)(2,1)} %bitcast.1.received_ref, bf16[1024,1024]{1,0:T(8,128)(2,1)} %fusion.5.table_ref._, s32[4096]{0:T(1024)} %_.7), custom_call_target="tpu_custom_call" | custom-call | flops 2147483648 | bytes 8388608 | tf_op jit(solution)/shard_map/delay_spectra/pallas_call | solution.py:127
  110.6 0.0 copy-start.2
  110.6 0.0 copy-start.3
  110.6 6.0 %delay_spectra.4.tail = bf16[2,4,8,128,128]{4,3,2,1,0:T(8,128)(2,1)} custom-call(bf16[16,8,192,128]{3,2,1,0:T(8,128)(2,1)} %bitcast.1.received_ref, bf16[1024,1024]{1,0:T(8,128)(2,1)} %fusion.5.table_ref._, s32[4096]{0:T(1024)} %_.7), custom_call_target="tpu_custom_call" | custom-call | flops 2147483648 | bytes 8388608 | tf_op jit(solution)/shard_map/delay_spectra/pallas_call | solution.py:127
  116.6 6.4 %collective-permute-start.1 = (bf16[2,4,8,128,128]{4,3,2,1,0:T(8,128)(2,1)}, bf16[2,4,8,128,128]{4,3,2,1,0:T(8,128)(2,1)S(1)}, u32[]{:S(2)}, u32[]{:S(2)}) collective-permute-start(bf16[2,4,8,128,128]{4,3,2,1,0:T(8,128)(2,1)} %delay_spectra.5.head), channel_id=1, source_target_pairs={{1,0},{2,1},{3,2},{4,3},{5,4},{6,5},{7,6},{8,7},{9,8},{10,9},{11,1... | collective-permute-start | bytes 6291464 | tf_op jit(solution)/shard_map/ppermute | solution.py:350
  123.1 1.9 %collective-permute-start = (bf16[2,4,8,128,128]{4,3,2,1,0:T(8,128)(2,1)}, bf16[2,4,8,128,128]{4,3,2,1,0:T(8,128)(2,1)}, u32[]{:S(2)}, u32[]{:S(2)}) collective-permute-start(bf16[2,4,8,128,128]{4,3,2,1,0:T(8,128)(2,1)} %delay_spectra.4.tail), channel_id=1, source_target_pairs={{0,1},{1,2},{2,3},{3,4},{4,5},{5,6},{6,7},{7,8},{8,9},{9,10},{10,1... | collective-permute-start | bytes 6291464 | tf_op jit(solution)/shard_map/ppermute | solution.py:351
  125.0 0.0 copy-done.2
  125.0 0.1 pad_dynamic-slice_fusion.1
  125.1 0.1 compare_bitcast_fusion
  125.2 0.0 copy-done.3
  125.2 0.1 and_convert_fusion
  125.3 0.1 copy.5
  125.4 6.0 %delay_spectra.6.middle = bf16[2,4,8,128,128]{4,3,2,1,0:T(8,128)(2,1)} custom-call(bf16[16,8,192,128]{3,2,1,0:T(8,128)(2,1)} %bitcast.1.received_ref, bf16[1024,1024]{1,0:T(8,128)(2,1)} %fusion.5.table_ref._, s32[4096]{0:T(1024)} %_.7), custom_call_target="tpu_custom_call" | custom-call | flops 2147483648 | bytes 8388608 | tf_op jit(solution)/shard_map/delay_spectra/pallas_call | solution.py:127
  131.3 8.9 %outer_pairs.1._.outer_ref = f32[8,24,8,128]{3,2,1,0:T(8,128)} custom-call(bf16[2,4,8,128,128]{4,3,2,1,0:T(8,128)(2,1)} %delay_spectra.5.head, bf16[2,4,8,128,128]{4,3,2,1,0:T(8,128)(2,1)} %delay_spectra.6.middle, bf16[2,4,8,128,128]{4,3,2,1,0:T(8,128)(2,1)} %delay_spectra.4.tail), custom_call_target="tpu_custom_call" | custom-call | flops 31457280 | bytes 6291456 | tf_op jit(solution)/shard_map/outer_pairs/pallas_call | solution.py:242
  140.3 0.0 all-to-all-done.1
  140.3 5.9 %delay_spectra.7.inner = bf16[2,4,8,128,128]{4,3,2,1,0:T(8,128)(2,1)} custom-call(bf16[16,8,64,128]{3,2,1,0:T(8,128)(2,1)} %bitcast.3.received_ref, bf16[1024,1024]{1,0:T(8,128)(2,1)} %fusion.5.table_ref._, f32[8,24,8,128]{3,2,1,0:T(8,128)} %outer_pairs.1._.outer_ref), custom_call_target="tpu_custom_call" | custom-call | flops 2147483648 | bytes 8388608 | tf_op jit(solution)/shard_map/delay_spectra/pallas_call | solution.py:127
  146.2 8.4 %inner_pairs.1.inner_ref = f32[8,16,8,128]{3,2,1,0:T(8,128)} custom-call(bf16[2,4,8,128,128]{4,3,2,1,0:T(8,128)(2,1)} %delay_spectra.5.head, bf16[2,4,8,128,128]{4,3,2,1,0:T(8,128)(2,1)} %delay_spectra.6.middle, bf16[2,4,8,128,128]{4,3,2,1,0:T(8,128)(2,1)} %delay_spectra.7.inner, bf16[2,4,8,128,128]{4,3,2,1,0:T(8,128)(2,1)} %delay_spectra.4.tail), custom_call_target="tpu_custom_call" | custom-call | flops 26214400 | bytes 6291456 | tf_op jit(solution)/shard_map/inner_pairs/pallas_call | solution.py:242
  154.6 0.0 collective-permute-done.1.after
  154.6 0.4 collective-permute-done.before
  155.0 0.1 broadcast_in_dim.22.valid_ref
  155.1 8.5 %pair_power.1 = f32[32,16,1024]{2,1,0:T(8,128)} custom-call(bf16[2,4,8,128,128]{4,3,2,1,0:T(8,128)(2,1)} %collective-permute-done.before, bf16[2,4,8,128,128]{4,3,2,1,0:T(8,128)(2,1)} %delay_spectra.5.head, bf16[2,4,8,128,128]{4,3,2,1,0:T(8,128)(2,1)} %delay_spectra.4.tail, bf16[2,4,8,128,128]{4,3,2,1,0:T(8,128)(2,1)S(1)} %collective-permute-done.1.after, ...), custom_call_target="tpu_custom_call" | custom-call | flops 18874368 | bytes 8388608 | tf_op jit(solution)/shard_map/pair_power/pallas_call | solution.py:242
  (2 shorter events, 0.0 us)
Async XLA Ops:
  0.0 3.4 %copy-start = (bf16[4,4096,2,128]{3,2,1,0:T(2,128)(2,1)S(1)}, bf16[4,4096,2,128]{3,2,1,0:T(2,128)(2,1)}, u32[]{:S(2)}) copy-start(bf16[4,4096,2,128]{3,2,1,0:T(2,128)(2,1)} %vis_ref.3) | copy-start | bytes 25165828
  12.6 84.5 %all-to-all-start = ((bf16[128,192,128]{2,1,0:T(8,128)(2,1)}), bf16[128,192,128]{2,1,0:T(8,128)(2,1)}, u32[]{:S(2)}, u32[]{:S(2)}) async-start(bf16[128,192,128]{2,1,0:T(8,128)(2,1)} %bitcast.20), calls=%async_computation | async-start | bytes 12582912 | tf_op jit(solution)/shard_map/all_to_all | solution.py:342
  41.2 3.4 %copy-start.1 = (bf16[4,4096,2,128]{3,2,1,0:T(2,128)(2,1)S(1)}, bf16[4,4096,2,128]{3,2,1,0:T(2,128)(2,1)}, u32[]{:S(2)}) copy-start(bf16[4,4096,2,128]{3,2,1,0:T(2,128)(2,1)} %vis_ref.3) | copy-start | bytes 25165828
  97.2 43.1 %all-to-all-start.1 = ((bf16[128,64,128]{2,1,0:T(8,128)(2,1)}), bf16[128,64,128]{2,1,0:T(8,128)(2,1)}, u32[]{:S(2)}, u32[]{:S(2)}) async-start(bf16[128,64,128]{2,1,0:T(8,128)(2,1)} %bitcast.21), calls=%async_computation.1 | async-start | bytes 4194304 | tf_op jit(solution)/shard_map/all_to_all | solution.py:342
  110.6 14.4 %copy-start.2 = (s32[4096]{0:T(1024)S(1)}, s32[4096]{0:T(1024)}, u32[]{:S(2)}) copy-start(s32[4096]{0:T(1024)} %_.7) | copy-start | bytes 49156
  110.6 14.6 %copy-start.3 = (s32[4096,8]{0,1:T(8,128)S(1)}, s32[4096,8]{0,1:T(8,128)}, u32[]{:S(2)}) copy-start(s32[4096,8]{0,1:T(8,128)} %param.7) | copy-start | bytes 393220
  116.6 38.0 %collective-permute-start.1 = (bf16[2,4,8,128,128]{4,3,2,1,0:T(8,128)(2,1)}, bf16[2,4,8,128,128]{4,3,2,1,0:T(8,128)(2,1)S(1)}, u32[]{:S(2)}, u32[]{:S(2)}) collective-permute-start(bf16[2,4,8,128,128]{4,3,2,1,0:T(8,128)(2,1)} %delay_spectra.5.head), channel_id=1, source_target_pairs={{1,0},{2,1},{3,2},{4,3},{5,4},{6,5},{7,6},{8,7},{9,8},{10,9},{11,1... | collective-permute-start | bytes 6291464 | tf_op jit(solution)/shard_map/ppermute | solution.py:350
  123.1 31.9 %collective-permute-start = (bf16[2,4,8,128,128]{4,3,2,1,0:T(8,128)(2,1)}, bf16[2,4,8,128,128]{4,3,2,1,0:T(8,128)(2,1)}, u32[]{:S(2)}, u32[]{:S(2)}) collective-permute-start(bf16[2,4,8,128,128]{4,3,2,1,0:T(8,128)(2,1)} %delay_spectra.4.tail), channel_id=1, source_target_pairs={{0,1},{1,2},{2,3},{3,4},{4,5},{5,6},{6,7},{7,8},{8,9},{9,10},{10,1... | collective-permute-start | bytes 6291464 | tf_op jit(solution)/shard_map/ppermute | solution.py:351

commit v7 on v3

--- a/solution.py
+++ b/solution.py
@@ -141,7 +141,7 @@
             transcendentals=0,
         ),
         name="delay_spectra",
-    )(in_hbm(received.reshape(n_tm, n_chan, pairs, lanes)), in_hbm(table), earlier)
+    )(in_hbm(received.reshape(n_tm, n_chan, pairs, lanes)), in_hbm(table), in_hbm(earlier))
 
 
 def fold_rows(sums):
@@ -178,24 +178,27 @@
 
 
 def outer_kernel(head, tail, out_ref, rows_ref):
-    load_rows(rows_ref, 0, head.at[0, 0])
-    load_rows(rows_ref, REACH, tail.at[0, 0])
-
-    def one_run(i, carry):
-        for j in range(REACH):
-            s = i * REACH + j
-            out_ref[0, s] = cross_tile(rows_ref, s, range(1, REACH - j))
+    def one_chunk(c, carry):
+        load_rows(rows_ref, 0, head.at[0, c])
+        load_rows(rows_ref, REACH, tail.at[0, c])
+        for first in (0, REACH):
+            for j in range(REACH):
+                out_ref[c, first + j] = cross_tile(rows_ref, first + j, range(1, REACH - j))
         return carry
 
-    lax.fori_loop(0, 2, one_run, 0)
+    lax.fori_loop(0, STEP, one_chunk, 0)
 
 
 def inner_kernel(head, inner, tail, out_ref, rows_ref):
-    load_rows(rows_ref, 0, head.at[0, 0])
-    load_rows(rows_ref, REACH, inner.at[0, 0])
-    load_rows(rows_ref, 3 * REACH, tail.at[0, 0])
-    for s in range(3 * REACH):
-        out_ref[0, s] = cross_tile(rows_ref, s, range(max(1, REACH - s), REACH + 1))
+    def one_chunk(c, carry):
+        load_rows(rows_ref, 0, head.at[0, c])
+        load_rows(rows_ref, REACH, inner.at[0, c])
+        load_rows(rows_ref, 3 * REACH, tail.at[0, c])
+        for s in range(3 * REACH):
+            out_ref[c, s] = cross_tile(rows_ref, s, range(max(1, REACH - s), REACH + 1))
+        return carry
+
+    lax.fori_loop(0, STEP, one_chunk, 0)
 
 
 def final_kernel(before, head, tail, after, outer_ref, inner_ref, valid_ref, out_ref, rows_ref):
@@ -205,42 +208,49 @@
     mirror = pl.program_id(0) == 1
     order = jnp.where(mirror, (LANES - lane) % LANES, lane)
     slots = out_ref.shape[0]
-    for i, source in enumerate((before, head, tail, after)):
-        load_rows(rows_ref, i * REACH, source.at[0, 0])
-    powers = {}
-    for s in range(-REACH, slots):
-        terms = []
-        if s < 0 or s >= slots - REACH:
-            j = s % REACH
-            at = j if s < 0 else 2 * REACH + j
-            terms.append(cross_tile(rows_ref, at, range(REACH - j, REACH + 1)))
-        if s in OUTER:
-            terms.append(outer_ref[0, OUTER.index(s)])
-        if 0 <= s < slots - REACH:
-            terms.append(inner_ref[0, s])
-        value = jnp.take_along_axis(sum(terms[1:], terms[0]), order, axis=1)
-        powers[s] = jnp.where(valid_ref[s + REACH] > 0.0, value * (1.0 / 64.0), 0.0)
-        if s >= 0:
-            out_ref[s, pl.ds(0, REACH), :] = powers[s]
-            backward = powers[s - 1]
-            for k in range(2, REACH + 1):
-                backward = jnp.where(row == k - 1, powers[s - k], backward)
-            out_ref[s, pl.ds(REACH, REACH), :] = backward
-
-
-CHUNKS = 4
+
+    def one_chunk(c, carry):
+        at = jnp.where(mirror, STEP - 1 - c, c)
+        lanes = pl.ds(pl.multiple_of(at * LANES, LANES), LANES)
+        for i, source in enumerate((before, head, tail, after)):
+            load_rows(rows_ref, i * REACH, source.at[0, c])
+        powers = {}
+        for s in range(-REACH, slots):
+            terms = []
+            if s < 0 or s >= slots - REACH:
+                j = s % REACH
+                start = j if s < 0 else 2 * REACH + j
+                terms.append(cross_tile(rows_ref, start, range(REACH - j, REACH + 1)))
+            if s in OUTER:
+                terms.append(outer_ref[c, OUTER.index(s)])
+            if 0 <= s < slots - REACH:
+                terms.append(inner_ref[c, s])
+            value = jnp.take_along_axis(sum(terms[1:], terms[0]), order, axis=1)
+            powers[s] = jnp.where(valid_ref[s + REACH] > 0.0, value * (1.0 / 64.0), 0.0)
+            if s >= 0:
+                out_ref[s, pl.ds(0, REACH), lanes] = powers[s]
+                backward = powers[s - 1]
+                for k in range(2, REACH + 1):
+                    backward = jnp.where(row == k - 1, powers[s - k], backward)
+                out_ref[s, pl.ds(REACH, REACH), lanes] = backward
+        return carry
+
+    lax.fori_loop(0, STEP, one_chunk, 0)
+
+
+CHUNKS, STEP = 4, 2
 
 
 def cross_call(kernel, name, operands, specs, out_specs, out_shape, held, pairs):
     rows = 128
     return pl.pallas_call(
         kernel,
-        grid=(2, CHUNKS),
+        grid=(2, CHUNKS // STEP),
         in_specs=specs,
         out_specs=out_specs,
         out_shape=out_shape,
         scratch_shapes=[pltpu.VMEM((held, rows, LANES), jnp.float32)],
-        compiler_params=pltpu.CompilerParams(vmem_limit_bytes=24 * MIB),
+        compiler_params=pltpu.CompilerParams(vmem_limit_bytes=32 * MIB),
         cost_estimate=pl.CostEstimate(
             flops=2 * pairs * rows * 1024,
             bytes_accessed=2 * held * rows * 1024,
@@ -251,11 +261,13 @@
 
 
 def spectra_spec(array):
-    return pl.BlockSpec((1, 1) + array.shape[2:], lambda i, j: (i, j, 0, 0, 0))
+    return pl.BlockSpec((1, STEP) + array.shape[2:], lambda i, j: (i, j, 0, 0, 0))
 
 
 def sums_spec(slots):
-    return pl.BlockSpec((1, slots, REACH, LANES), lambda i, j: (i * CHUNKS + j, 0, 0, 0))
+    return pl.BlockSpec(
+        (STEP, slots, REACH, LANES), lambda i, j: (i * (CHUNKS // STEP) + j, 0, 0, 0)
+    )
 
 
 def outer_powers(head, tail):
@@ -266,7 +278,7 @@
         [in_hbm(head), in_hbm(tail)],
         [spectra_spec(head)] * 2,
         sums_spec(slots),
-        jax.ShapeDtypeStruct((2 * CHUNKS, slots, REACH, LANES), jnp.float32),
+        pltpu.HBM((2 * CHUNKS, slots, REACH, LANES), jnp.float32),
         slots,
         56,
     )
@@ -280,7 +292,7 @@
         [in_hbm(head), in_hbm(inner), in_hbm(tail)],
         [spectra_spec(array) for array in (head, inner, tail)],
         sums_spec(slots),
-        jax.ShapeDtypeStruct((2 * CHUNKS, slots, REACH, LANES), jnp.float32),
+        pltpu.HBM((2 * CHUNKS, slots, REACH, LANES), jnp.float32),
         4 * REACH,
         164,
     )
@@ -292,7 +304,7 @@
     return cross_call(
         final_kernel,
         "pair_power",
-        [before, in_hbm(head), in_hbm(tail), after, outer_sums, inner_sums, valid],
+        [before, in_hbm(head), in_hbm(tail), after, in_hbm(outer_sums), in_hbm(inner_sums), valid],
         spectra_specs
         + [
             sums_spec(outer_sums.shape[1]),
@@ -300,8 +312,8 @@
             pl.BlockSpec(valid.shape, lambda i, j: (0, 0, 0)),
         ],
         pl.BlockSpec(
-            (slots, 2 * REACH, LANES),
-            lambda i, j: (0, 0, jnp.where(i == 0, j, 2 * CHUNKS - 1 - j)),
+            (slots, 2 * REACH, STEP * LANES),
+            lambda i, j: (0, 0, jnp.where(i == 0, j, 2 * CHUNKS // STEP - 1 - j)),
         ),
         jax.ShapeDtypeStruct((slots, 2 * REACH, 2 * CHUNKS * LANES), jnp.float32),
         slots,
@@ -339,7 +351,7 @@
     up = [(i, i + 1) for i in range(n_dev - 1)]
     down = [(i + 1, i) for i in range(n_dev - 1)]
     received_outer = exchange(OUTER, group_ids)
-    received_inner = exchange(INNER, table)
+    received_inner = exchange(INNER, group_ids)
     head = spectra(received_outer, table, n_tm, n_chan, 0, REACH, group_ids)
     tail = spectra(received_outer, table, n_tm, n_chan, REACH, REACH, group_ids)
     after = lax.ppermute(head, AXES, down)

time: 178 us -> 176 us (0.989)
  Pallas kernels: 58.8 us -> 56.5 us
    pallas_call x3, Pallas kernels: 23.7 us -> 21.4 us  [cross_call(): pl.pallas_call(kernel, grid=(2, CHUNKS // STEP), in_specs=specs, out_spec...]
where the time goes in v7:
time: 176 us; the launch traced here: 175 us
  waiting for transfers between devices  67.1 us (38%)
  Pallas kernels  56.5 us (32%)
  starting transfers between devices  26.1 us (15%)
  other arithmetic  17.4 us (10%)
  local copies, waits for them, and re-layouts  7.06 us (4%)
    all_to_all x2, waiting for transfers between devices, exchange(): return lax.all_to_all(send, AXES, 0, 0, tiled=True)  67.1 us
    pallas_call x3, Pallas kernels, cross_call(): pl.pallas_call(kernel, grid=(2, CHUNKS // STEP), in_specs=specs, out_spec...  21.4 us
    all_to_all x2, starting transfers between devices, exchange(): return lax.all_to_all(send, AXES, 0, 0, tiled=True)  20.6 us
    pallas_call x3, Pallas kernels, spectra(): pl.pallas_call(spectra_kernel, grid=(slots // step,), in_specs=[pl.BlockS...  20.3 us
    convert_element_type x1, other arithmetic, half_table(): return (weights_norm[:, None] * jnp.cos(phase_angle)).astype(jnp.bfloat16)  16.5 us
    pallas_call x2, Pallas kernels, gather(): pl.pallas_call(functools.partial(gather_kernel, slots, n_base // n_dev),...  14.8 us
    unnamed x8, local copies, waits for them, and re-layouts  6.77 us
  transfers between devices with their start and end apart: 4, of which 2 were waited for; matrix products, arithmetic and copies ran while one was open for 10% of the time, Pallas kernels for 24%

profile of v7, /device:TPU:46, one launch (start us, length us, event | category | flops | bytes accessed | tf_op | source)
XLA Modules:
  0.0 175.0 jit_solution(9777509124135332892)
XLA Ops:
  0.0 0.0 copy-start
  0.0 3.4 %copy-done = bf16[4,4096,2,128]{3,2,1,0:T(2,128)(2,1)S(1)} copy-done((bf16[4,4096,2,128]{3,2,1,0:T(2,128)(2,1)S(1)}, bf16[4,4096,2,128]{3,2,1,0:T(2,128)(2,1)}, u32[]{:S(2)}) %copy-start) | copy-done | bytes 8388632
  3.4 7.3 %slot_gather.2 = bf16[128,16,4,2,128]{4,3,2,1,0:T(2,128)(2,1)} custom-call(s32[4096]{0:T(1024)} %order_ref.3, bf16[4,4096,2,128]{3,2,1,0:T(2,128)(2,1)S(1)} %copy-done, s32[4096]{0:T(1024)} %_.7), custom_call_target="tpu_custom_call" | custom-call | bytes 8388608 | tf_op jit(solution)/shard_map/slot_gather/pallas_call | solution.py:63
  10.7 10.6 %all-to-all-start = ((bf16[128,128,128]{2,1,0:T(8,128)(2,1)}), bf16[128,128,128]{2,1,0:T(8,128)(2,1)}, u32[]{:S(2)}, u32[]{:S(2)}) async-start(bf16[128,128,128]{2,1,0:T(8,128)(2,1)} %bitcast.21), calls=%async_computation | async-start | bytes 8388608 | tf_op jit(solution)/shard_map/all_to_all | solution.py:349
  21.3 0.0 copy-start.1
  21.3 3.4 %copy-done.1 = bf16[4,4096,2,128]{3,2,1,0:T(2,128)(2,1)S(1)} copy-done((bf16[4,4096,2,128]{3,2,1,0:T(2,128)(2,1)S(1)}, bf16[4,4096,2,128]{3,2,1,0:T(2,128)(2,1)}, u32[]{:S(2)}) %copy-start.1) | copy-done | bytes 8388632
  24.7 7.5 %slot_gather.3 = bf16[128,16,4,2,128]{4,3,2,1,0:T(2,128)(2,1)} custom-call(s32[4096]{0:T(1024)} %order_ref.3, bf16[4,4096,2,128]{3,2,1,0:T(2,128)(2,1)S(1)} %copy-done.1, s32[4096]{0:T(1024)} %_.7), custom_call_target="tpu_custom_call" | custom-call | bytes 8388608 | tf_op jit(solution)/shard_map/slot_gather/pallas_call | solution.py:63
  32.1 37.5 %all-to-all-done = bf16[128,128,128]{2,1,0:T(8,128)(2,1)} async-done(((bf16[128,128,128]{2,1,0:T(8,128)(2,1)}), bf16[128,128,128]{2,1,0:T(8,128)(2,1)}, u32[]{:S(2)}, u32[]{:S(2)}) %all-to-all-start) | async-done | bytes 4194336 | tf_op jit(solution)/shard_map/all_to_all | solution.py:349
  69.6 10.0 %all-to-all-start.1 = ((bf16[128,128,128]{2,1,0:T(8,128)(2,1)}), bf16[128,128,128]{2,1,0:T(8,128)(2,1)}, u32[]{:S(2)}, u32[]{:S(2)}) async-start(bf16[128,128,128]{2,1,0:T(8,128)(2,1)} %bitcast.20), calls=%async_computation.1 | async-start | bytes 8388608 | tf_op jit(solution)/shard_map/all_to_all | solution.py:349
  79.6 0.7 multiply_reduce_fusion
  80.9 0.1 fusion.23
  81.0 16.5 %fusion.5.table_ref = bf16[1024,1024]{1,0:T(8,128)(2,1)} fusion(s32[1024]{0:T(1024)S(1)} %get-tuple-element.13, s32[1024]{0:T(1024)S(1)} %get-tuple-element.14, f32[1024]{0:T(1024)S(1)} %fusion.23), kind=kLoop, calls=%fused_computation.8 | loop fusion | flops 17825792 | bytes 2109440 | tf_op jit(solution)/shard_map/convert_element_type | solution.py:41
  97.5 5.9 %delay_spectra.4.head = bf16[2,4,8,128,128]{4,3,2,1,0:T(8,128)(2,1)} custom-call(bf16[16,8,128,128]{3,2,1,0:T(8,128)(2,1)} %bitcast.1.received_ref, bf16[1024,1024]{1,0:T(8,128)(2,1)} %fusion.5.table_ref, s32[4096]{0:T(1024)} %_.7), custom_call_target="tpu_custom_call" | custom-call | flops 2147483648 | bytes 8388608 | tf_op jit(solution)/shard_map/delay_spectra/pallas_call | solution.py:125
  103.4 0.0 copy-start.2
  103.5 0.0 copy-start.3
  103.5 6.0 %delay_spectra.3.tail = bf16[2,4,8,128,128]{4,3,2,1,0:T(8,128)(2,1)} custom-call(bf16[16,8,128,128]{3,2,1,0:T(8,128)(2,1)} %bitcast.1.received_ref, bf16[1024,1024]{1,0:T(8,128)(2,1)} %fusion.5.table_ref, s32[4096]{0:T(1024)} %_.7), custom_call_target="tpu_custom_call" | custom-call | flops 2147483648 | bytes 8388608 | tf_op jit(solution)/shard_map/delay_spectra/pallas_call | solution.py:125
  109.5 2.0 %collective-permute-start = (bf16[2,4,8,128,128]{4,3,2,1,0:T(8,128)(2,1)}, bf16[2,4,8,128,128]{4,3,2,1,0:T(8,128)(2,1)S(1)}, u32[]{:S(2)}, u32[]{:S(2)}) collective-permute-start(bf16[2,4,8,128,128]{4,3,2,1,0:T(8,128)(2,1)} %delay_spectra.3.tail), channel_id=1, source_target_pairs={{0,1},{1,2},{2,3},{3,4},{4,5},{5,6},{6,7},{7,8},{8,9},{9,10},{10,1... | collective-permute-start | bytes 6291464 | tf_op jit(solution)/shard_map/ppermute | solution.py:358
  111.5 3.5 %collective-permute-start.1 = (bf16[2,4,8,128,128]{4,3,2,1,0:T(8,128)(2,1)}, bf16[2,4,8,128,128]{4,3,2,1,0:T(8,128)(2,1)}, u32[]{:S(2)}, u32[]{:S(2)}) collective-permute-start(bf16[2,4,8,128,128]{4,3,2,1,0:T(8,128)(2,1)} %delay_spectra.4.head), channel_id=1, source_target_pairs={{1,0},{2,1},{3,2},{4,3},{5,4},{6,5},{7,6},{8,7},{9,8},{10,9},{11,1... | collective-permute-start | bytes 6291464 | tf_op jit(solution)/shard_map/ppermute | solution.py:357
  115.0 0.0 copy-done.2
  115.0 0.1 pad_dynamic-slice_fusion.1
  115.1 0.1 compare_bitcast_fusion
  115.2 0.0 copy-done.3
  115.2 0.1 and_convert_fusion
  115.3 0.1 copy.5
  115.4 5.2 %outer_pairs.1._.outer_ref = f32[8,16,8,128]{3,2,1,0:T(8,128)} custom-call(bf16[2,4,8,128,128]{4,3,2,1,0:T(8,128)(2,1)} %delay_spectra.4.head, bf16[2,4,8,128,128]{4,3,2,1,0:T(8,128)(2,1)} %delay_spectra.3.tail), custom_call_target="tpu_custom_call" | custom-call | flops 14680064 | bytes 4194304 | tf_op jit(solution)/shard_map/outer_pairs/pallas_call | solution.py:246
  120.6 29.7 %all-to-all-done.1 = bf16[128,128,128]{2,1,0:T(8,128)(2,1)} async-done(((bf16[128,128,128]{2,1,0:T(8,128)(2,1)}), bf16[128,128,128]{2,1,0:T(8,128)(2,1)}, u32[]{:S(2)}, u32[]{:S(2)}) %all-to-all-start.1) | async-done | bytes 4194336 | tf_op jit(solution)/shard_map/all_to_all | solution.py:349
  150.3 8.4 %delay_spectra.5.inner = bf16[2,4,16,128,128]{4,3,2,1,0:T(8,128)(2,1)} custom-call(bf16[16,8,128,128]{3,2,1,0:T(8,128)(2,1)} %bitcast.3.received_ref, bf16[1024,1024]{1,0:T(8,128)(2,1)} %fusion.5.table_ref, f32[8,16,8,128]{3,2,1,0:T(8,128)} %outer_pairs.1._.outer_ref), custom_call_target="tpu_custom_call" | custom-call | flops 4294967296 | bytes 16777216 | tf_op jit(solution)/shard_map/delay_spectra/pallas_call | solution.py:125
  158.7 9.0 %inner_pairs.1.inner_ref = f32[8,24,8,128]{3,2,1,0:T(8,128)} custom-call(bf16[2,4,8,128,128]{4,3,2,1,0:T(8,128)(2,1)} %delay_spectra.4.head, bf16[2,4,16,128,128]{4,3,2,1,0:T(8,128)(2,1)} %delay_spectra.5.inner, bf16[2,4,8,128,128]{4,3,2,1,0:T(8,128)(2,1)} %delay_spectra.3.tail), custom_call_target="tpu_custom_call" | custom-call | flops 42991616 | bytes 8388608 | tf_op jit(solution)/shard_map/inner_pairs/pallas_call | solution.py:246
  167.7 0.0 collective-permute-done.before
  167.7 0.0 collective-permute-done.1.after
  167.7 0.1 broadcast_in_dim.22.valid_ref
  167.8 7.2 %pair_power.1 = f32[32,16,1024]{2,1,0:T(8,128)} custom-call(bf16[2,4,8,128,128]{4,3,2,1,0:T(8,128)(2,1)S(1)} %collective-permute-done.before, bf16[2,4,8,128,128]{4,3,2,1,0:T(8,128)(2,1)} %delay_spectra.4.head, bf16[2,4,8,128,128]{4,3,2,1,0:T(8,128)(2,1)} %delay_spectra.3.tail, bf16[2,4,8,128,128]{4,3,2,1,0:T(8,128)(2,1)} %collective-permute-done.1.after, ...), custom_call_target="tpu_custom_call" | custom-call | flops 18874368 | bytes 8388608 | tf_op jit(solution)/shard_map/pair_power/pallas_call | solution.py:246
  (2 shorter events, 0.0 us)
Async XLA Ops:
  0.0 3.4 %copy-start = (bf16[4,4096,2,128]{3,2,1,0:T(2,128)(2,1)S(1)}, bf16[4,4096,2,128]{3,2,1,0:T(2,128)(2,1)}, u32[]{:S(2)}) copy-start(bf16[4,4096,2,128]{3,2,1,0:T(2,128)(2,1)} %vis_ref.3) | copy-start | bytes 25165828
  10.7 58.9 %all-to-all-start = ((bf16[128,128,128]{2,1,0:T(8,128)(2,1)}), bf16[128,128,128]{2,1,0:T(8,128)(2,1)}, u32[]{:S(2)}, u32[]{:S(2)}) async-start(bf16[128,128,128]{2,1,0:T(8,128)(2,1)} %bitcast.21), calls=%async_computation | async-start | bytes 8388608 | tf_op jit(solution)/shard_map/all_to_all | solution.py:349
  21.3 3.4 %copy-start.1 = (bf16[4,4096,2,128]{3,2,1,0:T(2,128)(2,1)S(1)}, bf16[4,4096,2,128]{3,2,1,0:T(2,128)(2,1)}, u32[]{:S(2)}) copy-start(bf16[4,4096,2,128]{3,2,1,0:T(2,128)(2,1)} %vis_ref.3) | copy-start | bytes 25165828
  69.6 80.7 %all-to-all-start.1 = ((bf16[128,128,128]{2,1,0:T(8,128)(2,1)}), bf16[128,128,128]{2,1,0:T(8,128)(2,1)}, u32[]{:S(2)}, u32[]{:S(2)}) async-start(bf16[128,128,128]{2,1,0:T(8,128)(2,1)} %bitcast.20), calls=%async_computation.1 | async-start | bytes 8388608 | tf_op jit(solution)/shard_map/all_to_all | solution.py:349
  103.4 11.6 %copy-start.2 = (s32[4096]{0:T(1024)S(1)}, s32[4096]{0:T(1024)}, u32[]{:S(2)}) copy-start(s32[4096]{0:T(1024)} %_.7) | copy-start | bytes 49156
  103.5 11.8 %copy-start.3 = (s32[4096,8]{0,1:T(8,128)S(1)}, s32[4096,8]{0,1:T(8,128)}, u32[]{:S(2)}) copy-start(s32[4096,8]{0,1:T(8,128)} %param.7) | copy-start | bytes 393220
  109.5 58.2 %collective-permute-start = (bf16[2,4,8,128,128]{4,3,2,1,0:T(8,128)(2,1)}, bf16[2,4,8,128,128]{4,3,2,1,0:T(8,128)(2,1)S(1)}, u32[]{:S(2)}, u32[]{:S(2)}) collective-permute-start(bf16[2,4,8,128,128]{4,3,2,1,0:T(8,128)(2,1)} %delay_spectra.3.tail), channel_id=1, source_target_pairs={{0,1},{1,2},{2,3},{3,4},{4,5},{5,6},{6,7},{7,8},{8,9},{9,10},{10,1... | collective-permute-start | bytes 6291464 | tf_op jit(solution)/shard_map/ppermute | solution.py:358
  111.5 56.2 %collective-permute-start.1 = (bf16[2,4,8,128,128]{4,3,2,1,0:T(8,128)(2,1)}, bf16[2,4,8,128,128]{4,3,2,1,0:T(8,128)(2,1)}, u32[]{:S(2)}, u32[]{:S(2)}) collective-permute-start(bf16[2,4,8,128,128]{4,3,2,1,0:T(8,128)(2,1)} %delay_spectra.4.head), channel_id=1, source_target_pairs={{1,0},{2,1},{3,2},{4,3},{5,4},{6,5},{7,6},{8,7},{9,8},{10,9},{11,1... | collective-permute-start | bytes 6291464 | tf_op jit(solution)/shard_map/ppermute | solution.py:357

commit v8 on v7

--- a/solution.py
+++ b/solution.py
@@ -41,45 +41,74 @@
     return (weights_norm[:, None] * jnp.cos(phase_angle)).astype(jnp.bfloat16)
 
 
-def gather_kernel(slots, per, order_ref, vis_ref, _, out_ref):
-    owners, count = out_ref.shape[0], out_ref.shape[2]
-    first = pl.program_id(0) * owners
-
-    def one_owner(owner, carry):
-        base = (first + owner) * per
-        for j, slot in enumerate(slots):
-            source = order_ref[base + slot]
-            for t in range(count):
-                out_ref[owner, j, t] = vis_ref[t, source]
-        return carry
-
-    lax.fori_loop(0, owners, one_owner, 0)
+def gather_kernel(slots, per, order_ref, vis_ref, _, out_ref, vis, rows, load_sems, store_sems):
+    count = vis.shape[0]
+    half = count // 2
+    loads = [
+        pltpu.make_async_copy(
+            vis_ref.at[pl.ds(h * half, half)], vis.at[pl.ds(h * half, half)], load_sems.at[h]
+        )
+        for h in range(2)
+    ]
+    for load in loads:
+        load.start()
+    n_dev = out_ref.shape[0]
+    groups = store_sems.shape[0]
+    owners = n_dev // groups
+
+    def sort_half(h, first, number):
+        def one_owner(i, carry):
+            owner = first + i
+            base = owner * per
+            for j, slot in enumerate(slots):
+                source = order_ref[base + slot]
+                for t in range(h * half, (h + 1) * half):
+                    rows[owner, j, t] = vis[t, source]
+            return carry
+
+        lax.fori_loop(0, number, one_owner, 0)
+
+    loads[0].wait()
+    sort_half(0, 0, n_dev)
+    loads[1].wait()
+    stores = []
+    for g in range(groups):
+        sort_half(1, g * owners, owners)
+        span = pl.ds(g * owners, owners)
+        store = pltpu.make_async_copy(rows.at[span], out_ref.at[span], store_sems.at[g])
+        store.start()
+        stores.append(store)
+    for store in stores:
+        store.wait()
 
 
 def gather(visibilities, order, slots, n_dev, earlier):
     count, n_base = visibilities.shape[:2]
     tail = visibilities.shape[2:]
-    steps = 8
+    groups = 8
+    shape = (n_dev, len(slots), count) + tail
+    anywhere = pl.BlockSpec(memory_space=pl.ANY)
     return pl.pallas_call(
         functools.partial(gather_kernel, slots, n_base // n_dev),
         grid_spec=pltpu.PrefetchScalarGridSpec(
             num_scalar_prefetch=1,
-            grid=(steps,),
-            in_specs=[
-                pl.BlockSpec(memory_space=pltpu.VMEM),
-                pl.BlockSpec(memory_space=pl.ANY),
+            grid=(),
+            in_specs=[anywhere] * 2,
+            out_specs=anywhere,
+            scratch_shapes=[
+                pltpu.VMEM(visibilities.shape, visibilities.dtype),
+                pltpu.VMEM(shape, visibilities.dtype),
+                pltpu.SemaphoreType.DMA((2,)),
+                pltpu.SemaphoreType.DMA((groups,)),
             ],
-            out_specs=pl.BlockSpec(
-                (n_dev // steps, len(slots), count) + tail, lambda i, o: (i, 0, 0, 0, 0)
-            ),
         ),
-        out_shape=pltpu.HBM((n_dev, len(slots), count) + tail, visibilities.dtype),
+        out_shape=pltpu.HBM(shape, visibilities.dtype),
         compiler_params=pltpu.CompilerParams(vmem_limit_bytes=24 * MIB),
         cost_estimate=pl.CostEstimate(
             flops=0, bytes_accessed=2 * count * n_dev * len(slots) * 512, transcendentals=0
         ),
         name="slot_gather",
-    )(in_hbm(order), visibilities, in_hbm(earlier))
+    )(in_hbm(order), in_hbm(visibilities), in_hbm(earlier))
 
 
 def spectra_kernel(received_ref, table_ref, _, out_ref):
@@ -321,6 +350,22 @@
     )
 
 
+def after_those(arrays, *earlier):
+    def kernel(*refs):
+        pass
+
+    count = len(arrays)
+    anywhere = pl.BlockSpec(memory_space=pl.ANY)
+    return pl.pallas_call(
+        kernel,
+        in_specs=[anywhere] * (count + len(earlier)),
+        out_specs=[anywhere] * count,
+        out_shape=[pltpu.HBM(array.shape, array.dtype) for array in arrays],
+        input_output_aliases={i: i for i in range(count)},
+        name="in_order",
+    )(*[in_hbm(array) for array in arrays], *earlier)
+
+
 def body(visibilities, owner_order, group_ids, partner_flags):
     n_tm = lax.axis_size("tm")
     n_chan = lax.axis_size("chan")
@@ -354,12 +399,13 @@
     received_inner = exchange(INNER, group_ids)
     head = spectra(received_outer, table, n_tm, n_chan, 0, REACH, group_ids)
     tail = spectra(received_outer, table, n_tm, n_chan, REACH, REACH, group_ids)
-    after = lax.ppermute(head, AXES, down)
-    before = lax.ppermute(tail, AXES, up)
     outer_sums = outer_powers(head, tail)
+    head_sent, tail_sent = after_those((head, tail), in_hbm(outer_sums))
+    after = lax.ppermute(head_sent, AXES, down)
+    before = lax.ppermute(tail_sent, AXES, up)
     inner = spectra(received_inner, table, n_tm, n_chan, 0, 2 * REACH, outer_sums)
-    inner_sums = inner_powers(head, inner, tail)
-    return final_powers(before, head, tail, after, outer_sums, inner_sums, valid)
+    inner_sums = inner_powers(head_sent, inner, tail_sent)
+    return final_powers(before, head_sent, tail_sent, after, outer_sums, inner_sums, valid)
 
 
 def solution(mesh):

time: 176 us -> 159 us (0.903)
  the two profiles are of different devices: /device:TPU:46 before, /device:TPU:32 now
where the time goes in v8:
time: 159 us; the launch traced here: 158 us
  Pallas kernels  61.2 us (38%)
  waiting for transfers between devices  51.3 us (32%)
  starting transfers between devices  27 us (17%)
  other arithmetic  17.4 us (11%)
    all_to_all x2, waiting for transfers between devices, exchange(): return lax.all_to_all(send, AXES, 0, 0, tiled=True)  49 us
    pallas_call x3, Pallas kernels, cross_call(): pl.pallas_call(kernel, grid=(2, CHUNKS // STEP), in_specs=specs, out_spec...  21.5 us
    pallas_call x3, Pallas kernels, spectra(): pl.pallas_call(spectra_kernel, grid=(slots // step,), in_specs=[pl.BlockS...  20.3 us
    pallas_call x2, Pallas kernels, gather(): pl.pallas_call(functools.partial(gather_kernel, slots, n_base // n_dev),...  19.5 us
    all_to_all x2, starting transfers between devices, exchange(): return lax.all_to_all(send, AXES, 0, 0, tiled=True)  17.2 us
    convert_element_type x1, other arithmetic, half_table(): return (weights_norm[:, None] * jnp.cos(phase_angle)).astype(jnp.bfloat16)  16.5 us
    ppermute x1, starting transfers between devices, body(): after = lax.ppermute(head_sent, AXES, down)  7.73 us
  transfers between devices with their start and end apart: 4, of which 3 were waited for; matrix products, arithmetic and copies ran while one was open for 11% of the time, Pallas kernels for 28%

profile of v8, /device:TPU:32, one launch (start us, length us, event | category | flops | bytes accessed | tf_op | source)
XLA Modules:
  0.0 158.1 jit_solution(11631652648873736645)
XLA Ops:
  0.0 9.6 %slot_gather.2 = bf16[128,16,4,2,128]{4,3,2,1,0:T(2,128)(2,1)} custom-call(s32[4096]{0:T(1024)} %order_ref.3, bf16[4,4096,2,128]{3,2,1,0:T(2,128)(2,1)} %vis_ref.3, s32[4096]{0:T(1024)} %_.7), custom_call_target="tpu_custom_call" | custom-call | bytes 8388608 | tf_op jit(solution)/shard_map/slot_gather/pallas_call | solution.py:91
  9.6 10.7 %all-to-all-start = ((bf16[128,128,128]{2,1,0:T(8,128)(2,1)}), bf16[128,128,128]{2,1,0:T(8,128)(2,1)}, u32[]{:S(2)}, u32[]{:S(2)}) async-start(bf16[128,128,128]{2,1,0:T(8,128)(2,1)} %bitcast.21), calls=%async_computation | async-start | bytes 8388608 | tf_op jit(solution)/shard_map/all_to_all | solution.py:394
  20.3 9.8 %slot_gather.3 = bf16[128,16,4,2,128]{4,3,2,1,0:T(2,128)(2,1)} custom-call(s32[4096]{0:T(1024)} %order_ref.3, bf16[4,4096,2,128]{3,2,1,0:T(2,128)(2,1)} %vis_ref.3, s32[4096]{0:T(1024)} %_.7), custom_call_target="tpu_custom_call" | custom-call | bytes 8388608 | tf_op jit(solution)/shard_map/slot_gather/pallas_call | solution.py:91
  30.2 41.9 %all-to-all-done = bf16[128,128,128]{2,1,0:T(8,128)(2,1)} async-done(((bf16[128,128,128]{2,1,0:T(8,128)(2,1)}), bf16[128,128,128]{2,1,0:T(8,128)(2,1)}, u32[]{:S(2)}, u32[]{:S(2)}) %all-to-all-start) | async-done | bytes 4194336 | tf_op jit(solution)/shard_map/all_to_all | solution.py:394
  72.1 6.5 %all-to-all-start.1 = ((bf16[128,128,128]{2,1,0:T(8,128)(2,1)}), bf16[128,128,128]{2,1,0:T(8,128)(2,1)}, u32[]{:S(2)}, u32[]{:S(2)}) async-start(bf16[128,128,128]{2,1,0:T(8,128)(2,1)} %bitcast.20), calls=%async_computation.1 | async-start | bytes 8388608 | tf_op jit(solution)/shard_map/all_to_all | solution.py:394
  78.6 0.7 multiply_reduce_fusion
  80.0 0.1 fusion.23
  80.0 16.5 %fusion.5.table_ref = bf16[1024,1024]{1,0:T(8,128)(2,1)} fusion(s32[1024]{0:T(1024)S(1)} %get-tuple-element.17, s32[1024]{0:T(1024)S(1)} %get-tuple-element.18, f32[1024]{0:T(1024)S(1)} %fusion.23), kind=kLoop, calls=%fused_computation.8 | loop fusion | flops 17825792 | bytes 2109440 | tf_op jit(solution)/shard_map/convert_element_type | solution.py:41
  96.6 5.9 %delay_spectra.4.tail.refs_1_ = bf16[2,4,8,128,128]{4,3,2,1,0:T(8,128)(2,1)} custom-call(bf16[16,8,128,128]{3,2,1,0:T(8,128)(2,1)} %bitcast.1.received_ref, bf16[1024,1024]{1,0:T(8,128)(2,1)} %fusion.5.table_ref, s32[4096]{0:T(1024)} %_.7), custom_call_target="tpu_custom_call" | custom-call | flops 2147483648 | bytes 8388608 | tf_op jit(solution)/shard_map/delay_spectra/pallas_call | solution.py:154
  102.5 6.0 %delay_spectra.3.head.refs_0_ = bf16[2,4,8,128,128]{4,3,2,1,0:T(8,128)(2,1)} custom-call(bf16[16,8,128,128]{3,2,1,0:T(8,128)(2,1)} %bitcast.1.received_ref, bf16[1024,1024]{1,0:T(8,128)(2,1)} %fusion.5.table_ref, s32[4096]{0:T(1024)} %_.7), custom_call_target="tpu_custom_call" | custom-call | flops 2147483648 | bytes 8388608 | tf_op jit(solution)/shard_map/delay_spectra/pallas_call | solution.py:154
  108.5 0.0 copy-start
  108.5 0.0 copy-start.1
  108.5 5.3 %outer_pairs.1.refs_2_._.outer_ref = f32[8,16,8,128]{3,2,1,0:T(8,128)} custom-call(bf16[2,4,8,128,128]{4,3,2,1,0:T(8,128)(2,1)} %delay_spectra.3.head.refs_0_, bf16[2,4,8,128,128]{4,3,2,1,0:T(8,128)(2,1)} %delay_spectra.4.tail.refs_1_), custom_call_target="tpu_custom_call" | custom-call | flops 14680064 | bytes 4194304 | tf_op jit(solution)/shard_map/outer_pairs/pallas_call | solution.py:275
  113.7 2.0 %collective-permute-start = (bf16[2,4,8,128,128]{4,3,2,1,0:T(8,128)(2,1)}, bf16[2,4,8,128,128]{4,3,2,1,0:T(8,128)(2,1)S(1)}, u32[]{:S(2)}, u32[]{:S(2)}) collective-permute-start(bf16[2,4,8,128,128]{4,3,2,1,0:T(8,128)(2,1)} %get-tuple-element.7.tail), channel_id=1, source_target_pairs={{0,1},{1,2},{2,3},{3,4},{4,5},{5,6},{6,7},{7,8},{8,9},{9,10},{10,1... | collective-permute-start | bytes 6291464 | tf_op jit(solution)/shard_map/ppermute | solution.py:405
  115.8 7.7 %collective-permute-start.1 = (bf16[2,4,8,128,128]{4,3,2,1,0:T(8,128)(2,1)}, bf16[2,4,8,128,128]{4,3,2,1,0:T(8,128)(2,1)}, u32[]{:S(2)}, u32[]{:S(2)}) collective-permute-start(bf16[2,4,8,128,128]{4,3,2,1,0:T(8,128)(2,1)} %get-tuple-element.8.head), channel_id=1, source_target_pairs={{1,0},{2,1},{3,2},{4,3},{5,4},{6,5},{7,6},{8,7},{9,8},{10,9},{11,1... | collective-permute-start | bytes 6291464 | tf_op jit(solution)/shard_map/ppermute | solution.py:404
  123.5 0.0 copy-done
  123.5 0.1 pad_dynamic-slice_fusion.1
  123.6 0.1 compare_bitcast_fusion
  123.7 0.0 copy-done.1
  123.8 0.1 and_convert_fusion
  123.8 0.1 copy.7
  123.9 7.1 %all-to-all-done.1 = bf16[128,128,128]{2,1,0:T(8,128)(2,1)} async-done(((bf16[128,128,128]{2,1,0:T(8,128)(2,1)}), bf16[128,128,128]{2,1,0:T(8,128)(2,1)}, u32[]{:S(2)}, u32[]{:S(2)}) %all-to-all-start.1) | async-done | bytes 4194336 | tf_op jit(solution)/shard_map/all_to_all | solution.py:394
  131.0 8.4 %delay_spectra.5.inner = bf16[2,4,16,128,128]{4,3,2,1,0:T(8,128)(2,1)} custom-call(bf16[16,8,128,128]{3,2,1,0:T(8,128)(2,1)} %bitcast.3.received_ref, bf16[1024,1024]{1,0:T(8,128)(2,1)} %fusion.5.table_ref, f32[8,16,8,128]{3,2,1,0:T(8,128)} %outer_pairs.1.refs_2_._.outer_ref), custom_call_target="tpu_custom_call" | custom-call | flops 4294967296 | bytes 16777216 | tf_op jit(solution)/shard_map/delay_spectra/pallas_call | solution.py:154
  139.4 9.0 %inner_pairs.1.inner_ref = f32[8,24,8,128]{3,2,1,0:T(8,128)} custom-call(bf16[2,4,8,128,128]{4,3,2,1,0:T(8,128)(2,1)} %get-tuple-element.8.head, bf16[2,4,16,128,128]{4,3,2,1,0:T(8,128)(2,1)} %delay_spectra.5.inner, bf16[2,4,8,128,128]{4,3,2,1,0:T(8,128)(2,1)} %get-tuple-element.7.tail), custom_call_target="tpu_custom_call" | custom-call | flops 42991616 | bytes 8388608 | tf_op jit(solution)/shard_map/inner_pairs/pallas_call | solution.py:275
  148.4 2.4 %collective-permute-done.before = bf16[2,4,8,128,128]{4,3,2,1,0:T(8,128)(2,1)S(1)} collective-permute-done((bf16[2,4,8,128,128]{4,3,2,1,0:T(8,128)(2,1)}, bf16[2,4,8,128,128]{4,3,2,1,0:T(8,128)(2,1)S(1)}, u32[]{:S(2)}, u32[]{:S(2)}) %collective-permute-start) | collective-permute-done | bytes 2097184 | tf_op jit(solution)/shard_map/ppermute | solution.py:405
  150.8 0.0 collective-permute-done.1.after
  150.8 0.1 broadcast_in_dim.22.valid_ref
  150.9 7.2 %pair_power.1 = f32[32,16,1024]{2,1,0:T(8,128)} custom-call(bf16[2,4,8,128,128]{4,3,2,1,0:T(8,128)(2,1)S(1)} %collective-permute-done.before, bf16[2,4,8,128,128]{4,3,2,1,0:T(8,128)(2,1)} %get-tuple-element.8.head, bf16[2,4,8,128,128]{4,3,2,1,0:T(8,128)(2,1)} %get-tuple-element.7.tail, bf16[2,4,8,128,128]{4,3,2,1,0:T(8,128)(2,1)} %collective-permute-done.1.after, ...), custom_call_target="tpu_custom_call" | custom-call | flops 18874368 | bytes 8388608 | tf_op jit(solution)/shard_map/pair_power/pallas_call | solution.py:275
  (3 shorter events, 0.0 us)
Async XLA Ops:
  9.6 62.4 %all-to-all-start = ((bf16[128,128,128]{2,1,0:T(8,128)(2,1)}), bf16[128,128,128]{2,1,0:T(8,128)(2,1)}, u32[]{:S(2)}, u32[]{:S(2)}) async-start(bf16[128,128,128]{2,1,0:T(8,128)(2,1)} %bitcast.21), calls=%async_computation | async-start | bytes 8388608 | tf_op jit(solution)/shard_map/all_to_all | solution.py:394
  72.1 59.0 %all-to-all-start.1 = ((bf16[128,128,128]{2,1,0:T(8,128)(2,1)}), bf16[128,128,128]{2,1,0:T(8,128)(2,1)}, u32[]{:S(2)}, u32[]{:S(2)}) async-start(bf16[128,128,128]{2,1,0:T(8,128)(2,1)} %bitcast.20), calls=%async_computation.1 | async-start | bytes 8388608 | tf_op jit(solution)/shard_map/all_to_all | solution.py:394
  108.5 15.1 %copy-start = (s32[4096]{0:T(1024)S(1)}, s32[4096]{0:T(1024)}, u32[]{:S(2)}) copy-start(s32[4096]{0:T(1024)} %_.7) | copy-start | bytes 49156
  108.5 15.3 %copy-start.1 = (s32[4096,8]{0,1:T(8,128)S(1)}, s32[4096,8]{0,1:T(8,128)}, u32[]{:S(2)}) copy-start(s32[4096,8]{0,1:T(8,128)} %param.7) | copy-start | bytes 393220
  113.7 37.0 %collective-permute-start = (bf16[2,4,8,128,128]{4,3,2,1,0:T(8,128)(2,1)}, bf16[2,4,8,128,128]{4,3,2,1,0:T(8,128)(2,1)S(1)}, u32[]{:S(2)}, u32[]{:S(2)}) collective-permute-start(bf16[2,4,8,128,128]{4,3,2,1,0:T(8,128)(2,1)} %get-tuple-element.7.tail), channel_id=1, source_target_pairs={{0,1},{1,2},{2,3},{3,4},{4,5},{5,6},{6,7},{7,8},{8,9},{9,10},{10,1... | collective-permute-start | bytes 6291464 | tf_op jit(solution)/shard_map/ppermute | solution.py:405
  115.8 35.0 %collective-permute-start.1 = (bf16[2,4,8,128,128]{4,3,2,1,0:T(8,128)(2,1)}, bf16[2,4,8,128,128]{4,3,2,1,0:T(8,128)(2,1)}, u32[]{:S(2)}, u32[]{:S(2)}) collective-permute-start(bf16[2,4,8,128,128]{4,3,2,1,0:T(8,128)(2,1)} %get-tuple-element.8.head), channel_id=1, source_target_pairs={{1,0},{2,1},{3,2},{4,3},{5,4},{6,5},{7,6},{8,7},{9,8},{10,9},{11,1... | collective-permute-start | bytes 6291464 | tf_op jit(solution)/shard_map/ppermute | solution.py:404

commit v9 on v8

--- a/solution.py
+++ b/solution.py
@@ -158,11 +158,11 @@
             pl.BlockSpec(
                 (n_tm, n_chan, 8 * step, lanes), lambda t: (0, 0, first // step + t, 0)
             ),
-            pl.BlockSpec(table.shape, lambda t: (0, 0), pipeline_mode=pl.Buffered(1)),
+            pl.BlockSpec(memory_space=pltpu.VMEM),
             pl.BlockSpec(memory_space=pl.ANY),
         ],
         out_specs=pl.BlockSpec((2, chunks, step, rows, LANES), lambda t: (0, 0, t, 0, 0)),
-        out_shape=pltpu.HBM((2, chunks, slots, rows, LANES), jnp.bfloat16),
+        out_shape=jax.ShapeDtypeStruct((2, chunks, slots, rows, LANES), jnp.bfloat16),
         compiler_params=pltpu.CompilerParams(vmem_limit_bytes=32 * MIB),
         cost_estimate=pl.CostEstimate(
             flops=16 * slots * n_tm * width * width,
@@ -170,7 +170,7 @@
             transcendentals=0,
         ),
         name="delay_spectra",
-    )(in_hbm(received.reshape(n_tm, n_chan, pairs, lanes)), in_hbm(table), in_hbm(earlier))
+    )(in_hbm(received.reshape(n_tm, n_chan, pairs, lanes)), table, earlier)
 
 
 def fold_rows(sums):
@@ -207,9 +207,11 @@
 
 
 def outer_kernel(head, tail, out_ref, rows_ref):
+    sign, first_chunk = pl.program_id(0), pl.program_id(1) * STEP
+
     def one_chunk(c, carry):
-        load_rows(rows_ref, 0, head.at[0, c])
-        load_rows(rows_ref, REACH, tail.at[0, c])
+        load_rows(rows_ref, 0, head.at[sign, first_chunk + c])
+        load_rows(rows_ref, REACH, tail.at[sign, first_chunk + c])
         for first in (0, REACH):
             for j in range(REACH):
                 out_ref[c, first + j] = cross_tile(rows_ref, first + j, range(1, REACH - j))
@@ -219,10 +221,12 @@
 
 
 def inner_kernel(head, inner, tail, out_ref, rows_ref):
+    sign, first_chunk = pl.program_id(0), pl.program_id(1) * STEP
+
     def one_chunk(c, carry):
-        load_rows(rows_ref, 0, head.at[0, c])
-        load_rows(rows_ref, REACH, inner.at[0, c])
-        load_rows(rows_ref, 3 * REACH, tail.at[0, c])
+        load_rows(rows_ref, 0, head.at[sign, first_chunk + c])
+        load_rows(rows_ref, REACH, inner.at[sign, first_chunk + c])
+        load_rows(rows_ref, 3 * REACH, tail.at[sign, first_chunk + c])
         for s in range(3 * REACH):
             out_ref[c, s] = cross_tile(rows_ref, s, range(max(1, REACH - s), REACH + 1))
         return carry
@@ -238,11 +242,16 @@
     order = jnp.where(mirror, (LANES - lane) % LANES, lane)
     slots = out_ref.shape[0]
 
+    first_chunk = pl.program_id(1) * STEP
+    first_sums = pl.program_id(0) * CHUNKS + first_chunk
+
     def one_chunk(c, carry):
         at = jnp.where(mirror, STEP - 1 - c, c)
         lanes = pl.ds(pl.multiple_of(at * LANES, LANES), LANES)
-        for i, source in enumerate((before, head, tail, after)):
-            load_rows(rows_ref, i * REACH, source.at[0, c])
+        load_rows(rows_ref, 0, before.at[0, c])
+        load_rows(rows_ref, REACH, head.at[pl.program_id(0), first_chunk + c])
+        load_rows(rows_ref, 2 * REACH, tail.at[pl.program_id(0), first_chunk + c])
+        load_rows(rows_ref, 3 * REACH, after.at[0, c])
         powers = {}
         for s in range(-REACH, slots):
             terms = []
@@ -251,9 +260,9 @@
                 start = j if s < 0 else 2 * REACH + j
                 terms.append(cross_tile(rows_ref, start, range(REACH - j, REACH + 1)))
             if s in OUTER:
-                terms.append(outer_ref[c, OUTER.index(s)])
+                terms.append(outer_ref[first_sums + c, OUTER.index(s)])
             if 0 <= s < slots - REACH:
-                terms.append(inner_ref[c, s])
+                terms.append(inner_ref[first_sums + c, s])
             value = jnp.take_along_axis(sum(terms[1:], terms[0]), order, axis=1)
             powers[s] = jnp.where(valid_ref[s + REACH] > 0.0, value * (1.0 / 64.0), 0.0)
             if s >= 0:
@@ -289,8 +298,12 @@
     )(*operands)
 
 
-def spectra_spec(array):
+def chunks_spec(array):
     return pl.BlockSpec((1, STEP) + array.shape[2:], lambda i, j: (i, j, 0, 0, 0))
+
+
+def whole():
+    return pl.BlockSpec(memory_space=pltpu.VMEM)
 
 
 def sums_spec(slots):
@@ -304,10 +317,10 @@
     return cross_call(
         outer_kernel,
         "outer_pairs",
-        [in_hbm(head), in_hbm(tail)],
-        [spectra_spec(head)] * 2,
+        [head, tail],
+        [whole()] * 2,
         sums_spec(slots),
-        pltpu.HBM((2 * CHUNKS, slots, REACH, LANES), jnp.float32),
+        jax.ShapeDtypeStruct((2 * CHUNKS, slots, REACH, LANES), jnp.float32),
         slots,
         56,
     )
@@ -318,10 +331,10 @@
     return cross_call(
         inner_kernel,
         "inner_pairs",
-        [in_hbm(head), in_hbm(inner), in_hbm(tail)],
-        [spectra_spec(array) for array in (head, inner, tail)],
+        [head, inner, tail],
+        [whole()] * 3,
         sums_spec(slots),
-        pltpu.HBM((2 * CHUNKS, slots, REACH, LANES), jnp.float32),
+        jax.ShapeDtypeStruct((2 * CHUNKS, slots, REACH, LANES), jnp.float32),
         4 * REACH,
         164,
     )
@@ -329,17 +342,12 @@
 
 def final_powers(before, head, tail, after, outer_sums, inner_sums, valid):
     slots = 4 * REACH
-    spectra_specs = [spectra_spec(array) for array in (before, head, tail, after)]
+    operands = [before, head, tail, after, outer_sums, inner_sums, valid]
     return cross_call(
         final_kernel,
         "pair_power",
-        [before, in_hbm(head), in_hbm(tail), after, in_hbm(outer_sums), in_hbm(inner_sums), valid],
-        spectra_specs
-        + [
-            sums_spec(outer_sums.shape[1]),
-            sums_spec(inner_sums.shape[1]),
-            pl.BlockSpec(valid.shape, lambda i, j: (0, 0, 0)),
-        ],
+        operands,
+        [chunks_spec(before), whole(), whole(), chunks_spec(after), whole(), whole(), whole()],
         pl.BlockSpec(
             (slots, 2 * REACH, STEP * LANES),
             lambda i, j: (0, 0, jnp.where(i == 0, j, 2 * CHUNKS // STEP - 1 - j)),
@@ -360,10 +368,10 @@
         kernel,
         in_specs=[anywhere] * (count + len(earlier)),
         out_specs=[anywhere] * count,
-        out_shape=[pltpu.HBM(array.shape, array.dtype) for array in arrays],
+        out_shape=[jax.ShapeDtypeStruct(array.shape, array.dtype) for array in arrays],
         input_output_aliases={i: i for i in range(count)},
         name="in_order",
-    )(*[in_hbm(array) for array in arrays], *earlier)
+    )(*arrays, *earlier)
 
 
 def body(visibilities, owner_order, group_ids, partner_flags):
@@ -400,7 +408,7 @@
     head = spectra(received_outer, table, n_tm, n_chan, 0, REACH, group_ids)
     tail = spectra(received_outer, table, n_tm, n_chan, REACH, REACH, group_ids)
     outer_sums = outer_powers(head, tail)
-    head_sent, tail_sent = after_those((head, tail), in_hbm(outer_sums))
+    head_sent, tail_sent = after_those((head, tail), outer_sums, valid)
     after = lax.ppermute(head_sent, AXES, down)
     before = lax.ppermute(tail_sent, AXES, up)
     inner = spectra(received_inner, table, n_tm, n_chan, 0, 2 * REACH, outer_sums)

time: 159 us -> 170 us (1.069)
  the two profiles are of different devices: /device:TPU:32 before, /device:TPU:46 now
where the time goes in v9:
time: 170 us
  waiting for transfers between devices  71.9 us (42%)
  Pallas kernels  52.1 us (31%)
  starting transfers between devices  26.4 us (16%)
  other arithmetic  16.7 us (10%)
  local copies, waits for them, and re-layouts  1.8 us (1%)
    all_to_all x2, waiting for transfers between devices, exchange(): return lax.all_to_all(send, AXES, 0, 0, tiled=True)  71.9 us
    all_to_all x2, starting transfers between devices, exchange(): return lax.all_to_all(send, AXES, 0, 0, tiled=True)  20.7 us
    pallas_call x2, Pallas kernels, gather(): pl.pallas_call(functools.partial(gather_kernel, slots, n_base // n_dev),...  19.5 us
    pallas_call x3, Pallas kernels, spectra(): pl.pallas_call(spectra_kernel, grid=(slots // step,), in_specs=[pl.BlockS...  16.4 us
    pallas_call x3, Pallas kernels, cross_call(): pl.pallas_call(kernel, grid=(2, CHUNKS // STEP), in_specs=specs, out_spec...  16.2 us
    convert_element_type x1, other arithmetic, half_table(): return (weights_norm[:, None] * jnp.cos(phase_angle)).astype(jnp.bfloat16)  15.8 us
    ppermute x1, starting transfers between devices, body(): after = lax.ppermute(head_sent, AXES, down)  3.51 us
  transfers between devices with their start and end apart: 4, of which 2 were waited for; matrix products, arithmetic and copies ran while one was open for 10% of the time, Pallas kernels for 21%

profile of v9, /device:TPU:46, one launch (start us, length us, event | category | flops | bytes accessed | tf_op | source)
XLA Modules:
  0.0 169.8 jit_solution(2399306811804017164)
XLA Ops:
  0.0 9.6 %slot_gather.2 = bf16[128,16,4,2,128]{4,3,2,1,0:T(2,128)(2,1)} custom-call(s32[4096]{0:T(1024)} %order_ref.3, bf16[4,4096,2,128]{3,2,1,0:T(2,128)(2,1)} %vis_ref.3, s32[4096]{0:T(1024)} %_.7), custom_call_target="tpu_custom_call" | custom-call | bytes 8388608 | tf_op jit(solution)/shard_map/slot_gather/pallas_call | solution.py:91
  9.7 10.6 %all-to-all-start = ((bf16[128,128,128]{2,1,0:T(8,128)(2,1)}), bf16[128,128,128]{2,1,0:T(8,128)(2,1)}, u32[]{:S(2)}, u32[]{:S(2)}) async-start(bf16[128,128,128]{2,1,0:T(8,128)(2,1)} %bitcast.21), calls=%async_computation | async-start | bytes 8388608 | tf_op jit(solution)/shard_map/all_to_all | solution.py:402
  20.3 9.8 %slot_gather.3 = bf16[128,16,4,2,128]{4,3,2,1,0:T(2,128)(2,1)} custom-call(s32[4096]{0:T(1024)} %order_ref.3, bf16[4,4096,2,128]{3,2,1,0:T(2,128)(2,1)} %vis_ref.3, s32[4096]{0:T(1024)} %_.7), custom_call_target="tpu_custom_call" | custom-call | bytes 8388608 | tf_op jit(solution)/shard_map/slot_gather/pallas_call | solution.py:91
  30.1 38.5 %all-to-all-done = bf16[128,128,128]{2,1,0:T(8,128)(2,1)} async-done(((bf16[128,128,128]{2,1,0:T(8,128)(2,1)}), bf16[128,128,128]{2,1,0:T(8,128)(2,1)}, u32[]{:S(2)}, u32[]{:S(2)}) %all-to-all-start) | async-done | bytes 4194336 | tf_op jit(solution)/shard_map/all_to_all | solution.py:402
  68.6 0.0 copy-start.9
  68.6 0.0 copy-start.10
  68.6 10.1 %all-to-all-start.1 = ((bf16[128,128,128]{2,1,0:T(8,128)(2,1)}), bf16[128,128,128]{2,1,0:T(8,128)(2,1)}, u32[]{:S(2)}, u32[]{:S(2)}) async-start(bf16[128,128,128]{2,1,0:T(8,128)(2,1)} %bitcast.20), calls=%async_computation.1 | async-start | bytes 8388608 | tf_op jit(solution)/shard_map/all_to_all | solution.py:402
  78.7 0.7 multiply_reduce_fusion
  80.0 0.0 copy-done.9
  80.0 0.1 pad_dynamic-slice_fusion.1
  80.1 0.1 compare_bitcast_fusion
  80.3 0.0 copy-done.10
  80.3 0.1 and_convert_fusion
  80.3 0.1 copy.7
  80.4 0.1 fusion.23
  80.5 15.8 %fusion.5.table_ref = bf16[1024,1024]{1,0:T(8,128)(2,1)S(1)} fusion(s32[1024]{0:T(1024)S(1)} %get-tuple-element.17, s32[1024]{0:T(1024)S(1)} %get-tuple-element.18, f32[1024]{0:T(1024)S(1)} %fusion.23), kind=kLoop, calls=%fused_computation.8 | loop fusion | flops 17825792 | bytes 2109440 | tf_op jit(solution)/shard_map/convert_element_type | solution.py:41
  96.3 0.0 copy-start.4
  96.3 4.8 %delay_spectra.4.tail.refs_1_ = bf16[2,4,8,128,128]{4,3,2,1,0:T(8,128)(2,1)S(1)} custom-call(bf16[16,8,128,128]{3,2,1,0:T(8,128)(2,1)} %bitcast.1.received_ref, bf16[1024,1024]{1,0:T(8,128)(2,1)S(1)} %fusion.5.table_ref, s32[4096]{0:T(1024)S(1)} %copy-done.9), custom_call_target="tpu_custom_call" | custom-call | flops 2147483648 | bytes 8388608 | tf_op jit(solution)/shard_map/delay_spectra/pallas_call | solution.py:154
  101.1 0.0 copy-done.4
  101.1 0.0 copy-start
  101.1 4.8 %delay_spectra.3.head.refs_0_ = bf16[2,4,8,128,128]{4,3,2,1,0:T(8,128)(2,1)S(1)} custom-call(bf16[16,8,128,128]{3,2,1,0:T(8,128)(2,1)} %bitcast.1.received_ref, bf16[1024,1024]{1,0:T(8,128)(2,1)S(1)} %fusion.5.table_ref, s32[4096]{0:T(1024)S(1)} %copy-done.9), custom_call_target="tpu_custom_call" | custom-call | flops 2147483648 | bytes 8388608 | tf_op jit(solution)/shard_map/delay_spectra/pallas_call | solution.py:154
  105.9 0.0 copy-done
  105.9 0.0 copy-start.2
  105.9 2.7 %outer_pairs.1.refs_2_._.outer_ref = f32[8,16,8,128]{3,2,1,0:T(8,128)S(1)} custom-call(bf16[2,4,8,128,128]{4,3,2,1,0:T(8,128)(2,1)S(1)} %delay_spectra.3.head.refs_0_, bf16[2,4,8,128,128]{4,3,2,1,0:T(8,128)(2,1)S(1)} %delay_spectra.4.tail.refs_1_), custom_call_target="tpu_custom_call" | custom-call | flops 14680064 | bytes 4194304 | tf_op jit(solution)/shard_map/outer_pairs/pallas_call | solution.py:284
  108.7 0.0 copy-done.2
  108.7 0.0 copy-start.6
  108.7 0.8 copy-done.6
  109.5 0.0 copy-start.5
  109.5 0.8 broadcast_in_dim.22.refs_3_.valid_ref
  110.2 0.0 copy-start.7
  110.3 2.2 %collective-permute-start = (bf16[2,4,8,128,128]{4,3,2,1,0:T(8,128)(2,1)}, bf16[2,4,8,128,128]{4,3,2,1,0:T(8,128)(2,1)}, u32[]{:S(2)}, u32[]{:S(2)}) collective-permute-start(bf16[2,4,8,128,128]{4,3,2,1,0:T(8,128)(2,1)} %get-tuple-element.7.tail), channel_id=1, source_target_pairs={{0,1},{1,2},{2,3},{3,4},{4,5},{5,6},{6,7},{7,8},{8,9},{9,10},{10,1... | collective-permute-start | bytes 6291464 | tf_op jit(solution)/shard_map/ppermute | solution.py:413
  112.4 3.5 %collective-permute-start.1 = (bf16[2,4,8,128,128]{4,3,2,1,0:T(8,128)(2,1)}, bf16[2,4,8,128,128]{4,3,2,1,0:T(8,128)(2,1)}, u32[]{:S(2)}, u32[]{:S(2)}) collective-permute-start(bf16[2,4,8,128,128]{4,3,2,1,0:T(8,128)(2,1)} %get-tuple-element.8.head), channel_id=1, source_target_pairs={{1,0},{2,1},{3,2},{4,3},{5,4},{6,5},{7,6},{8,7},{9,8},{10,9},{11,1... | collective-permute-start | bytes 6291464 | tf_op jit(solution)/shard_map/ppermute | solution.py:412
  116.0 33.5 %all-to-all-done.1 = bf16[128,128,128]{2,1,0:T(8,128)(2,1)} async-done(((bf16[128,128,128]{2,1,0:T(8,128)(2,1)}), bf16[128,128,128]{2,1,0:T(8,128)(2,1)}, u32[]{:S(2)}, u32[]{:S(2)}) %all-to-all-start.1) | async-done | bytes 4194336 | tf_op jit(solution)/shard_map/all_to_all | solution.py:402
  149.4 0.0 copy-done.5
  149.4 0.0 copy-done.7
  149.4 0.0 copy-start.1
  149.4 0.0 copy-start.3
  149.4 6.9 %delay_spectra.5.inner = bf16[2,4,16,128,128]{4,3,2,1,0:T(8,128)(2,1)S(1)} custom-call(bf16[16,8,128,128]{3,2,1,0:T(8,128)(2,1)} %bitcast.11.received_ref, bf16[1024,1024]{1,0:T(8,128)(2,1)S(1)} %copy-done.5, f32[8,16,8,128]{3,2,1,0:T(8,128)S(1)} %copy-done.7), custom_call_target="tpu_custom_call" | custom-call | flops 4294967296 | bytes 16777216 | tf_op jit(solution)/shard_map/delay_spectra/pallas_call | solution.py:154
  156.3 0.0 copy-done.1
  156.3 0.0 copy-done.3
  156.3 0.0 copy-start.8
  156.4 6.8 %inner_pairs.1.inner_ref = f32[8,24,8,128]{3,2,1,0:T(8,128)S(1)} custom-call(bf16[2,4,8,128,128]{4,3,2,1,0:T(8,128)(2,1)S(1)} %copy-done.3, bf16[2,4,16,128,128]{4,3,2,1,0:T(8,128)(2,1)S(1)} %delay_spectra.5.inner, bf16[2,4,8,128,128]{4,3,2,1,0:T(8,128)(2,1)S(1)} %copy-done.1), custom_call_target="tpu_custom_call" | custom-call | flops 42991616 | bytes 8388608 | tf_op jit(solution)/shard_map/inner_pairs/pallas_call | solution.py:284
  163.1 0.0 collective-permute-done.before
  163.1 0.0 collective-permute-done.1.after
  163.1 0.0 copy-done.8
  163.2 6.6 %pair_power.1 = f32[32,16,1024]{2,1,0:T(8,128)} custom-call(bf16[2,4,8,128,128]{4,3,2,1,0:T(8,128)(2,1)} %collective-permute-done.before, bf16[2,4,8,128,128]{4,3,2,1,0:T(8,128)(2,1)S(1)} %copy-done.3, bf16[2,4,8,128,128]{4,3,2,1,0:T(8,128)(2,1)S(1)} %copy-done.1, bf16[2,4,8,128,128]{4,3,2,1,0:T(8,128)(2,1)} %collective-permute-done.1.after, ...), custom_call_target="tpu_custom_call" | custom-call | flops 18874368 | bytes 8388608 | tf_op jit(solution)/shard_map/pair_power/pallas_call | solution.py:284
  (3 shorter events, 0.0 us)
Async XLA Ops:
  9.7 58.9 %all-to-all-start = ((bf16[128,128,128]{2,1,0:T(8,128)(2,1)}), bf16[128,128,128]{2,1,0:T(8,128)(2,1)}, u32[]{:S(2)}, u32[]{:S(2)}) async-start(bf16[128,128,128]{2,1,0:T(8,128)(2,1)} %bitcast.21), calls=%async_computation | async-start | bytes 8388608 | tf_op jit(solution)/shard_map/all_to_all | solution.py:402
  68.6 11.5 %copy-start.9 = (s32[4096]{0:T(1024)S(1)}, s32[4096]{0:T(1024)}, u32[]{:S(2)}) copy-start(s32[4096]{0:T(1024)} %_.7) | copy-start | bytes 49156
  68.6 11.7 %copy-start.10 = (s32[4096,8]{0,1:T(8,128)S(1)}, s32[4096,8]{0,1:T(8,128)}, u32[]{:S(2)}) copy-start(s32[4096,8]{0,1:T(8,128)} %param.7) | copy-start | bytes 393220
  68.6 80.8 %all-to-all-start.1 = ((bf16[128,128,128]{2,1,0:T(8,128)(2,1)}), bf16[128,128,128]{2,1,0:T(8,128)(2,1)}, u32[]{:S(2)}, u32[]{:S(2)}) async-start(bf16[128,128,128]{2,1,0:T(8,128)(2,1)} %bitcast.20), calls=%async_computation.1 | async-start | bytes 8388608 | tf_op jit(solution)/shard_map/all_to_all | solution.py:402
  96.3 4.8 %copy-start.4 = (bf16[1024,1024]{1,0:T(8,128)(2,1)}, bf16[1024,1024]{1,0:T(8,128)(2,1)S(1)}, u32[]{:S(2)}) copy-start(bf16[1024,1024]{1,0:T(8,128)(2,1)S(1)} %fusion.5.table_ref) | copy-start | bytes 6291460
  101.1 4.8 %copy-start = (bf16[2,4,8,128,128]{4,3,2,1,0:T(8,128)(2,1)}, bf16[2,4,8,128,128]{4,3,2,1,0:T(8,128)(2,1)S(1)}, u32[]{:S(2)}) copy-start(bf16[2,4,8,128,128]{4,3,2,1,0:T(8,128)(2,1)S(1)} %delay_spectra.4.tail.refs_1_) | copy-start | bytes 6291460
  105.9 2.8 %copy-start.2 = (bf16[2,4,8,128,128]{4,3,2,1,0:T(8,128)(2,1)}, bf16[2,4,8,128,128]{4,3,2,1,0:T(8,128)(2,1)S(1)}, u32[]{:S(2)}) copy-start(bf16[2,4,8,128,128]{4,3,2,1,0:T(8,128)(2,1)S(1)} %delay_spectra.3.head.refs_0_) | copy-start | bytes 6291460
  108.7 0.8 copy-start.6
  109.5 39.9 %copy-start.5 = (bf16[1024,1024]{1,0:T(8,128)(2,1)S(1)}, bf16[1024,1024]{1,0:T(8,128)(2,1)}, u32[]{:S(2)}) copy-start(bf16[1024,1024]{1,0:T(8,128)(2,1)} %copy-done.4) | copy-start | bytes 6291460
  110.2 39.2 %copy-start.7 = (f32[8,16,8,128]{3,2,1,0:T(8,128)S(1)}, f32[8,16,8,128]{3,2,1,0:T(8,128)}, u32[]{:S(2)}) copy-start(f32[8,16,8,128]{3,2,1,0:T(8,128)} %copy-done.6) | copy-start | bytes 1572868
  110.3 52.9 %collective-permute-start = (bf16[2,4,8,128,128]{4,3,2,1,0:T(8,128)(2,1)}, bf16[2,4,8,128,128]{4,3,2,1,0:T(8,128)(2,1)}, u32[]{:S(2)}, u32[]{:S(2)}) collective-permute-start(bf16[2,4,8,128,128]{4,3,2,1,0:T(8,128)(2,1)} %get-tuple-element.7.tail), channel_id=1, source_target_pairs={{0,1},{1,2},{2,3},{3,4},{4,5},{5,6},{6,7},{7,8},{8,9},{9,10},{10,1... | collective-permute-start | bytes 6291464 | tf_op jit(solution)/shard_map/ppermute | solution.py:413
  112.4 50.7 %collective-permute-start.1 = (bf16[2,4,8,128,128]{4,3,2,1,0:T(8,128)(2,1)}, bf16[2,4,8,128,128]{4,3,2,1,0:T(8,128)(2,1)}, u32[]{:S(2)}, u32[]{:S(2)}) collective-permute-start(bf16[2,4,8,128,128]{4,3,2,1,0:T(8,128)(2,1)} %get-tuple-element.8.head), channel_id=1, source_target_pairs={{1,0},{2,1},{3,2},{4,3},{5,4},{6,5},{7,6},{8,7},{9,8},{10,9},{11,1... | collective-permute-start | bytes 6291464 | tf_op jit(solution)/shard_map/ppermute | solution.py:412
  149.4 6.9 %copy-start.1 = (bf16[2,4,8,128,128]{4,3,2,1,0:T(8,128)(2,1)S(1)}, bf16[2,4,8,128,128]{4,3,2,1,0:T(8,128)(2,1)}, u32[]{:S(2)}) copy-start(bf16[2,4,8,128,128]{4,3,2,1,0:T(8,128)(2,1)} %get-tuple-element.7.tail) | copy-start | bytes 6291460
  149.4 6.9 %copy-start.3 = (bf16[2,4,8,128,128]{4,3,2,1,0:T(8,128)(2,1)S(1)}, bf16[2,4,8,128,128]{4,3,2,1,0:T(8,128)(2,1)}, u32[]{:S(2)}) copy-start(bf16[2,4,8,128,128]{4,3,2,1,0:T(8,128)(2,1)} %get-tuple-element.8.head) | copy-start | bytes 6291460
  156.3 6.8 %copy-start.8 = (f32[40,8,128]{2,1,0:T(8,128)S(1)}, f32[40,8,128]{2,1,0:T(8,128)}, u32[]{:S(2)}) copy-start(f32[40,8,128]{2,1,0:T(8,128)} %broadcast_in_dim.22.refs_3_.valid_ref) | copy-start | bytes 491524

commit v10 on v9

--- a/solution.py
+++ b/solution.py
@@ -145,7 +145,7 @@
     store(1, chunks - 1, jnp.where(first, minus[0], minus[-1]))
 
 
-def spectra(received, table, n_tm, n_chan, first, slots, earlier):
+def spectra(received, table, n_tm, n_chan, first, slots, earlier, stays):
     _, pairs, lanes = received.shape
     step = REACH
     width = table.shape[1]
@@ -158,11 +158,15 @@
             pl.BlockSpec(
                 (n_tm, n_chan, 8 * step, lanes), lambda t: (0, 0, first // step + t, 0)
             ),
-            pl.BlockSpec(memory_space=pltpu.VMEM),
+            whole()
+            if stays
+            else pl.BlockSpec(table.shape, lambda t: (0, 0), pipeline_mode=pl.Buffered(1)),
             pl.BlockSpec(memory_space=pl.ANY),
         ],
         out_specs=pl.BlockSpec((2, chunks, step, rows, LANES), lambda t: (0, 0, t, 0, 0)),
-        out_shape=jax.ShapeDtypeStruct((2, chunks, slots, rows, LANES), jnp.bfloat16),
+        out_shape=(jax.ShapeDtypeStruct if stays else pltpu.HBM)(
+            (2, chunks, slots, rows, LANES), jnp.bfloat16
+        ),
         compiler_params=pltpu.CompilerParams(vmem_limit_bytes=32 * MIB),
         cost_estimate=pl.CostEstimate(
             flops=16 * slots * n_tm * width * width,
@@ -170,7 +174,11 @@
             transcendentals=0,
         ),
         name="delay_spectra",
-    )(in_hbm(received.reshape(n_tm, n_chan, pairs, lanes)), table, earlier)
+    )(
+        in_hbm(received.reshape(n_tm, n_chan, pairs, lanes)),
+        table if stays else in_hbm(table),
+        earlier,
+    )
 
 
 def fold_rows(sums):
@@ -207,11 +215,9 @@
 
 
 def outer_kernel(head, tail, out_ref, rows_ref):
-    sign, first_chunk = pl.program_id(0), pl.program_id(1) * STEP
-
     def one_chunk(c, carry):
-        load_rows(rows_ref, 0, head.at[sign, first_chunk + c])
-        load_rows(rows_ref, REACH, tail.at[sign, first_chunk + c])
+        load_rows(rows_ref, 0, head.at[0, c])
+        load_rows(rows_ref, REACH, tail.at[0, c])
         for first in (0, REACH):
             for j in range(REACH):
                 out_ref[c, first + j] = cross_tile(rows_ref, first + j, range(1, REACH - j))
@@ -317,8 +323,8 @@
     return cross_call(
         outer_kernel,
         "outer_pairs",
-        [head, tail],
-        [whole()] * 2,
+        [in_hbm(head), in_hbm(tail)],
+        [chunks_spec(head)] * 2,
         sums_spec(slots),
         jax.ShapeDtypeStruct((2 * CHUNKS, slots, REACH, LANES), jnp.float32),
         slots,
@@ -368,10 +374,10 @@
         kernel,
         in_specs=[anywhere] * (count + len(earlier)),
         out_specs=[anywhere] * count,
-        out_shape=[jax.ShapeDtypeStruct(array.shape, array.dtype) for array in arrays],
+        out_shape=[pltpu.HBM(array.shape, array.dtype) for array in arrays],
         input_output_aliases={i: i for i in range(count)},
         name="in_order",
-    )(*arrays, *earlier)
+    )(*[in_hbm(array) for array in arrays], *earlier)
 
 
 def body(visibilities, owner_order, group_ids, partner_flags):
@@ -405,13 +411,13 @@
     down = [(i + 1, i) for i in range(n_dev - 1)]
     received_outer = exchange(OUTER, group_ids)
     received_inner = exchange(INNER, group_ids)
-    head = spectra(received_outer, table, n_tm, n_chan, 0, REACH, group_ids)
-    tail = spectra(received_outer, table, n_tm, n_chan, REACH, REACH, group_ids)
+    head = spectra(received_outer, table, n_tm, n_chan, 0, REACH, group_ids, False)
+    tail = spectra(received_outer, table, n_tm, n_chan, REACH, REACH, group_ids, False)
     outer_sums = outer_powers(head, tail)
     head_sent, tail_sent = after_those((head, tail), outer_sums, valid)
     after = lax.ppermute(head_sent, AXES, down)
     before = lax.ppermute(tail_sent, AXES, up)
-    inner = spectra(received_inner, table, n_tm, n_chan, 0, 2 * REACH, outer_sums)
+    inner = spectra(received_inner, table, n_tm, n_chan, 0, 2 * REACH, outer_sums, True)
     inner_sums = inner_powers(head_sent, inner, tail_sent)
     return final_powers(before, head_sent, tail_sent, after, outer_sums, inner_sums, valid)
 

time: 170 us -> 158 us (0.929)
  the two profiles are of different devices: /device:TPU:46 before, /device:TPU:32 now
where the time goes in v10:
time: 158 us
  Pallas kernels  56.3 us (36%)
  waiting for transfers between devices  54 us (34%)
  starting transfers between devices  27.3 us (17%)
  other arithmetic  17.4 us (11%)
  local copies, waits for them, and re-layouts  1.8 us (1%)
    all_to_all x2, waiting for transfers between devices, exchange(): return lax.all_to_all(send, AXES, 0, 0, tiled=True)  47.9 us
    pallas_call x2, Pallas kernels, gather(): pl.pallas_call(functools.partial(gather_kernel, slots, n_base // n_dev),...  19.4 us
    pallas_call x3, Pallas kernels, spectra(): pl.pallas_call(spectra_kernel, grid=(slots // step,), in_specs=[pl.BlockS...  18.8 us
    pallas_call x3, Pallas kernels, cross_call(): pl.pallas_call(kernel, grid=(2, CHUNKS // STEP), in_specs=specs, out_spec...  18.1 us
    all_to_all x2, starting transfers between devices, exchange(): return lax.all_to_all(send, AXES, 0, 0, tiled=True)  17.4 us
    convert_element_type x1, other arithmetic, half_table(): return (weights_norm[:, None] * jnp.cos(phase_angle)).astype(jnp.bfloat16)  16.5 us
    ppermute x1, starting transfers between devices, body(): after = lax.ppermute(head_sent, AXES, down)  7.73 us
    ppermute x1, waiting for transfers between devices, body(): before = lax.ppermute(tail_sent, AXES, up)  6.15 us
  transfers between devices with their start and end apart: 4, of which 3 were waited for; matrix products, arithmetic and copies ran while one was open for 12% of the time, Pallas kernels for 25%

profile of v10, /device:TPU:32, one launch (start us, length us, event | category | flops | bytes accessed | tf_op | source)
XLA Modules:
  0.0 157.7 jit_solution(12356387307714275347)
XLA Ops:
  0.0 9.6 %slot_gather.2 = bf16[128,16,4,2,128]{4,3,2,1,0:T(2,128)(2,1)} custom-call(s32[4096]{0:T(1024)} %order_ref.3, bf16[4,4096,2,128]{3,2,1,0:T(2,128)(2,1)} %vis_ref.3, s32[4096]{0:T(1024)} %_.7), custom_call_target="tpu_custom_call" | custom-call | bytes 8388608 | tf_op jit(solution)/shard_map/slot_gather/pallas_call | solution.py:91
  9.6 10.7 %all-to-all-start = ((bf16[128,128,128]{2,1,0:T(8,128)(2,1)}), bf16[128,128,128]{2,1,0:T(8,128)(2,1)}, u32[]{:S(2)}, u32[]{:S(2)}) async-start(bf16[128,128,128]{2,1,0:T(8,128)(2,1)} %bitcast.21), calls=%async_computation | async-start | bytes 8388608 | tf_op jit(solution)/shard_map/all_to_all | solution.py:408
  20.3 9.8 %slot_gather.3 = bf16[128,16,4,2,128]{4,3,2,1,0:T(2,128)(2,1)} custom-call(s32[4096]{0:T(1024)} %order_ref.3, bf16[4,4096,2,128]{3,2,1,0:T(2,128)(2,1)} %vis_ref.3, s32[4096]{0:T(1024)} %_.7), custom_call_target="tpu_custom_call" | custom-call | bytes 8388608 | tf_op jit(solution)/shard_map/slot_gather/pallas_call | solution.py:91
  30.2 41.9 %all-to-all-done = bf16[128,128,128]{2,1,0:T(8,128)(2,1)} async-done(((bf16[128,128,128]{2,1,0:T(8,128)(2,1)}), bf16[128,128,128]{2,1,0:T(8,128)(2,1)}, u32[]{:S(2)}, u32[]{:S(2)}) %all-to-all-start) | async-done | bytes 4194336 | tf_op jit(solution)/shard_map/all_to_all | solution.py:408
  72.1 0.0 copy-start.6
  72.1 0.0 copy-start.7
  72.1 6.7 %all-to-all-start.1 = ((bf16[128,128,128]{2,1,0:T(8,128)(2,1)}), bf16[128,128,128]{2,1,0:T(8,128)(2,1)}, u32[]{:S(2)}, u32[]{:S(2)}) async-start(bf16[128,128,128]{2,1,0:T(8,128)(2,1)} %bitcast.20), calls=%async_computation.1 | async-start | bytes 8388608 | tf_op jit(solution)/shard_map/all_to_all | solution.py:408
  78.7 0.7 multiply_reduce_fusion
  80.1 0.0 copy-done.6
  80.1 0.1 pad_dynamic-slice_fusion.1
  80.2 0.1 compare_bitcast_fusion
  80.3 0.0 copy-done.7
  80.3 0.1 and_convert_fusion
  80.4 0.1 copy.7
  80.5 0.1 fusion.23
  80.6 16.5 %fusion.5.table_ref = bf16[1024,1024]{1,0:T(8,128)(2,1)} fusion(s32[1024]{0:T(1024)S(1)} %get-tuple-element.17, s32[1024]{0:T(1024)S(1)} %get-tuple-element.18, f32[1024]{0:T(1024)S(1)} %fusion.23), kind=kLoop, calls=%fused_computation.8 | loop fusion | flops 17825792 | bytes 2109440 | tf_op jit(solution)/shard_map/convert_element_type | solution.py:41
  97.1 5.9 %delay_spectra.4.tail.refs_1_ = bf16[2,4,8,128,128]{4,3,2,1,0:T(8,128)(2,1)} custom-call(bf16[16,8,128,128]{3,2,1,0:T(8,128)(2,1)} %bitcast.1.received_ref, bf16[1024,1024]{1,0:T(8,128)(2,1)} %fusion.5.table_ref, s32[4096]{0:T(1024)S(1)} %copy-done.6), custom_call_target="tpu_custom_call" | custom-call | flops 2147483648 | bytes 8388608 | tf_op jit(solution)/shard_map/delay_spectra/pallas_call | solution.py:154
  103.0 6.0 %delay_spectra.3.head.refs_0_ = bf16[2,4,8,128,128]{4,3,2,1,0:T(8,128)(2,1)} custom-call(bf16[16,8,128,128]{3,2,1,0:T(8,128)(2,1)} %bitcast.1.received_ref, bf16[1024,1024]{1,0:T(8,128)(2,1)} %fusion.5.table_ref, s32[4096]{0:T(1024)S(1)} %copy-done.6), custom_call_target="tpu_custom_call" | custom-call | flops 2147483648 | bytes 8388608 | tf_op jit(solution)/shard_map/delay_spectra/pallas_call | solution.py:154
  109.0 0.0 copy-start.2
  109.0 4.7 %outer_pairs.1.refs_2_._.outer_ref = f32[8,16,8,128]{3,2,1,0:T(8,128)S(1)} custom-call(bf16[2,4,8,128,128]{4,3,2,1,0:T(8,128)(2,1)} %delay_spectra.3.head.refs_0_, bf16[2,4,8,128,128]{4,3,2,1,0:T(8,128)(2,1)} %delay_spectra.4.tail.refs_1_), custom_call_target="tpu_custom_call" | custom-call | flops 14680064 | bytes 4194304 | tf_op jit(solution)/shard_map/outer_pairs/pallas_call | solution.py:290
  113.7 0.0 copy-start.3
  113.7 0.8 copy-done.3
  114.5 0.8 broadcast_in_dim.22.refs_3_.valid_ref
  115.3 0.0 copy-start.4
  115.3 2.2 %collective-permute-start = (bf16[2,4,8,128,128]{4,3,2,1,0:T(8,128)(2,1)}, bf16[2,4,8,128,128]{4,3,2,1,0:T(8,128)(2,1)}, u32[]{:S(2)}, u32[]{:S(2)}) collective-permute-start(bf16[2,4,8,128,128]{4,3,2,1,0:T(8,128)(2,1)} %get-tuple-element.7.tail), channel_id=1, source_target_pairs={{0,1},{1,2},{2,3},{3,4},{4,5},{5,6},{6,7},{7,8},{8,9},{9,10},{10,1... | collective-permute-start | bytes 6291464 | tf_op jit(solution)/shard_map/ppermute | solution.py:419
  117.4 7.7 %collective-permute-start.1 = (bf16[2,4,8,128,128]{4,3,2,1,0:T(8,128)(2,1)}, bf16[2,4,8,128,128]{4,3,2,1,0:T(8,128)(2,1)}, u32[]{:S(2)}, u32[]{:S(2)}) collective-permute-start(bf16[2,4,8,128,128]{4,3,2,1,0:T(8,128)(2,1)} %get-tuple-element.8.head), channel_id=1, source_target_pairs={{1,0},{2,1},{3,2},{4,3},{5,4},{6,5},{7,6},{8,7},{9,8},{10,9},{11,1... | collective-permute-start | bytes 6291464 | tf_op jit(solution)/shard_map/ppermute | solution.py:418
  125.2 6.0 %all-to-all-done.1 = bf16[128,128,128]{2,1,0:T(8,128)(2,1)} async-done(((bf16[128,128,128]{2,1,0:T(8,128)(2,1)}), bf16[128,128,128]{2,1,0:T(8,128)(2,1)}, u32[]{:S(2)}, u32[]{:S(2)}) %all-to-all-start.1) | async-done | bytes 4194336 | tf_op jit(solution)/shard_map/all_to_all | solution.py:408
  131.2 0.0 copy-done.2
  131.2 0.0 copy-done.4
  131.2 0.0 copy-start
  131.2 0.0 copy-start.1
  131.2 6.9 %delay_spectra.5.inner = bf16[2,4,16,128,128]{4,3,2,1,0:T(8,128)(2,1)S(1)} custom-call(bf16[16,8,128,128]{3,2,1,0:T(8,128)(2,1)} %bitcast.11.received_ref, bf16[1024,1024]{1,0:T(8,128)(2,1)S(1)} %copy-done.2, f32[8,16,8,128]{3,2,1,0:T(8,128)S(1)} %copy-done.4), custom_call_target="tpu_custom_call" | custom-call | flops 4294967296 | bytes 16777216 | tf_op jit(solution)/shard_map/delay_spectra/pallas_call | solution.py:154
  138.1 0.0 copy-done
  138.1 0.0 copy-done.1
  138.1 0.0 copy-start.5
  138.1 6.8 %inner_pairs.1.inner_ref = f32[8,24,8,128]{3,2,1,0:T(8,128)S(1)} custom-call(bf16[2,4,8,128,128]{4,3,2,1,0:T(8,128)(2,1)S(1)} %copy-done.1, bf16[2,4,16,128,128]{4,3,2,1,0:T(8,128)(2,1)S(1)} %delay_spectra.5.inner, bf16[2,4,8,128,128]{4,3,2,1,0:T(8,128)(2,1)S(1)} %copy-done), custom_call_target="tpu_custom_call" | custom-call | flops 42991616 | bytes 8388608 | tf_op jit(solution)/shard_map/inner_pairs/pallas_call | solution.py:290
  144.9 6.2 %collective-permute-done.before = bf16[2,4,8,128,128]{4,3,2,1,0:T(8,128)(2,1)} collective-permute-done((bf16[2,4,8,128,128]{4,3,2,1,0:T(8,128)(2,1)}, bf16[2,4,8,128,128]{4,3,2,1,0:T(8,128)(2,1)}, u32[]{:S(2)}, u32[]{:S(2)}) %collective-permute-start) | collective-permute-done | bytes 2097184 | tf_op jit(solution)/shard_map/ppermute | solution.py:419
  151.0 0.0 collective-permute-done.1.after
  151.0 0.0 copy-done.5
  151.0 6.6 %pair_power.1 = f32[32,16,1024]{2,1,0:T(8,128)} custom-call(bf16[2,4,8,128,128]{4,3,2,1,0:T(8,128)(2,1)} %collective-permute-done.before, bf16[2,4,8,128,128]{4,3,2,1,0:T(8,128)(2,1)S(1)} %copy-done.1, bf16[2,4,8,128,128]{4,3,2,1,0:T(8,128)(2,1)S(1)} %copy-done, bf16[2,4,8,128,128]{4,3,2,1,0:T(8,128)(2,1)} %collective-permute-done.1.after, ...), custom_call_target="tpu_custom_call" | custom-call | flops 18874368 | bytes 8388608 | tf_op jit(solution)/shard_map/pair_power/pallas_call | solution.py:290
  (3 shorter events, 0.0 us)
Async XLA Ops:
  9.6 62.4 %all-to-all-start = ((bf16[128,128,128]{2,1,0:T(8,128)(2,1)}), bf16[128,128,128]{2,1,0:T(8,128)(2,1)}, u32[]{:S(2)}, u32[]{:S(2)}) async-start(bf16[128,128,128]{2,1,0:T(8,128)(2,1)} %bitcast.21), calls=%async_computation | async-start | bytes 8388608 | tf_op jit(solution)/shard_map/all_to_all | solution.py:408
  72.1 8.1 %copy-start.6 = (s32[4096]{0:T(1024)S(1)}, s32[4096]{0:T(1024)}, u32[]{:S(2)}) copy-start(s32[4096]{0:T(1024)} %_.7) | copy-start | bytes 49156
  72.1 8.3 %copy-start.7 = (s32[4096,8]{0,1:T(8,128)S(1)}, s32[4096,8]{0,1:T(8,128)}, u32[]{:S(2)}) copy-start(s32[4096,8]{0,1:T(8,128)} %param.7) | copy-start | bytes 393220
  72.1 59.1 %all-to-all-start.1 = ((bf16[128,128,128]{2,1,0:T(8,128)(2,1)}), bf16[128,128,128]{2,1,0:T(8,128)(2,1)}, u32[]{:S(2)}, u32[]{:S(2)}) async-start(bf16[128,128,128]{2,1,0:T(8,128)(2,1)} %bitcast.20), calls=%async_computation.1 | async-start | bytes 8388608 | tf_op jit(solution)/shard_map/all_to_all | solution.py:408
  109.0 22.2 %copy-start.2 = (bf16[1024,1024]{1,0:T(8,128)(2,1)S(1)}, bf16[1024,1024]{1,0:T(8,128)(2,1)}, u32[]{:S(2)}) copy-start(bf16[1024,1024]{1,0:T(8,128)(2,1)} %fusion.5.table_ref) | copy-start | bytes 6291460
  113.7 0.8 copy-start.3
  115.3 15.9 %copy-start.4 = (f32[8,16,8,128]{3,2,1,0:T(8,128)S(1)}, f32[8,16,8,128]{3,2,1,0:T(8,128)}, u32[]{:S(2)}) copy-start(f32[8,16,8,128]{3,2,1,0:T(8,128)} %copy-done.3) | copy-start | bytes 1572868
  115.3 35.8 %collective-permute-start = (bf16[2,4,8,128,128]{4,3,2,1,0:T(8,128)(2,1)}, bf16[2,4,8,128,128]{4,3,2,1,0:T(8,128)(2,1)}, u32[]{:S(2)}, u32[]{:S(2)}) collective-permute-start(bf16[2,4,8,128,128]{4,3,2,1,0:T(8,128)(2,1)} %get-tuple-element.7.tail), channel_id=1, source_target_pairs={{0,1},{1,2},{2,3},{3,4},{4,5},{5,6},{6,7},{7,8},{8,9},{9,10},{10,1... | collective-permute-start | bytes 6291464 | tf_op jit(solution)/shard_map/ppermute | solution.py:419
  117.4 33.6 %collective-permute-start.1 = (bf16[2,4,8,128,128]{4,3,2,1,0:T(8,128)(2,1)}, bf16[2,4,8,128,128]{4,3,2,1,0:T(8,128)(2,1)}, u32[]{:S(2)}, u32[]{:S(2)}) collective-permute-start(bf16[2,4,8,128,128]{4,3,2,1,0:T(8,128)(2,1)} %get-tuple-element.8.head), channel_id=1, source_target_pairs={{1,0},{2,1},{3,2},{4,3},{5,4},{6,5},{7,6},{8,7},{9,8},{10,9},{11,1... | collective-permute-start | bytes 6291464 | tf_op jit(solution)/shard_map/ppermute | solution.py:418
  131.2 6.9 %copy-start = (bf16[2,4,8,128,128]{4,3,2,1,0:T(8,128)(2,1)S(1)}, bf16[2,4,8,128,128]{4,3,2,1,0:T(8,128)(2,1)}, u32[]{:S(2)}) copy-start(bf16[2,4,8,128,128]{4,3,2,1,0:T(8,128)(2,1)} %get-tuple-element.7.tail) | copy-start | bytes 6291460
  131.2 6.9 %copy-start.1 = (bf16[2,4,8,128,128]{4,3,2,1,0:T(8,128)(2,1)S(1)}, bf16[2,4,8,128,128]{4,3,2,1,0:T(8,128)(2,1)}, u32[]{:S(2)}) copy-start(bf16[2,4,8,128,128]{4,3,2,1,0:T(8,128)(2,1)} %get-tuple-element.8.head) | copy-start | bytes 6291460
  138.1 12.9 %copy-start.5 = (f32[40,8,128]{2,1,0:T(8,128)S(1)}, f32[40,8,128]{2,1,0:T(8,128)}, u32[]{:S(2)}) copy-start(f32[40,8,128]{2,1,0:T(8,128)} %broadcast_in_dim.22.refs_3_.valid_ref) | copy-start | bytes 491524

commit v11 on v10

--- a/solution.py
+++ b/solution.py
@@ -240,7 +240,9 @@
     lax.fori_loop(0, STEP, one_chunk, 0)
 
 
-def final_kernel(before, head, tail, after, outer_ref, inner_ref, valid_ref, out_ref, rows_ref):
+def final_kernel(
+    before, head, tail, after, outer_ref, inner_ref, valid_ref, out_ref, rows_ref, near, sems
+):
     shape = (REACH, LANES)
     lane = lax.broadcasted_iota(jnp.int32, shape, 1)
     row = lax.broadcasted_iota(jnp.int32, shape, 0)
@@ -248,16 +250,34 @@
     order = jnp.where(mirror, (LANES - lane) % LANES, lane)
     slots = out_ref.shape[0]
 
+    steps = CHUNKS // STEP
+    step = pl.program_id(0) * steps + pl.program_id(1)
+
+    def arrival(side, number):
+        source = (before, after)[side]
+        span = pl.ds(number % steps * STEP, STEP)
+        return pltpu.make_async_copy(
+            source.at[number // steps, span], near.at[side, number], sems.at[side, number]
+        )
+
+    @pl.when(step == 0)
+    def _():
+        for number in range(2 * steps):
+            for side in range(2):
+                arrival(side, number).start()
+
+    for side in range(2):
+        arrival(side, step).wait()
     first_chunk = pl.program_id(1) * STEP
     first_sums = pl.program_id(0) * CHUNKS + first_chunk
 
     def one_chunk(c, carry):
         at = jnp.where(mirror, STEP - 1 - c, c)
         lanes = pl.ds(pl.multiple_of(at * LANES, LANES), LANES)
-        load_rows(rows_ref, 0, before.at[0, c])
+        load_rows(rows_ref, 0, near.at[0, step, c])
         load_rows(rows_ref, REACH, head.at[pl.program_id(0), first_chunk + c])
         load_rows(rows_ref, 2 * REACH, tail.at[pl.program_id(0), first_chunk + c])
-        load_rows(rows_ref, 3 * REACH, after.at[0, c])
+        load_rows(rows_ref, 3 * REACH, near.at[1, step, c])
         powers = {}
         for s in range(-REACH, slots):
             terms = []
@@ -285,7 +305,7 @@
 CHUNKS, STEP = 4, 2
 
 
-def cross_call(kernel, name, operands, specs, out_specs, out_shape, held, pairs):
+def cross_call(kernel, name, operands, specs, out_specs, out_shape, held, pairs, extra=()):
     rows = 128
     return pl.pallas_call(
         kernel,
@@ -293,7 +313,7 @@
         in_specs=specs,
         out_specs=out_specs,
         out_shape=out_shape,
-        scratch_shapes=[pltpu.VMEM((held, rows, LANES), jnp.float32)],
+        scratch_shapes=[pltpu.VMEM((held, rows, LANES), jnp.float32), *extra],
         compiler_params=pltpu.CompilerParams(vmem_limit_bytes=32 * MIB),
         cost_estimate=pl.CostEstimate(
             flops=2 * pairs * rows * 1024,
@@ -348,12 +368,14 @@
 
 def final_powers(before, head, tail, after, outer_sums, inner_sums, valid):
     slots = 4 * REACH
-    operands = [before, head, tail, after, outer_sums, inner_sums, valid]
+    operands = [in_hbm(before), head, tail, in_hbm(after), outer_sums, inner_sums, valid]
+    anywhere = pl.BlockSpec(memory_space=pl.ANY)
+    near = (2, 2 * CHUNKS // STEP, STEP) + before.shape[2:]
     return cross_call(
         final_kernel,
         "pair_power",
         operands,
-        [chunks_spec(before), whole(), whole(), chunks_spec(after), whole(), whole(), whole()],
+        [anywhere, whole(), whole(), anywhere, whole(), whole(), whole()],
         pl.BlockSpec(
             (slots, 2 * REACH, STEP * LANES),
             lambda i, j: (0, 0, jnp.where(i == 0, j, 2 * CHUNKS // STEP - 1 - j)),
@@ -361,6 +383,7 @@
         jax.ShapeDtypeStruct((slots, 2 * REACH, 2 * CHUNKS * LANES), jnp.float32),
         slots,
         72,
+        [pltpu.VMEM(near, before.dtype), pltpu.SemaphoreType.DMA(near[:2])],
     )
 
 

time: 158 us -> 158 us (level)
  no operation moved by 1% of the time
where the time goes in v11:
time: 158 us; the launch traced here: 157 us
  Pallas kernels  55.9 us (35%)
  waiting for transfers between devices  54 us (34%)
  starting transfers between devices  27.3 us (17%)
  other arithmetic  17.4 us (11%)
  local copies, waits for them, and re-layouts  1.8 us (1%)
    all_to_all x2, waiting for transfers between devices, exchange(): return lax.all_to_all(send, AXES, 0, 0, tiled=True)  47.9 us
    pallas_call x2, Pallas kernels, gather(): pl.pallas_call(functools.partial(gather_kernel, slots, n_base // n_dev),...  19.4 us
    pallas_call x3, Pallas kernels, spectra(): pl.pallas_call(spectra_kernel, grid=(slots // step,), in_specs=[pl.BlockS...  18.8 us
    pallas_call x3, Pallas kernels, cross_call(): pl.pallas_call(kernel, grid=(2, CHUNKS // STEP), in_specs=specs, out_spec...  17.7 us
    all_to_all x2, starting transfers between devices, exchange(): return lax.all_to_all(send, AXES, 0, 0, tiled=True)  17.4 us
    convert_element_type x1, other arithmetic, half_table(): return (weights_norm[:, None] * jnp.cos(phase_angle)).astype(jnp.bfloat16)  16.5 us
    ppermute x1, starting transfers between devices, body(): after = lax.ppermute(head_sent, AXES, down)  7.73 us
    ppermute x1, waiting for transfers between devices, body(): before = lax.ppermute(tail_sent, AXES, up)  6.15 us
  transfers between devices with their start and end apart: 4, of which 3 were waited for; matrix products, arithmetic and copies ran while one was open for 12% of the time, Pallas kernels for 25%

profile of v11, /device:TPU:32, one launch (start us, length us, event | category | flops | bytes accessed | tf_op | source)
XLA Modules:
  0.0 157.3 jit_solution(4849136816822586885)
XLA Ops:
  0.0 9.6 %slot_gather.2 = bf16[128,16,4,2,128]{4,3,2,1,0:T(2,128)(2,1)} custom-call(s32[4096]{0:T(1024)} %order_ref.3, bf16[4,4096,2,128]{3,2,1,0:T(2,128)(2,1)} %vis_ref.3, s32[4096]{0:T(1024)} %_.7), custom_call_target="tpu_custom_call" | custom-call | bytes 8388608 | tf_op jit(solution)/shard_map/slot_gather/pallas_call | solution.py:91
  9.6 10.7 %all-to-all-start = ((bf16[128,128,128]{2,1,0:T(8,128)(2,1)}), bf16[128,128,128]{2,1,0:T(8,128)(2,1)}, u32[]{:S(2)}, u32[]{:S(2)}) async-start(bf16[128,128,128]{2,1,0:T(8,128)(2,1)} %bitcast.21), calls=%async_computation | async-start | bytes 8388608 | tf_op jit(solution)/shard_map/all_to_all | solution.py:431
  20.3 9.8 %slot_gather.3 = bf16[128,16,4,2,128]{4,3,2,1,0:T(2,128)(2,1)} custom-call(s32[4096]{0:T(1024)} %order_ref.3, bf16[4,4096,2,128]{3,2,1,0:T(2,128)(2,1)} %vis_ref.3, s32[4096]{0:T(1024)} %_.7), custom_call_target="tpu_custom_call" | custom-call | bytes 8388608 | tf_op jit(solution)/shard_map/slot_gather/pallas_call | solution.py:91
  30.2 41.9 %all-to-all-done = bf16[128,128,128]{2,1,0:T(8,128)(2,1)} async-done(((bf16[128,128,128]{2,1,0:T(8,128)(2,1)}), bf16[128,128,128]{2,1,0:T(8,128)(2,1)}, u32[]{:S(2)}, u32[]{:S(2)}) %all-to-all-start) | async-done | bytes 4194336 | tf_op jit(solution)/shard_map/all_to_all | solution.py:431
  72.1 0.0 copy-start.6
  72.1 0.0 copy-start.7
  72.1 6.7 %all-to-all-start.1 = ((bf16[128,128,128]{2,1,0:T(8,128)(2,1)}), bf16[128,128,128]{2,1,0:T(8,128)(2,1)}, u32[]{:S(2)}, u32[]{:S(2)}) async-start(bf16[128,128,128]{2,1,0:T(8,128)(2,1)} %bitcast.20), calls=%async_computation.1 | async-start | bytes 8388608 | tf_op jit(solution)/shard_map/all_to_all | solution.py:431
  78.7 0.7 multiply_reduce_fusion
  80.1 0.0 copy-done.6
  80.1 0.1 pad_dynamic-slice_fusion.1
  80.2 0.1 compare_bitcast_fusion
  80.3 0.0 copy-done.7
  80.3 0.1 and_convert_fusion
  80.4 0.1 copy.7
  80.5 0.1 fusion.23
  80.6 16.5 %fusion.5.table_ref = bf16[1024,1024]{1,0:T(8,128)(2,1)} fusion(s32[1024]{0:T(1024)S(1)} %get-tuple-element.17, s32[1024]{0:T(1024)S(1)} %get-tuple-element.18, f32[1024]{0:T(1024)S(1)} %fusion.23), kind=kLoop, calls=%fused_computation.8 | loop fusion | flops 17825792 | bytes 2109440 | tf_op jit(solution)/shard_map/convert_element_type | solution.py:41
  97.1 5.9 %delay_spectra.4.tail.refs_1_ = bf16[2,4,8,128,128]{4,3,2,1,0:T(8,128)(2,1)} custom-call(bf16[16,8,128,128]{3,2,1,0:T(8,128)(2,1)} %bitcast.1.received_ref, bf16[1024,1024]{1,0:T(8,128)(2,1)} %fusion.5.table_ref, s32[4096]{0:T(1024)S(1)} %copy-done.6), custom_call_target="tpu_custom_call" | custom-call | flops 2147483648 | bytes 8388608 | tf_op jit(solution)/shard_map/delay_spectra/pallas_call | solution.py:154
  103.0 6.0 %delay_spectra.3.head.refs_0_ = bf16[2,4,8,128,128]{4,3,2,1,0:T(8,128)(2,1)} custom-call(bf16[16,8,128,128]{3,2,1,0:T(8,128)(2,1)} %bitcast.1.received_ref, bf16[1024,1024]{1,0:T(8,128)(2,1)} %fusion.5.table_ref, s32[4096]{0:T(1024)S(1)} %copy-done.6), custom_call_target="tpu_custom_call" | custom-call | flops 2147483648 | bytes 8388608 | tf_op jit(solution)/shard_map/delay_spectra/pallas_call | solution.py:154
  109.0 0.0 copy-start.2
  109.0 4.7 %outer_pairs.1.refs_2_._.outer_ref = f32[8,16,8,128]{3,2,1,0:T(8,128)S(1)} custom-call(bf16[2,4,8,128,128]{4,3,2,1,0:T(8,128)(2,1)} %delay_spectra.3.head.refs_0_, bf16[2,4,8,128,128]{4,3,2,1,0:T(8,128)(2,1)} %delay_spectra.4.tail.refs_1_), custom_call_target="tpu_custom_call" | custom-call | flops 14680064 | bytes 4194304 | tf_op jit(solution)/shard_map/outer_pairs/pallas_call | solution.py:310
  113.7 0.0 copy-start.3
  113.7 0.8 copy-done.3
  114.5 0.8 broadcast_in_dim.22.refs_3_.valid_ref
  115.3 0.0 copy-start.4
  115.3 2.2 %collective-permute-start = (bf16[2,4,8,128,128]{4,3,2,1,0:T(8,128)(2,1)}, bf16[2,4,8,128,128]{4,3,2,1,0:T(8,128)(2,1)}, u32[]{:S(2)}, u32[]{:S(2)}) collective-permute-start(bf16[2,4,8,128,128]{4,3,2,1,0:T(8,128)(2,1)} %get-tuple-element.7.tail), channel_id=1, source_target_pairs={{0,1},{1,2},{2,3},{3,4},{4,5},{5,6},{6,7},{7,8},{8,9},{9,10},{10,1... | collective-permute-start | bytes 6291464 | tf_op jit(solution)/shard_map/ppermute | solution.py:442
  117.4 7.7 %collective-permute-start.1 = (bf16[2,4,8,128,128]{4,3,2,1,0:T(8,128)(2,1)}, bf16[2,4,8,128,128]{4,3,2,1,0:T(8,128)(2,1)}, u32[]{:S(2)}, u32[]{:S(2)}) collective-permute-start(bf16[2,4,8,128,128]{4,3,2,1,0:T(8,128)(2,1)} %get-tuple-element.8.head), channel_id=1, source_target_pairs={{1,0},{2,1},{3,2},{4,3},{5,4},{6,5},{7,6},{8,7},{9,8},{10,9},{11,1... | collective-permute-start | bytes 6291464 | tf_op jit(solution)/shard_map/ppermute | solution.py:441
  125.2 6.0 %all-to-all-done.1 = bf16[128,128,128]{2,1,0:T(8,128)(2,1)} async-done(((bf16[128,128,128]{2,1,0:T(8,128)(2,1)}), bf16[128,128,128]{2,1,0:T(8,128)(2,1)}, u32[]{:S(2)}, u32[]{:S(2)}) %all-to-all-start.1) | async-done | bytes 4194336 | tf_op jit(solution)/shard_map/all_to_all | solution.py:431
  131.2 0.0 copy-done.2
  131.2 0.0 copy-done.4
  131.2 0.0 copy-start
  131.2 0.0 copy-start.1
  131.2 6.9 %delay_spectra.5.inner = bf16[2,4,16,128,128]{4,3,2,1,0:T(8,128)(2,1)S(1)} custom-call(bf16[16,8,128,128]{3,2,1,0:T(8,128)(2,1)} %bitcast.11.received_ref, bf16[1024,1024]{1,0:T(8,128)(2,1)S(1)} %copy-done.2, f32[8,16,8,128]{3,2,1,0:T(8,128)S(1)} %copy-done.4), custom_call_target="tpu_custom_call" | custom-call | flops 4294967296 | bytes 16777216 | tf_op jit(solution)/shard_map/delay_spectra/pallas_call | solution.py:154
  138.1 0.0 copy-done
  138.1 0.0 copy-done.1
  138.1 0.0 copy-start.5
  138.1 6.8 %inner_pairs.1.inner_ref = f32[8,24,8,128]{3,2,1,0:T(8,128)S(1)} custom-call(bf16[2,4,8,128,128]{4,3,2,1,0:T(8,128)(2,1)S(1)} %copy-done.1, bf16[2,4,16,128,128]{4,3,2,1,0:T(8,128)(2,1)S(1)} %delay_spectra.5.inner, bf16[2,4,8,128,128]{4,3,2,1,0:T(8,128)(2,1)S(1)} %copy-done), custom_call_target="tpu_custom_call" | custom-call | flops 42991616 | bytes 8388608 | tf_op jit(solution)/shard_map/inner_pairs/pallas_call | solution.py:310
  144.9 6.2 %collective-permute-done.before = bf16[2,4,8,128,128]{4,3,2,1,0:T(8,128)(2,1)} collective-permute-done((bf16[2,4,8,128,128]{4,3,2,1,0:T(8,128)(2,1)}, bf16[2,4,8,128,128]{4,3,2,1,0:T(8,128)(2,1)}, u32[]{:S(2)}, u32[]{:S(2)}) %collective-permute-start) | collective-permute-done | bytes 2097184 | tf_op jit(solution)/shard_map/ppermute | solution.py:442
  151.0 0.0 collective-permute-done.1.after
  151.0 0.0 copy-done.5
  151.0 6.2 %pair_power.1 = f32[32,16,1024]{2,1,0:T(8,128)} custom-call(bf16[2,4,8,128,128]{4,3,2,1,0:T(8,128)(2,1)} %collective-permute-done.before, bf16[2,4,8,128,128]{4,3,2,1,0:T(8,128)(2,1)S(1)} %copy-done.1, bf16[2,4,8,128,128]{4,3,2,1,0:T(8,128)(2,1)S(1)} %copy-done, bf16[2,4,8,128,128]{4,3,2,1,0:T(8,128)(2,1)} %collective-permute-done.1.after, ...), custom_call_target="tpu_custom_call" | custom-call | flops 18874368 | bytes 8388608 | tf_op jit(solution)/shard_map/pair_power/pallas_call | solution.py:310
  (3 shorter events, 0.0 us)
Async XLA Ops:
  9.6 62.4 %all-to-all-start = ((bf16[128,128,128]{2,1,0:T(8,128)(2,1)}), bf16[128,128,128]{2,1,0:T(8,128)(2,1)}, u32[]{:S(2)}, u32[]{:S(2)}) async-start(bf16[128,128,128]{2,1,0:T(8,128)(2,1)} %bitcast.21), calls=%async_computation | async-start | bytes 8388608 | tf_op jit(solution)/shard_map/all_to_all | solution.py:431
  72.1 8.1 %copy-start.6 = (s32[4096]{0:T(1024)S(1)}, s32[4096]{0:T(1024)}, u32[]{:S(2)}) copy-start(s32[4096]{0:T(1024)} %_.7) | copy-start | bytes 49156
  72.1 8.3 %copy-start.7 = (s32[4096,8]{0,1:T(8,128)S(1)}, s32[4096,8]{0,1:T(8,128)}, u32[]{:S(2)}) copy-start(s32[4096,8]{0,1:T(8,128)} %param.7) | copy-start | bytes 393220
  72.1 59.1 %all-to-all-start.1 = ((bf16[128,128,128]{2,1,0:T(8,128)(2,1)}), bf16[128,128,128]{2,1,0:T(8,128)(2,1)}, u32[]{:S(2)}, u32[]{:S(2)}) async-start(bf16[128,128,128]{2,1,0:T(8,128)(2,1)} %bitcast.20), calls=%async_computation.1 | async-start | bytes 8388608 | tf_op jit(solution)/shard_map/all_to_all | solution.py:431
  109.0 22.2 %copy-start.2 = (bf16[1024,1024]{1,0:T(8,128)(2,1)S(1)}, bf16[1024,1024]{1,0:T(8,128)(2,1)}, u32[]{:S(2)}) copy-start(bf16[1024,1024]{1,0:T(8,128)(2,1)} %fusion.5.table_ref) | copy-start | bytes 6291460
  113.7 0.8 copy-start.3
  115.3 15.9 %copy-start.4 = (f32[8,16,8,128]{3,2,1,0:T(8,128)S(1)}, f32[8,16,8,128]{3,2,1,0:T(8,128)}, u32[]{:S(2)}) copy-start(f32[8,16,8,128]{3,2,1,0:T(8,128)} %copy-done.3) | copy-start | bytes 1572868
  115.3 35.8 %collective-permute-start = (bf16[2,4,8,128,128]{4,3,2,1,0:T(8,128)(2,1)}, bf16[2,4,8,128,128]{4,3,2,1,0:T(8,128)(2,1)}, u32[]{:S(2)}, u32[]{:S(2)}) collective-permute-start(bf16[2,4,8,128,128]{4,3,2,1,0:T(8,128)(2,1)} %get-tuple-element.7.tail), channel_id=1, source_target_pairs={{0,1},{1,2},{2,3},{3,4},{4,5},{5,6},{6,7},{7,8},{8,9},{9,10},{10,1... | collective-permute-start | bytes 6291464 | tf_op jit(solution)/shard_map/ppermute | solution.py:442
  117.4 33.6 %collective-permute-start.1 = (bf16[2,4,8,128,128]{4,3,2,1,0:T(8,128)(2,1)}, bf16[2,4,8,128,128]{4,3,2,1,0:T(8,128)(2,1)}, u32[]{:S(2)}, u32[]{:S(2)}) collective-permute-start(bf16[2,4,8,128,128]{4,3,2,1,0:T(8,128)(2,1)} %get-tuple-element.8.head), channel_id=1, source_target_pairs={{1,0},{2,1},{3,2},{4,3},{5,4},{6,5},{7,6},{8,7},{9,8},{10,9},{11,1... | collective-permute-start | bytes 6291464 | tf_op jit(solution)/shard_map/ppermute | solution.py:441
  131.2 6.9 %copy-start = (bf16[2,4,8,128,128]{4,3,2,1,0:T(8,128)(2,1)S(1)}, bf16[2,4,8,128,128]{4,3,2,1,0:T(8,128)(2,1)}, u32[]{:S(2)}) copy-start(bf16[2,4,8,128,128]{4,3,2,1,0:T(8,128)(2,1)} %get-tuple-element.7.tail) | copy-start | bytes 6291460
  131.2 6.9 %copy-start.1 = (bf16[2,4,8,128,128]{4,3,2,1,0:T(8,128)(2,1)S(1)}, bf16[2,4,8,128,128]{4,3,2,1,0:T(8,128)(2,1)}, u32[]{:S(2)}) copy-start(bf16[2,4,8,128,128]{4,3,2,1,0:T(8,128)(2,1)} %get-tuple-element.8.head) | copy-start | bytes 6291460
  138.1 12.9 %copy-start.5 = (f32[40,8,128]{2,1,0:T(8,128)S(1)}, f32[40,8,128]{2,1,0:T(8,128)}, u32[]{:S(2)}) copy-start(f32[40,8,128]{2,1,0:T(8,128)} %broadcast_in_dim.22.refs_3_.valid_ref) | copy-start | bytes 491524
